TPU v7x, 256 devices: a whole 4x4x8 slice. The times are simulated.
256 devices in a mesh: grp: 8 (over y, z_lo), row: 32 (over z_hi, x, core).
Axes of the slice: x: 4, y: 4, z: 8 (z_hi: 4, z_lo: 2; z = z_hi * 2 + z_lo), core: 2. Of those that a mesh axis runs over, the one named last changes fastest.
Arguments:
- matrix: float32 [1048576, 256], P(('grp', 'row')), may hold values from -6 to 6
- row_signs: int32 [1048576], P(('grp', 'row')), may hold values from -1 to 1, as said below
- block_dest: int32 [8192], P(('grp', 'row')), may hold values from 0 to 15
- block_signs: int32 [8192], P(('grp', 'row')), may hold values from -1 to 1, as said below
Outputs:
- sketch: float32 [2048, 256], P('row')
Inputs may be any that keep to these rules, and one draw needn't show every extreme that they name: `row_signs`: each entry is -1 or 1. `block_signs`: each entry is -1 or 1.
All inputs are finite; a program needn't handle non-finite values.
Results may differ from a plain program's by a relative error of at most 0.0003.
Values sent between devices are 32-bit elements; how exact they have to be, the bound alone decides.
No kernel may reach another device: no remote copies, remote signals or barrier semaphores. Data moves between devices by JAX's collectives and lax.ppermute only.
A program may use at most 64 MiB of HBM per device.

v0:
```python
import math

import jax
import jax.numpy as jnp
from jax import lax
from jax.sharding import PartitionSpec as P

SKETCH = 2048


def swapped(array, axis, stride):
    return lax.ppermute(array, axis, [(i, i ^ 1 << stride) for i in range(lax.axis_size(axis))])


def sylvester(order):
    indices = jnp.arange(order, dtype=jnp.int32)
    common = indices[:, None] & indices[None, :]
    parity = jnp.zeros((order, order), jnp.int32)
    for section in range(order.bit_length() - 1):
        parity = parity + (common >> section & 1)
    return (1 - 2 * (parity % 2)).astype(jnp.float32)


def unit_weights(dests, signs, start, piece, block, target_count):
    unit_rows = min(piece, block)
    unit_count = piece // unit_rows
    starts = start + jnp.arange(unit_count, dtype=jnp.int32) * unit_rows
    which_block = starts // block
    offset = starts % block // unit_rows
    dest_sel = jnp.take(dests, which_block, axis=1)
    sign_sel = jnp.take(signs, which_block, axis=1).astype(jnp.float32)
    targets = jnp.arange(target_count, dtype=jnp.int32)
    within = jnp.arange(block // unit_rows, dtype=jnp.int32)
    to_dest = (dest_sel[None, :, :] == targets[:, None, None]).astype(jnp.float32) * sign_sel[
        None, :, :
    ]
    to_slot = (offset[None, :] == within[:, None]).astype(jnp.float32)
    return to_dest[:, None, :, :] * to_slot[None, :, None, :]


def place(weights, held, block):
    sources, piece, columns = held.shape
    unit_rows = min(piece, block)
    grid = held.reshape(sources, piece // unit_rows, unit_rows, columns)
    return jnp.einsum("sjmk,mkuc->sjuc", weights, grid, precision=lax.Precision.HIGHEST)


def body(matrix, row_signs, block_dest, block_signs):
    precise = lax.Precision.HIGHEST
    row_count, col_count = matrix.shape
    block = row_count // block_dest.shape[0]
    target_count = SKETCH // block
    dev_count = lax.axis_size("row")
    my_index = lax.axis_index("row")
    exponent = row_count.bit_length() - 1
    first_size = 1 << exponent // 2
    second_size = row_count // first_size
    signed = matrix * row_signs[:, None].astype(jnp.float32)
    shaped = signed.reshape(first_size, second_size, col_count)
    shaped = jnp.einsum("ya,abc->ybc", sylvester(first_size), shaped, precision=precise)
    shaped = jnp.einsum("zb,abc->azc", sylvester(second_size), shaped, precision=precise)
    mixed = shaped.reshape(row_count, col_count) / math.sqrt(row_count)
    flipped = mixed
    inverse_root = 1.0 / math.sqrt(2.0)
    for section in range(dev_count.bit_length() - 1):
        partner = swapped(flipped, "row", section)
        upper = my_index >> section & 1 == 1
        flipped = jnp.where(upper, partner - flipped, flipped + partner) * inverse_root
    weights = unit_weights(
        block_dest[None, :], block_signs[None, :], 0, row_count, block, target_count
    )
    partial_value = place(weights, flipped[None, :, :], block)
    partial_value = partial_value.reshape(SKETCH, col_count)
    group_count = lax.axis_size("grp")
    share = lax.psum_scatter(partial_value, "row", scatter_dimension=0, tiled=True)
    summed = lax.psum(share, "grp")
    total_rows = row_count * dev_count * group_count
    return summed * math.sqrt(SKETCH / total_rows)


def solution(mesh):
    return jax.shard_map(
        body,
        mesh=mesh,
        in_specs=(P(("grp", "row"), None), P(("grp", "row")), P(("grp", "row")), P(("grp", "row"))),
        out_specs=P("row", None),
        check_vma=False,
    )
```

profile of v0, /device:TPU:2, one launch (start us, length us, event | category | flops | bytes accessed | tf_op | source)
XLA Modules:
  0.0 799.0 jit_solution(16415899795226942938)
XLA Ops:
  6.5 0.0 copy-start
  6.5 0.0 reduce-scatter.2.cloned.1.call-start
  6.5 0.7 convert_element_type.29
  7.3 2.6 broadcast_multiply_fusion
  9.9 6.3 fusion.2
  16.1 7.1 fusion.6
  23.2 0.0 collective-permute-start
  23.3 7.5 collective-permute-done
  30.8 5.9 select_multiply_fusion.4
  36.7 2.3 collective-permute-start.1
  39.0 91.2 %collective-permute-done.1 = f32[4096,256]{1,0:T(8,128)} collective-permute-done((f32[4096,256]{1,0:T(8,128)}, f32[4096,256]{1,0:T(8,128)}, u32[]{:S(2)}, u32[]{:S(2)}) %collective-permute-start.1) | collective-permute-done | bytes 4194336 | tf_op jit(solution)/shard_map/ppermute | solution.py:12
  130.2 5.9 select_multiply_fusion.3
  136.1 1.6 collective-permute-start.2
  137.7 92.3 %collective-permute-done.2 = f32[4096,256]{1,0:T(8,128)} collective-permute-done((f32[4096,256]{1,0:T(8,128)}, f32[4096,256]{1,0:T(8,128)}, u32[]{:S(2)}, u32[]{:S(2)}) %collective-permute-start.2) | collective-permute-done | bytes 4194336 | tf_op jit(solution)/shard_map/ppermute | solution.py:12
  230.0 5.9 select_multiply_fusion.2
  236.0 2.4 collective-permute-start.3
  238.4 0.0 copy-start.1
  238.4 179.9 %collective-permute-done.3 = f32[4096,256]{1,0:T(8,128)} collective-permute-done((f32[4096,256]{1,0:T(8,128)}, f32[4096,256]{1,0:T(8,128)}, u32[]{:S(2)}, u32[]{:S(2)}) %collective-permute-start.3) | collective-permute-done | bytes 4194336 | tf_op jit(solution)/shard_map/ppermute | solution.py:12
  418.3 5.9 select_multiply_fusion.1
  424.2 6.0 collective-permute-start.4
  430.3 0.0 copy-done
  430.3 0.7 gather_fusion
  431.0 0.0 copy-done.1
  431.0 0.7 gather_fusion.1
  431.7 179.9 %collective-permute-done.4 = f32[4096,256]{1,0:T(8,128)} collective-permute-done((f32[4096,256]{1,0:T(8,128)}, f32[4096,256]{1,0:T(8,128)}, u32[]{:S(2)}, u32[]{:S(2)}) %collective-permute-start.4) | collective-permute-done | bytes 4194336 | tf_op jit(solution)/shard_map/ppermute | solution.py:12
  611.6 4.0 select_multiply_fusion
  615.6 4.4 fusion.4
  620.0 2.6 copy.6
  622.6 0.0 reduce-scatter.2.cloned.1.call-update
  622.6 0.0 all-reduce.2.cloned.1.call-start
  622.6 89.8 %reduce-scatter.2.cloned.1.call-done = f32[64,256]{1,0:T(8,128)} async-done(((f32[2048,256]{1,0:T(8,128)}), f32[64,256]{1,0:T(8,128)}) %reduce-scatter.2.cloned.1.call-update) | async-done | bytes 65552 | tf_op jit(solution)/shard_map/reduce_scatter | solution.py:75
  712.4 0.0 all-reduce.2.cloned.1.call-update
  712.5 78.2 %all-reduce.2.cloned.1.call-done = f32[64,256]{1,0:T(8,128)} async-done(((f32[64,256]{1,0:T(8,128)}), f32[64,256]{1,0:T(8,128)}) %all-reduce.2.cloned.1.call-update) | async-done | bytes 65552 | tf_op jit(solution)/shard_map/psum | solution.py:76
  790.7 1.5 broadcast_multiply_fusion.1
  (4 shorter events, 0.1 us)
Async XLA Ops:
  6.5 423.7 %copy-start = (s32[32]{0:T(128)S(1)}, s32[32]{0:T(128)}, u32[]{:S(2)}) copy-start(s32[32]{0:T(128)} %param.8) | copy-start | bytes 388
  6.5 705.9 %reduce-scatter.2.cloned.1.call-start = ((), (), s32[]{:S(2)}) async-start(), calls=%async_computation.1 | async-start | bytes 2162688 | tf_op jit(solution)/shard_map/reduce_scatter | solution.py:75
  23.2 7.5 collective-permute-start
  36.7 93.5 %collective-permute-start.1 = (f32[4096,256]{1,0:T(8,128)}, f32[4096,256]{1,0:T(8,128)}, u32[]{:S(2)}, u32[]{:S(2)}) collective-permute-start(f32[4096,256]{1,0:T(8,128)} %select_multiply_fusion.4), channel_id=1, source_target_pairs={{0,2},{1,3},{2,0},{3,1},{4,6},{5,7},{6,4},{7,5},{8,10},{9,11},{10,... | collective-permute-start | bytes 12582920 | tf_op jit(solution)/shard_map/ppermute | solution.py:12
  136.1 93.9 %collective-permute-start.2 = (f32[4096,256]{1,0:T(8,128)}, f32[4096,256]{1,0:T(8,128)}, u32[]{:S(2)}, u32[]{:S(2)}) collective-permute-start(f32[4096,256]{1,0:T(8,128)} %select_multiply_fusion.3), channel_id=1, source_target_pairs={{0,4},{1,5},{2,6},{3,7},{4,0},{5,1},{6,2},{7,3},{8,12},{9,13},{10,... | collective-permute-start | bytes 12582920 | tf_op jit(solution)/shard_map/ppermute | solution.py:12
  236.0 182.3 %collective-permute-start.3 = (f32[4096,256]{1,0:T(8,128)}, f32[4096,256]{1,0:T(8,128)}, u32[]{:S(2)}, u32[]{:S(2)}) collective-permute-start(f32[4096,256]{1,0:T(8,128)} %select_multiply_fusion.2), channel_id=1, source_target_pairs={{0,8},{1,9},{2,10},{3,11},{4,12},{5,13},{6,14},{7,15},{8,0},{9,1},... | collective-permute-start | bytes 12582920 | tf_op jit(solution)/shard_map/ppermute | solution.py:12
  238.4 192.6 %copy-start.1 = (s32[32]{0:T(128)S(1)}, s32[32]{0:T(128)}, u32[]{:S(2)}) copy-start(s32[32]{0:T(128)} %param.9) | copy-start | bytes 388
  424.2 187.4 %collective-permute-start.4 = (f32[4096,256]{1,0:T(8,128)}, f32[4096,256]{1,0:T(8,128)}, u32[]{:S(2)}, u32[]{:S(2)}) collective-permute-start(f32[4096,256]{1,0:T(8,128)} %select_multiply_fusion.1), channel_id=1, source_target_pairs={{0,16},{1,17},{2,18},{3,19},{4,20},{5,21},{6,22},{7,23},{8,24},{9,... | collective-permute-start | bytes 12582920 | tf_op jit(solution)/shard_map/ppermute | solution.py:12
  622.6 168.1 %all-reduce.2.cloned.1.call-start = ((), (), s32[]{:S(2)}) async-start(), calls=%async_computation.2 | async-start | bytes 131072 | tf_op jit(solution)/shard_map/psum | solution.py:76
Sparse Core Ops, SparseCore 0:
  622.7 89.6 reduce-scatter.1
  715.0 75.5 all-reduce.1
where the time goes:
time: 799 us
  waiting for transfers between devices  719 us (90%)
  other arithmetic  32.6 us (4%)
  matrix products  17.8 us (2%)
  between operations  13.5 us (2%)
  starting transfers between devices  12.4 us (2%)
    ppermute x5, waiting for transfers between devices, swapped(): lax.ppermute(array, axis, [(i, i ^ 1 << stride) for i in range(lax.axis_s...  551 us
    reduce_scatter x1, waiting for transfers between devices, body(): lax.psum_scatter(partial_value, 'row', scatter_dimension=0, tiled=True)  89.8 us
    psum x1, waiting for transfers between devices, body(): summed = lax.psum(share, 'grp')  78.2 us
    mul x5, other arithmetic, body(): jnp.where(upper, partner - flipped, flipped + partner) * inverse_root  27.8 us
  transfers between devices with their start and end apart: 7, of which 7 were waited for; matrix products, arithmetic and copies ran while one was open for 0% of the time, Pallas kernels for 0%

commit v1 on v0

v1 whole, which is shorter than its diff:
```python
import functools
import math

import jax
import jax.numpy as jnp
from jax import lax
from jax.experimental import pallas as pl
from jax.experimental.pallas import tpu as pltpu
from jax.sharding import PartitionSpec as P

SKETCH = 2048
MIB = 1 << 20
AXES = ("grp", "row")


def parity(bits):
    for shift in (8, 4, 2, 1):
        bits = bits ^ bits >> shift
    return bits & 1


def hadamard_sign(rows, cols):
    return (1 - 2 * parity(rows & cols)).astype(jnp.float32)


def two_parts(value):
    high = value.astype(jnp.bfloat16)
    low = (value - high.astype(jnp.float32)).astype(jnp.bfloat16)
    return high, low


def transform_kernel(core_ref, matrix_ref, signs_ref, own_ref, send_ref):
    count, block, cols = matrix_ref.shape
    half = block // 2
    core = core_ref[0]
    out_row = lax.broadcasted_iota(jnp.int32, (block, block), 0)
    in_row = lax.broadcasted_iota(jnp.int32, (block, block), 1)
    hadamard = hadamard_sign(out_row ^ core * half, in_row)
    for unit in range(count):
        high, low = two_parts(matrix_ref[unit])
        signed = (hadamard * signs_ref[pl.ds(unit, 1), :].astype(jnp.float32)).astype(jnp.bfloat16)
        result = jnp.dot(
            jnp.concatenate([signed, signed], axis=1),
            jnp.concatenate([high, low], axis=0),
            preferred_element_type=jnp.float32,
        )
        own_ref[unit] = result[:half]
        send_ref[unit] = result[half:]


def transform(core, matrix, row_signs):
    count, block, cols = matrix.shape
    step = 8
    half = jax.ShapeDtypeStruct((count, block // 2, cols), jnp.float32)
    return pl.pallas_call(
        transform_kernel,
        grid_spec=pltpu.PrefetchScalarGridSpec(
            num_scalar_prefetch=1,
            grid=(count // step,),
            in_specs=[
                pl.BlockSpec((step, block, cols), lambda i, core: (i, 0, 0)),
                pl.BlockSpec((step, block), lambda i, core: (i, 0)),
            ],
            out_specs=[
                pl.BlockSpec((step, block // 2, cols), lambda i, core: (i, 0, 0)),
                pl.BlockSpec((step, block // 2, cols), lambda i, core: (i, 0, 0)),
            ],
        ),
        out_shape=[half, half],
        compiler_params=pltpu.CompilerParams(vmem_limit_bytes=16 * MIB),
        cost_estimate=pl.CostEstimate(flops=2 * 2 * 128 * 128 * 256 * 32, bytes_accessed=8 * MIB, transcendentals=0),
        name="transform",
    )(core, matrix, row_signs)


def mix_kernel(scale, me_ref, meta_ref, own_ref, other_ref, out_ref):
    sources, _, units = meta_ref.shape
    _, half, cols = own_ref.shape
    targets = out_ref.shape[1]
    me = me_ref[0]
    target = lax.broadcasted_iota(jnp.int32, (targets, units), 0)
    sums = [jnp.zeros((targets, units), jnp.float32) for _ in range(2)]
    for source in range(sources):
        flip = 1 - 2 * parity((me >> 1) & (source >> 1))
        dests = meta_ref[source, 0:1, :]
        signs = meta_ref[source, 1:2, :] * flip
        routed = jnp.where(dests == target, signs.astype(jnp.float32), 0.0)
        sums[source & 1] = sums[source & 1] + routed
    side = (1 - 2 * (me & 1)).astype(jnp.float32)
    wide = units * 8
    unit_row = lax.broadcasted_iota(jnp.int32, (units, wide), 0)
    unit_col = lax.broadcasted_iota(jnp.int32, (units, wide), 1)
    spread = (hadamard_sign(unit_row, unit_col >> 3) * scale).astype(jnp.bfloat16)
    keep = (lax.broadcasted_iota(jnp.int32, (targets * 8, wide), 0) & 7) == (
        lax.broadcasted_iota(jnp.int32, (targets * 8, wide), 1) & 7
    )
    highs, lows = [], []
    for total in (sums[0] + side * sums[1], sums[0] - side * sums[1]):
        tall = jnp.broadcast_to(total[:, None, :], (targets, 8, units)).reshape(targets * 8, units)
        weights = jnp.dot(tall.astype(jnp.bfloat16), spread, preferred_element_type=jnp.float32)
        high, low = two_parts(jnp.where(keep, weights, 0.0))
        highs.append(high)
        lows.append(low)
    left = jnp.concatenate(highs + highs + lows, axis=1)
    for piece in range(half // 8):
        rows = pl.ds(piece * 8, 8)
        parts = [two_parts(ref[:, rows, :].reshape(wide, cols)) for ref in (own_ref, other_ref)]
        high = [part[0] for part in parts]
        low = [part[1] for part in parts]
        result = jnp.dot(left, jnp.concatenate(high + low + high, axis=0), preferred_element_type=jnp.float32)
        out_ref[piece] = result.reshape(targets, 8, cols)


def mix(scale, me, meta, own, other, targets):
    units, half, cols = own.shape
    vmem = pl.BlockSpec(memory_space=pltpu.VMEM)
    return pl.pallas_call(
        functools.partial(mix_kernel, scale),
        in_specs=[pl.BlockSpec(memory_space=pltpu.SMEM), vmem, vmem, vmem],
        out_specs=vmem,
        out_shape=jax.ShapeDtypeStruct((half // 8, targets, 8, cols), jnp.float32),
        compiler_params=pltpu.CompilerParams(vmem_limit_bytes=24 * MIB),
        cost_estimate=pl.CostEstimate(flops=2 * 3 * 128 * 512 * 256 * 8, bytes_accessed=5 * MIB, transcendentals=0),
        name="mix",
    )(me, meta, own, other)


def body(matrix, row_signs, block_dest, block_signs):
    row_count, col_count = matrix.shape
    units = block_dest.shape[0]
    block = row_count // units
    targets = SKETCH // block
    groups = lax.axis_size("grp")
    devs = lax.axis_size("row")
    total_rows = row_count * devs * groups
    scale = math.sqrt(SKETCH / total_rows) / math.sqrt(row_count * devs)
    me = lax.axis_index("row").astype(jnp.int32).reshape(1)

    mine = jnp.stack([block_dest, block_signs])
    meta = lax.all_to_all(jnp.broadcast_to(mine[None], (devs, 2, units)), "row", 0, 0)
    own, send = transform(me & 1, matrix.reshape(units, block, col_count), row_signs.reshape(units, block))
    other = lax.ppermute(send, "row", [(i, i ^ 1) for i in range(devs)])
    partial = mix(scale, me, meta, own, other, targets)

    pieces = partial.reshape(groups * targets, 8, col_count)
    same_core = [
        [g * devs + 2 * t + core for g in range(groups) for t in range(devs // 2)] for core in range(2)
    ]
    pieces = lax.all_to_all(pieces, AXES, 0, 0, axis_index_groups=same_core)
    share = jnp.sum(pieces, axis=0)
    full = lax.all_to_all(jnp.broadcast_to(share[None], (groups, 8, col_count)), "grp", 0, 0)
    return full.reshape(groups * 8, col_count)


def solution(mesh):
    return jax.shard_map(
        body,
        mesh=mesh,
        in_specs=(P(AXES, None), P(AXES), P(AXES), P(AXES)),
        out_specs=P("row", None),
        check_vma=False,
    )
```

time: 799 us -> 75.1 us (0.09)
  waiting for transfers between devices: 719 us -> 0.01 us
  blocking collectives: 0 us -> 68.1 us
  other arithmetic: 32.6 us -> 0.15 us
  matrix products: 17.8 us -> 0 us
  between operations: 13.5 us -> 0.07 us
  starting transfers between devices: 12.4 us -> 0.09 us
    ppermute x5 -> x1, waiting for transfers between devices: 551 us -> 0.01 us  [body(): other = lax.ppermute(send, 'row', [(i, i ^ 1) for i in range(devs)])]
    reduce_scatter x1 -> x0, waiting for transfers between devices: 89.8 us -> none  [body(): lax.psum_scatter(partial_value, 'row', scatter_dimension=0, tiled=True)]
    psum x1 -> x0, waiting for transfers between devices: 78.2 us -> none  [body(): summed = lax.psum(share, 'grp')]
    all_to_all x0 -> x3, blocking collectives: none -> 68.1 us  [the longest x1 39.1 us: body(): pieces = lax.all_to_all(pieces, AXES, 0, 0, axis_index_groups=same_core)]
    mul x7 -> x0, other arithmetic: 31.8 us -> none  [the longest x5 27.8 us: body(): jnp.where(upper, partner - flipped, flipped + partner) * inverse_root]
    dot_general x3 -> x0, matrix products: 17.8 us -> none  [the longest x1 7.12 us: body(): jnp.einsum('zb,abc->azc', sylvester(second_size), shaped, precision=precise)]
    ppermute x5 -> x1, starting transfers between devices: 12.3 us -> 0.09 us  [body(): other = lax.ppermute(send, 'row', [(i, i ^ 1) for i in range(devs)])]
  transfers between devices with their start and end apart: 7 -> 1, of which waited for: 7 -> 0; matrix products, arithmetic and copies ran while one was open for 0% -> 0% of each run, Pallas kernels for 0% -> 0%
where the time goes in v1:
time: 75.1 us; the launch traced here: 74.8 us
  blocking collectives  68.1 us (91%)
  local copies, waits for them, and re-layouts  3.56 us (5%)
  Pallas kernels  2.81 us (4%)
    all_to_all x1, blocking collectives, body(): pieces = lax.all_to_all(pieces, AXES, 0, 0, axis_index_groups=same_core)  39.1 us
    all_to_all x1, blocking collectives, body(): lax.all_to_all(jnp.broadcast_to(mine[None], (devs, 2, units)), 'row', 0, 0)  20.1 us
    all_to_all x1, blocking collectives, body(): lax.all_to_all(jnp.broadcast_to(share[None], (groups, 8, col_count)), 'gr...  8.9 us
    unnamed x9, local copies, waits for them, and re-layouts  3.54 us
  transfers between devices with their start and end apart: 1, of which 0 were waited for; matrix products, arithmetic and copies ran while one was open for 0% of the time, Pallas kernels for 0%

profile of v1, /device:TPU:2, one launch (start us, length us, event | category | flops | bytes accessed | tf_op | source)
XLA Modules:
  0.0 74.8 jit_solution(7434701448715190606)
XLA Ops:
  0.0 0.0 copy-start
  0.0 2.2 %copy-done = f32[4096,256]{1,0:T(8,128)S(1)} copy-done((f32[4096,256]{1,0:T(8,128)S(1)}, f32[4096,256]{1,0:T(8,128)}, u32[]{:S(2)}) %copy-start) | copy-done | bytes 4194328
  2.2 0.0 copy-start.1
  2.2 0.7 copy-done.1
  2.9 0.0 copy-start.2
  2.9 0.0 copy-start.3
  2.9 1.5 %transform.1 = (f32[32,64,256]{2,1,0:T(8,128)S(1)}, f32[32,64,256]{2,1,0:T(8,128)S(1)}) custom-call(s32[1]{0:T(128)S(6)} %and.4.core_ref, f32[32,128,256]{2,1,0:T(8,128)S(1)} %bitcast.7, s32[32,128]{1,0:T(8,128)S(1)} %bitcast.9), custom_call_target="tpu_custom_call" | custom-call | flops 536870912 | bytes 8388608 | tf_op jit(solution)/shard_map/transform/pallas_call | solution.py:55
  4.4 0.1 collective-permute-start
  4.5 0.0 copy-done.2
  4.5 0.0 copy-done.3
  4.5 20.1 %all_to_all.15.meta_ref = s32[32,2,32]{2,1,0:T(2,128)S(1)} all-to-all(s32[32,2,32]{2,1,0:T(2,128)S(1)} %broadcast_in_dim.4), channel_id=1, replica_groups=mesh['grp'=8,'row'=32] {'row'}, dimensions={0} | all-to-all | bytes 16384 | tf_op jit(solution)/shard_map/all_to_all | solution.py:140
  24.6 0.0 collective-permute-done.other_ref
  24.7 1.4 %mix.1 = f32[8,16,8,256]{3,2,1,0:T(8,128)S(1)} custom-call(s32[1]{0:T(128)} %bitcast.me_ref, s32[32,2,32]{2,1,0:T(2,128)S(1)} %all_to_all.15.meta_ref, f32[32,64,256]{2,1,0:T(8,128)S(1)} %get-tuple-element.7.own_ref, f32[32,64,256]{2,1,0:T(8,128)S(1)} %collective-permute-done.other_ref), custom_call_target="tpu_custom_call" | custom-call | flops 805306368 | bytes 5242880 | tf_op jit(solution)/shard_map/mix/pallas_call | solution.py:117
  26.0 39.1 %all_to_all.16 = f32[128,8,256]{2,1,0:T(8,128)S(1)} all-to-all(f32[128,8,256]{2,1,0:T(8,128)S(1)} %bitcast.8), channel_id=1, replica_groups={{0,2,4,6,8,10,12,14,16,18,20,22,24,26,28,30,32,34,36,38,40,42,44,46,48,..., dimensions={0} | all-to-all | bytes 2097152 | tf_op jit(solution)/shard_map/all_to_all | solution.py:149
  65.1 0.1 reduce_sum.9
  65.3 8.9 %all_to_all.17 = f32[8,8,256]{2,1,0:T(8,128)S(1)} all-to-all(f32[8,8,256]{2,1,0:T(8,128)S(1)} %broadcast_in_dim.5), channel_id=1, replica_groups=mesh['grp'=8,'row'=32] {'grp'}, dimensions={0} | all-to-all | bytes 131072 | tf_op jit(solution)/shard_map/all_to_all | solution.py:151
  74.2 0.6 copy.6
  (3 shorter events, 0.0 us)
Async XLA Ops:
  0.0 2.2 %copy-start = (f32[4096,256]{1,0:T(8,128)S(1)}, f32[4096,256]{1,0:T(8,128)}, u32[]{:S(2)}) copy-start(f32[4096,256]{1,0:T(8,128)} %param.4) | copy-start | bytes 12582916
  2.2 0.7 copy-start.1
  2.9 1.6 %copy-start.2 = (s32[32]{0:T(128)S(1)}, s32[32]{0:T(128)}, u32[]{:S(2)}) copy-start(s32[32]{0:T(128)} %param.7) | copy-start | bytes 388
  2.9 1.6 %copy-start.3 = (s32[32]{0:T(128)S(1)}, s32[32]{0:T(128)}, u32[]{:S(2)}) copy-start(s32[32]{0:T(128)} %param.6) | copy-start | bytes 388
  4.4 20.3 %collective-permute-start = (f32[32,64,256]{2,1,0:T(8,128)S(1)}, f32[32,64,256]{2,1,0:T(8,128)S(1)}, u32[]{:S(2)}, u32[]{:S(2)}) collective-permute-start(f32[32,64,256]{2,1,0:T(8,128)S(1)} %get-tuple-element.8), channel_id=1, source_target_pairs={{0,1},{1,0},{2,3},{3,2},{4,5},{5,4},{6,7},{7,6},{8,9},{9,8},{10,11... | collective-permute-start | bytes 6291464 | tf_op jit(solution)/shard_map/ppermute | solution.py:142

commit v2 on v1

v2 whole, which is shorter than its diff:
```python
import functools
import itertools
import math

import jax
import jax.numpy as jnp
from jax import lax
from jax.experimental import pallas as pl
from jax.experimental.pallas import tpu as pltpu
from jax.sharding import PartitionSpec as P

SKETCH = 2048
MIB = 1 << 20
AXES = ("grp", "row")


def parity(bits):
    for shift in (8, 4, 2, 1):
        bits = bits ^ bits >> shift
    return bits & 1


def hadamard_sign(rows, cols):
    return (1 - 2 * parity(rows & cols)).astype(jnp.float32)


def two_parts(value):
    high = value.astype(jnp.bfloat16)
    low = (value - high.astype(jnp.float32)).astype(jnp.bfloat16)
    return high, low


def transform_kernel(core_ref, matrix_hbm, signs_hbm, own_ref, send_ref, matrix_ref, signs_ref, sems, signs_sem):
    parts = matrix_ref.shape[0]
    step, block, cols = matrix_ref.shape[1:]
    half = block // 2
    signs_copy = pltpu.make_async_copy(signs_hbm, signs_ref, signs_sem)
    signs_copy.start()
    copies = [
        pltpu.make_async_copy(matrix_hbm.at[pl.ds(part * step, step)], matrix_ref.at[part], sems.at[part])
        for part in range(parts)
    ]
    for copy in copies:
        copy.start()
    core = core_ref[0]
    out_row = lax.broadcasted_iota(jnp.int32, (block, block), 0)
    in_row = lax.broadcasted_iota(jnp.int32, (block, block), 1)
    hadamard = hadamard_sign(out_row ^ core * half, in_row)
    signs_copy.wait()
    for part in range(parts):
        copies[part].wait()
        for place in range(step):
            unit = part * step + place
            high, low = two_parts(matrix_ref[part, place])
            signed = (hadamard * signs_ref[pl.ds(unit, 1), :].astype(jnp.float32)).astype(jnp.bfloat16)
            result = jnp.dot(
                jnp.concatenate([signed, signed], axis=1),
                jnp.concatenate([high, low], axis=0),
                preferred_element_type=jnp.float32,
            )
            own_ref[unit] = result[:half]
            send_ref[unit] = result[half:]


def transform(core, matrix, row_signs):
    count, block, cols = matrix.shape
    step = 2
    half = jax.ShapeDtypeStruct((count, block // 2, cols), jnp.float32)
    hbm = pl.BlockSpec(memory_space=pltpu.HBM)
    vmem = pl.BlockSpec(memory_space=pltpu.VMEM)
    return pl.pallas_call(
        transform_kernel,
        in_specs=[pl.BlockSpec(memory_space=pltpu.SMEM), hbm, hbm],
        out_specs=[vmem, vmem],
        out_shape=[half, half],
        scratch_shapes=[
            pltpu.VMEM((count // step, step, block, cols), jnp.float32),
            pltpu.VMEM((count, block), jnp.int32),
            pltpu.SemaphoreType.DMA((count // step,)),
            pltpu.SemaphoreType.DMA,
        ],
        compiler_params=pltpu.CompilerParams(vmem_limit_bytes=46 * MIB),
        cost_estimate=pl.CostEstimate(flops=2 * 2 * 128 * 128 * 256 * 32, bytes_accessed=8 * MIB, transcendentals=0),
        name="transform",
    )(core, matrix, row_signs)


def mix_kernel(scale, near, me_ref, meta_ref, own_ref, other_ref, *out_refs):
    sources, _, units = meta_ref.shape
    _, half, cols = own_ref.shape
    far = out_refs[0].shape[0]
    targets = near * far
    me = me_ref[0]
    place = lax.broadcasted_iota(jnp.int32, (targets, units), 0)
    target = place % far * near + (place // far + (me >> 1)) % near
    sums = [jnp.zeros((targets, units), jnp.float32) for _ in range(2)]
    for source in range(sources):
        flip = 1 - 2 * parity((me >> 1) & (source >> 1))
        dests = meta_ref[source, 0:1, :]
        signs = meta_ref[source, 1:2, :] * flip
        routed = jnp.where(dests == target, signs.astype(jnp.float32), 0.0)
        sums[source & 1] = sums[source & 1] + routed
    side = (1 - 2 * (me & 1)).astype(jnp.float32)
    wide = units * 8
    unit_row = lax.broadcasted_iota(jnp.int32, (units, wide), 0)
    unit_col = lax.broadcasted_iota(jnp.int32, (units, wide), 1)
    spread = (hadamard_sign(unit_row, unit_col >> 3) * scale).astype(jnp.bfloat16)
    keep = (lax.broadcasted_iota(jnp.int32, (targets * 8, wide), 0) & 7) == (
        lax.broadcasted_iota(jnp.int32, (targets * 8, wide), 1) & 7
    )
    highs, lows = [], []
    for total in (sums[0] + side * sums[1], sums[0] - side * sums[1]):
        tall = jnp.broadcast_to(total[:, None, :], (targets, 8, units)).reshape(targets * 8, units)
        weights = jnp.dot(tall.astype(jnp.bfloat16), spread, preferred_element_type=jnp.float32)
        high, low = two_parts(jnp.where(keep, weights, 0.0))
        highs.append(high)
        lows.append(low)
    left = jnp.concatenate(highs + highs + lows, axis=1)
    for piece in range(half // 8):
        rows = pl.ds(piece * 8, 8)
        parts = [two_parts(ref[:, rows, :].reshape(wide, cols)) for ref in (own_ref, other_ref)]
        high = [part[0] for part in parts]
        low = [part[1] for part in parts]
        result = jnp.dot(left, jnp.concatenate(high + low + high, axis=0), preferred_element_type=jnp.float32)
        result = result.reshape(near, far, 8, cols)
        for step, out_ref in enumerate(out_refs):
            out_ref[:, rows, :] = result[step]


def mix(scale, me, meta, own, other, near, far):
    units, half, cols = own.shape
    vmem = pl.BlockSpec(memory_space=pltpu.VMEM)
    return pl.pallas_call(
        functools.partial(mix_kernel, scale, near),
        in_specs=[pl.BlockSpec(memory_space=pltpu.SMEM), vmem, vmem, vmem],
        out_specs=[vmem] * near,
        out_shape=[jax.ShapeDtypeStruct((far, half, cols), jnp.float32)] * near,
        compiler_params=pltpu.CompilerParams(vmem_limit_bytes=24 * MIB),
        cost_estimate=pl.CostEstimate(flops=2 * 3 * 128 * 512 * 256 * 8, bytes_accessed=5 * MIB, transcendentals=0),
        name="mix",
    )(me, meta, own, other)


Y, Z_LOW, Z_HIGH, X, CORE = 4, 2, 4, 4, 2


def flat_index(y, z_low, z_high, x, core):
    return (((y % Y * Z_LOW + z_low) * Z_HIGH + z_high) * X + x % X) * CORE + core


def places():
    return itertools.product(range(Y), range(Z_LOW), range(Z_HIGH), range(X), range(CORE))


def shifted(value, y=0, x=0):
    pairs = [(flat_index(*p), flat_index(p[0] + y, p[1], p[2], p[3] + x, p[4])) for p in places()]
    return lax.ppermute(value, AXES, pairs)


def body(matrix, row_signs, block_dest, block_signs):
    row_count, col_count = matrix.shape
    units = block_dest.shape[0]
    block = row_count // units
    groups = lax.axis_size("grp")
    devs = lax.axis_size("row")
    total_rows = row_count * devs * groups
    scale = math.sqrt(SKETCH / total_rows) / math.sqrt(row_count * devs)
    me = lax.axis_index("row").astype(jnp.int32).reshape(1)

    mine = jnp.stack([block_dest, block_signs])
    meta = lax.all_to_all(jnp.broadcast_to(mine[None], (devs, 2, units)), "row", 0, 0)
    own, send = transform(me & 1, matrix.reshape(units, block, col_count), row_signs.reshape(units, block))
    other = lax.ppermute(send, "row", [(i, i ^ 1) for i in range(devs)])
    part, *rest = mix(scale, me, meta, own, other, X, Z_HIGH)

    got = {step: shifted(rest[step - 1], x=step) for step in (2, 1, 3)}
    part = part + got[2] + (got[1] + got[3])
    lines = [
        [flat_index(y, z_low, z_high, x, core) for z_low in range(Z_LOW) for z_high in range(Z_HIGH)]
        for y in range(Y)
        for x in range(X)
        for core in range(CORE)
    ]
    both = jnp.broadcast_to(part[None], (Z_LOW, *part.shape)).reshape(Z_LOW * Z_HIGH, *part.shape[1:])
    part = jnp.sum(lax.all_to_all(both, AXES, 0, 0, axis_index_groups=lines), axis=0)
    got = {step: shifted(part, y=step) for step in (2, 1, 3)}
    return (part + got[2]) + (got[1] + got[3])


def solution(mesh):
    return jax.shard_map(
        body,
        mesh=mesh,
        in_specs=(P(AXES, None), P(AXES), P(AXES), P(AXES)),
        out_specs=P("row", None),
        check_vma=False,
    )
```

time: 75.1 us -> 72 us (0.959)
  the two profiles are of different devices: /device:TPU:2 before, /device:TPU:56 now
where the time goes in v2:
time: 72 us; the launch traced here: 71.8 us
  blocking collectives  40.1 us (56%)
  waiting for transfers between devices  16.5 us (23%)
  starting transfers between devices  8.06 us (11%)
  Pallas kernels  5.54 us (8%)
  local copies, waits for them, and re-layouts  0.77 us (1%)
  other arithmetic  0.76 us (1%)
    all_to_all x1, blocking collectives, body(): lax.all_to_all(jnp.broadcast_to(mine[None], (devs, 2, units)), 'row', 0, 0)  20.1 us
    all_to_all x1, blocking collectives, body(): lax.all_to_all(both, AXES, 0, 0, axis_index_groups=lines)  19.9 us
    ppermute x6, waiting for transfers between devices, shifted(): return lax.ppermute(value, AXES, pairs)  16.5 us
    ppermute x6, starting transfers between devices, shifted(): return lax.ppermute(value, AXES, pairs)  7.97 us
    pallas_call x1, Pallas kernels, transform(): pl.pallas_call(transform_kernel, in_specs=[pl.BlockSpec(memory_space=pltp...  4.21 us
  transfers between devices with their start and end apart: 7, of which 4 were waited for; matrix products, arithmetic and copies ran while one was open for 0% of the time, Pallas kernels for 0%

profile of v2, /device:TPU:56, one launch (start us, length us, event | category | flops | bytes accessed | tf_op | source)
XLA Modules:
  0.0 71.8 jit_solution(7817779046672053546)
XLA Ops:
  0.0 0.0 copy-start
  0.0 0.7 copy-done
  0.7 0.0 copy-start.1
  0.7 0.0 copy-start.2
  0.7 4.2 %transform.1 = (f32[32,64,256]{2,1,0:T(8,128)S(1)}, f32[32,64,256]{2,1,0:T(8,128)S(1)}) custom-call(s32[1]{0:T(128)S(6)} %and.4.core_ref, f32[32,128,256]{2,1,0:T(8,128)} %bitcast.7, s32[32,128]{1,0:T(8,128)S(1)} %bitcast.6), custom_call_target="tpu_custom_call" | custom-call | flops 536870912 | bytes 8388608 | tf_op jit(solution)/shard_map/transform/pallas_call | solution.py:71
  4.9 0.1 collective-permute-start
  5.0 0.0 copy-done.1
  5.1 0.0 copy-done.2
  5.1 20.1 %all_to_all.10.meta_ref = s32[32,2,32]{2,1,0:T(2,128)S(1)} all-to-all(s32[32,2,32]{2,1,0:T(2,128)S(1)} %broadcast_in_dim.4), channel_id=1, replica_groups=mesh['grp'=8,'row'=32] {'row'}, dimensions={0} | all-to-all | bytes 16384 | tf_op jit(solution)/shard_map/all_to_all | solution.py:171
  25.2 0.0 collective-permute-done.other_ref
  25.2 1.3 %mix.1 = (f32[4,64,256]{2,1,0:T(8,128)S(1)}, f32[4,64,256]{2,1,0:T(8,128)S(1)}, f32[4,64,256]{2,1,0:T(8,128)S(1)}, f32[4,64,256]{2,1,0:T(8,128)S(1)}) custom-call(s32[1]{0:T(128)} %bitcast.me_ref, s32[32,2,32]{2,1,0:T(2,128)S(1)} %all_to_all.10.meta_ref, f32[32,64,256]{2,1,0:T(8,128)S(1)} %get-tuple-element.11.own_ref, ...), custom_call_target="tpu_custom_call" | custom-call | flops 805306368 | bytes 5242880 | tf_op jit(solution)/shard_map/mix/pallas_call | solution.py:133
  26.6 1.2 %collective-permute-start.1 = (f32[4,64,256]{2,1,0:T(8,128)S(1)}, f32[4,64,256]{2,1,0:T(8,128)S(1)}, u32[]{:S(2)}, u32[]{:S(2)}) collective-permute-start(f32[4,64,256]{2,1,0:T(8,128)S(1)} %get-tuple-element.14), channel_id=1, source_target_pairs={{0,4},{1,5},{2,6},{3,7},{4,0},{5,1},{6,2},{7,3},{8,12},{9,13},{10,... | collective-permute-start | bytes 786440 | tf_op jit(solution)/shard_map/ppermute | solution.py:157
  27.8 0.9 %collective-permute-start.2 = (f32[4,64,256]{2,1,0:T(8,128)S(1)}, f32[4,64,256]{2,1,0:T(8,128)S(1)}, u32[]{:S(2)}, u32[]{:S(2)}) collective-permute-start(f32[4,64,256]{2,1,0:T(8,128)S(1)} %get-tuple-element.15), channel_id=1, source_target_pairs={{0,2},{1,3},{2,4},{3,5},{4,6},{5,7},{6,0},{7,1},{8,10},{9,11},{10,... | collective-permute-start | bytes 786440 | tf_op jit(solution)/shard_map/ppermute | solution.py:157
  28.7 2.3 %collective-permute-start.3 = (f32[4,64,256]{2,1,0:T(8,128)S(1)}, f32[4,64,256]{2,1,0:T(8,128)S(1)}, u32[]{:S(2)}, u32[]{:S(2)}) collective-permute-start(f32[4,64,256]{2,1,0:T(8,128)S(1)} %get-tuple-element.16), channel_id=1, source_target_pairs={{0,6},{1,7},{2,0},{3,1},{4,2},{5,3},{6,4},{7,5},{8,14},{9,15},{10,... | collective-permute-start | bytes 786440 | tf_op jit(solution)/shard_map/ppermute | solution.py:157
  31.0 6.3 %collective-permute-done.1 = f32[4,64,256]{2,1,0:T(8,128)S(1)} collective-permute-done((f32[4,64,256]{2,1,0:T(8,128)S(1)}, f32[4,64,256]{2,1,0:T(8,128)S(1)}, u32[]{:S(2)}, u32[]{:S(2)}) %collective-permute-start.1) | collective-permute-done | bytes 262176 | tf_op jit(solution)/shard_map/ppermute | solution.py:157
  37.3 4.7 %collective-permute-done.2 = f32[4,64,256]{2,1,0:T(8,128)S(1)} collective-permute-done((f32[4,64,256]{2,1,0:T(8,128)S(1)}, f32[4,64,256]{2,1,0:T(8,128)S(1)}, u32[]{:S(2)}, u32[]{:S(2)}) %collective-permute-start.2) | collective-permute-done | bytes 262176 | tf_op jit(solution)/shard_map/ppermute | solution.py:157
  42.1 0.0 collective-permute-done.3
  42.1 0.1 add_add_fusion
  42.2 19.9 %all_to_all.11 = f32[8,64,256]{2,1,0:T(8,128)S(1)} all-to-all(f32[8,64,256]{2,1,0:T(8,128)S(1)} %bitcast.8), channel_id=1, replica_groups={{0,8,16,24,32,40,48,56},{1,9,17,25,33,41,49,57},{2,10,18,26,34,42,50,58..., dimensions={0} | all-to-all | bytes 1048576 | tf_op jit(solution)/shard_map/all_to_all | solution.py:185
  62.2 1.3 %collective-permute-start.4 = (f32[64,256]{1,0:T(8,128)S(1)}, f32[64,256]{1,0:T(8,128)S(1)}, u32[]{:S(2)}, u32[]{:S(2)}) collective-permute-start(f32[64,256]{1,0:T(8,128)S(1)} %reduce_sum.9), channel_id=1, source_target_pairs={{0,128},{1,129},{2,130},{3,131},{4,132},{5,133},{6,134},{7,135},{8... | collective-permute-start | bytes 196616 | tf_op jit(solution)/shard_map/ppermute | solution.py:157
  63.5 2.2 %collective-permute-start.5 = (f32[64,256]{1,0:T(8,128)S(1)}, f32[64,256]{1,0:T(8,128)S(1)}, u32[]{:S(2)}, u32[]{:S(2)}) collective-permute-start(f32[64,256]{1,0:T(8,128)S(1)} %reduce_sum.9), channel_id=1, source_target_pairs={{0,64},{1,65},{2,66},{3,67},{4,68},{5,69},{6,70},{7,71},{8,72},{9,... | collective-permute-start | bytes 196616 | tf_op jit(solution)/shard_map/ppermute | solution.py:157
  65.7 0.0 collective-permute-start.6
  65.7 2.4 %collective-permute-done.4 = f32[64,256]{1,0:T(8,128)S(1)} collective-permute-done((f32[64,256]{1,0:T(8,128)S(1)}, f32[64,256]{1,0:T(8,128)S(1)}, u32[]{:S(2)}, u32[]{:S(2)}) %collective-permute-start.4) | collective-permute-done | bytes 65568 | tf_op jit(solution)/shard_map/ppermute | solution.py:157
  68.1 0.0 collective-permute-done.5
  68.1 3.1 %collective-permute-done.6 = f32[64,256]{1,0:T(8,128)S(1)} collective-permute-done((f32[64,256]{1,0:T(8,128)S(1)}, f32[64,256]{1,0:T(8,128)S(1)}, u32[]{:S(2)}, u32[]{:S(2)}) %collective-permute-start.6) | collective-permute-done | bytes 65568 | tf_op jit(solution)/shard_map/ppermute | solution.py:157
  71.2 0.6 add_add_fusion.1
  (4 shorter events, 0.1 us)
Async XLA Ops:
  0.0 0.7 copy-start
  0.7 4.3 %copy-start.1 = (s32[32]{0:T(128)S(1)}, s32[32]{0:T(128)}, u32[]{:S(2)}) copy-start(s32[32]{0:T(128)} %param.7) | copy-start | bytes 388
  0.7 4.3 %copy-start.2 = (s32[32]{0:T(128)S(1)}, s32[32]{0:T(128)}, u32[]{:S(2)}) copy-start(s32[32]{0:T(128)} %param.6) | copy-start | bytes 388
  4.9 20.3 %collective-permute-start = (f32[32,64,256]{2,1,0:T(8,128)S(1)}, f32[32,64,256]{2,1,0:T(8,128)S(1)}, u32[]{:S(2)}, u32[]{:S(2)}) collective-permute-start(f32[32,64,256]{2,1,0:T(8,128)S(1)} %get-tuple-element.12), channel_id=1, source_target_pairs={{0,1},{1,0},{2,3},{3,2},{4,5},{5,4},{6,7},{7,6},{8,9},{9,8},{10,11... | collective-permute-start | bytes 6291464 | tf_op jit(solution)/shard_map/ppermute | solution.py:173
  26.6 10.8 %collective-permute-start.1 = (f32[4,64,256]{2,1,0:T(8,128)S(1)}, f32[4,64,256]{2,1,0:T(8,128)S(1)}, u32[]{:S(2)}, u32[]{:S(2)}) collective-permute-start(f32[4,64,256]{2,1,0:T(8,128)S(1)} %get-tuple-element.14), channel_id=1, source_target_pairs={{0,4},{1,5},{2,6},{3,7},{4,0},{5,1},{6,2},{7,3},{8,12},{9,13},{10,... | collective-permute-start | bytes 786440 | tf_op jit(solution)/shard_map/ppermute | solution.py:157
  27.8 14.3 %collective-permute-start.2 = (f32[4,64,256]{2,1,0:T(8,128)S(1)}, f32[4,64,256]{2,1,0:T(8,128)S(1)}, u32[]{:S(2)}, u32[]{:S(2)}) collective-permute-start(f32[4,64,256]{2,1,0:T(8,128)S(1)} %get-tuple-element.15), channel_id=1, source_target_pairs={{0,2},{1,3},{2,4},{3,5},{4,6},{5,7},{6,0},{7,1},{8,10},{9,11},{10,... | collective-permute-start | bytes 786440 | tf_op jit(solution)/shard_map/ppermute | solution.py:157
  28.7 13.4 %collective-permute-start.3 = (f32[4,64,256]{2,1,0:T(8,128)S(1)}, f32[4,64,256]{2,1,0:T(8,128)S(1)}, u32[]{:S(2)}, u32[]{:S(2)}) collective-permute-start(f32[4,64,256]{2,1,0:T(8,128)S(1)} %get-tuple-element.16), channel_id=1, source_target_pairs={{0,6},{1,7},{2,0},{3,1},{4,2},{5,3},{6,4},{7,5},{8,14},{9,15},{10,... | collective-permute-start | bytes 786440 | tf_op jit(solution)/shard_map/ppermute | solution.py:157
  62.2 5.9 %collective-permute-start.4 = (f32[64,256]{1,0:T(8,128)S(1)}, f32[64,256]{1,0:T(8,128)S(1)}, u32[]{:S(2)}, u32[]{:S(2)}) collective-permute-start(f32[64,256]{1,0:T(8,128)S(1)} %reduce_sum.9), channel_id=1, source_target_pairs={{0,128},{1,129},{2,130},{3,131},{4,132},{5,133},{6,134},{7,135},{8... | collective-permute-start | bytes 196616 | tf_op jit(solution)/shard_map/ppermute | solution.py:157
  63.5 4.6 %collective-permute-start.5 = (f32[64,256]{1,0:T(8,128)S(1)}, f32[64,256]{1,0:T(8,128)S(1)}, u32[]{:S(2)}, u32[]{:S(2)}) collective-permute-start(f32[64,256]{1,0:T(8,128)S(1)} %reduce_sum.9), channel_id=1, source_target_pairs={{0,64},{1,65},{2,66},{3,67},{4,68},{5,69},{6,70},{7,71},{8,72},{9,... | collective-permute-start | bytes 196616 | tf_op jit(solution)/shard_map/ppermute | solution.py:157
  65.7 5.5 %collective-permute-start.6 = (f32[64,256]{1,0:T(8,128)S(1)}, f32[64,256]{1,0:T(8,128)S(1)}, u32[]{:S(2)}, u32[]{:S(2)}) collective-permute-start(f32[64,256]{1,0:T(8,128)S(1)} %reduce_sum.9), channel_id=1, source_target_pairs={{0,192},{1,193},{2,194},{3,195},{4,196},{5,197},{6,198},{7,199},{8... | collective-permute-start | bytes 196616 | tf_op jit(solution)/shard_map/ppermute | solution.py:157

commit v3 on v2

--- a/solution.py
+++ b/solution.py
@@ -11,6 +11,7 @@
 
 SKETCH = 2048
 MIB = 1 << 20
+AHEAD = 2
 AXES = ("grp", "row")
 
 
@@ -30,7 +31,7 @@
     return high, low
 
 
-def transform_kernel(core_ref, matrix_hbm, signs_hbm, own_ref, send_ref, matrix_ref, signs_ref, sems, signs_sem):
+def transform_kernel(place_ref, matrix_hbm, signs_hbm, own_ref, send_ref, matrix_ref, signs_ref, sems, signs_sem):
     parts = matrix_ref.shape[0]
     step, block, cols = matrix_ref.shape[1:]
     half = block // 2
@@ -40,15 +41,17 @@
         pltpu.make_async_copy(matrix_hbm.at[pl.ds(part * step, step)], matrix_ref.at[part], sems.at[part])
         for part in range(parts)
     ]
-    for copy in copies:
+    for copy in copies[:AHEAD]:
         copy.start()
-    core = core_ref[0]
+    core = place_ref[0] & 1
     out_row = lax.broadcasted_iota(jnp.int32, (block, block), 0)
     in_row = lax.broadcasted_iota(jnp.int32, (block, block), 1)
     hadamard = hadamard_sign(out_row ^ core * half, in_row)
     signs_copy.wait()
     for part in range(parts):
         copies[part].wait()
+        if part + AHEAD < parts:
+            copies[part + AHEAD].start()
         for place in range(step):
             unit = part * step + place
             high, low = two_parts(matrix_ref[part, place])
@@ -62,9 +65,9 @@
             send_ref[unit] = result[half:]
 
 
-def transform(core, matrix, row_signs):
+def transform(place, matrix, row_signs):
     count, block, cols = matrix.shape
-    step = 2
+    step = 4
     half = jax.ShapeDtypeStruct((count, block // 2, cols), jnp.float32)
     hbm = pl.BlockSpec(memory_space=pltpu.HBM)
     vmem = pl.BlockSpec(memory_space=pltpu.VMEM)
@@ -82,17 +85,20 @@
         compiler_params=pltpu.CompilerParams(vmem_limit_bytes=46 * MIB),
         cost_estimate=pl.CostEstimate(flops=2 * 2 * 128 * 128 * 256 * 32, bytes_accessed=8 * MIB, transcendentals=0),
         name="transform",
-    )(core, matrix, row_signs)
-
-
-def mix_kernel(scale, near, me_ref, meta_ref, own_ref, other_ref, *out_refs):
+    )(place, matrix, row_signs)
+
+
+def mix_kernel(scale, near, place_ref, meta_ref, own_ref, other_ref, *out_refs):
+    _, half, cols = own_ref.shape
+    _, low_count, far = out_refs[0].shape[:3]
+    targets = near * far
     sources, _, units = meta_ref.shape
-    _, half, cols = own_ref.shape
-    far = out_refs[0].shape[0]
-    targets = near * far
-    me = me_ref[0]
+    me = place_ref[0] % sources
+    core = me & 1
+    first_x = jnp.where(core == 0, me >> 1, 0)
+    first_y = jnp.where(core == 0, 0, place_ref[0] // sources // low_count)
     place = lax.broadcasted_iota(jnp.int32, (targets, units), 0)
-    target = place % far * near + (place // far + (me >> 1)) % near
+    target = place % far * near + (place // far + first_x) % near
     sums = [jnp.zeros((targets, units), jnp.float32) for _ in range(2)]
     for source in range(sources):
         flip = 1 - 2 * parity((me >> 1) & (source >> 1))
@@ -116,29 +122,38 @@
         highs.append(high)
         lows.append(low)
     left = jnp.concatenate(highs + highs + lows, axis=1)
-    for piece in range(half // 8):
-        rows = pl.ds(piece * 8, 8)
+    for step, low_z in itertools.product(range(near), range(low_count)):
+        piece = (first_y + step) % near * low_count + low_z
+        rows = pl.ds(pl.multiple_of(piece * 8, 8), 8)
         parts = [two_parts(ref[:, rows, :].reshape(wide, cols)) for ref in (own_ref, other_ref)]
         high = [part[0] for part in parts]
         low = [part[1] for part in parts]
         result = jnp.dot(left, jnp.concatenate(high + low + high, axis=0), preferred_element_type=jnp.float32)
         result = result.reshape(near, far, 8, cols)
-        for step, out_ref in enumerate(out_refs):
-            out_ref[:, rows, :] = result[step]
-
-
-def mix(scale, me, meta, own, other, near, far):
+
+        @pl.when(core == 0)
+        def _():
+            for turn, out_ref in enumerate(out_refs):
+                out_ref[step, low_z] = result[turn]
+
+        @pl.when(core == 1)
+        def _():
+            for turn in range(near):
+                out_refs[step][turn, low_z] = result[turn]
+
+
+def mix(scale, place, meta, own, other, near, low_count, far):
     units, half, cols = own.shape
     vmem = pl.BlockSpec(memory_space=pltpu.VMEM)
     return pl.pallas_call(
         functools.partial(mix_kernel, scale, near),
         in_specs=[pl.BlockSpec(memory_space=pltpu.SMEM), vmem, vmem, vmem],
         out_specs=[vmem] * near,
-        out_shape=[jax.ShapeDtypeStruct((far, half, cols), jnp.float32)] * near,
+        out_shape=[jax.ShapeDtypeStruct((near, low_count, far, 8, cols), jnp.float32)] * near,
         compiler_params=pltpu.CompilerParams(vmem_limit_bytes=24 * MIB),
         cost_estimate=pl.CostEstimate(flops=2 * 3 * 128 * 512 * 256 * 8, bytes_accessed=5 * MIB, transcendentals=0),
         name="mix",
-    )(me, meta, own, other)
+    )(place, meta, own, other)
 
 
 Y, Z_LOW, Z_HIGH, X, CORE = 4, 2, 4, 4, 2
@@ -152,9 +167,25 @@
     return itertools.product(range(Y), range(Z_LOW), range(Z_HIGH), range(X), range(CORE))
 
 
-def shifted(value, y=0, x=0):
-    pairs = [(flat_index(*p), flat_index(p[0] + y, p[1], p[2], p[3] + x, p[4])) for p in places()]
+def first_shift(value, step):
+    pairs = []
+    for y, z_low, z_high, x, core in places():
+        to = (y, z_low, z_high, x + step, core) if core == 0 else (y + step, z_low, z_high, x, core)
+        pairs.append((flat_index(y, z_low, z_high, x, core), flat_index(*to)))
     return lax.ppermute(value, AXES, pairs)
+
+
+def second_groups():
+    groups = []
+    for core, fixed in itertools.product(range(CORE), range(X)):
+        members = itertools.product(range(Y), range(Z_LOW), range(Z_HIGH))
+        groups.append(
+            [
+                flat_index(free, z_low, z_high, fixed, core) if core == 0 else flat_index(fixed, z_low, z_high, free, core)
+                for free, z_low, z_high in members
+            ]
+        )
+    return groups
 
 
 def body(matrix, row_signs, block_dest, block_signs):
@@ -165,26 +196,21 @@
     devs = lax.axis_size("row")
     total_rows = row_count * devs * groups
     scale = math.sqrt(SKETCH / total_rows) / math.sqrt(row_count * devs)
-    me = lax.axis_index("row").astype(jnp.int32).reshape(1)
+    place = lax.axis_index(AXES).astype(jnp.int32).reshape(1)
 
     mine = jnp.stack([block_dest, block_signs])
     meta = lax.all_to_all(jnp.broadcast_to(mine[None], (devs, 2, units)), "row", 0, 0)
-    own, send = transform(me & 1, matrix.reshape(units, block, col_count), row_signs.reshape(units, block))
+    own, send = transform(place, matrix.reshape(units, block, col_count), row_signs.reshape(units, block))
     other = lax.ppermute(send, "row", [(i, i ^ 1) for i in range(devs)])
-    part, *rest = mix(scale, me, meta, own, other, X, Z_HIGH)
-
-    got = {step: shifted(rest[step - 1], x=step) for step in (2, 1, 3)}
-    part = part + got[2] + (got[1] + got[3])
-    lines = [
-        [flat_index(y, z_low, z_high, x, core) for z_low in range(Z_LOW) for z_high in range(Z_HIGH)]
-        for y in range(Y)
-        for x in range(X)
-        for core in range(CORE)
-    ]
-    both = jnp.broadcast_to(part[None], (Z_LOW, *part.shape)).reshape(Z_LOW * Z_HIGH, *part.shape[1:])
-    part = jnp.sum(lax.all_to_all(both, AXES, 0, 0, axis_index_groups=lines), axis=0)
-    got = {step: shifted(part, y=step) for step in (2, 1, 3)}
-    return (part + got[2]) + (got[1] + got[3])
+    part, *rest = mix(scale, place, meta, own, other, X, Z_LOW, Z_HIGH)
+
+    got = {step: first_shift(rest[step - 1], step) for step in (2, 1, 3)}
+    part = (part + got[2]) + (got[1] + got[3])
+    pieces = part.reshape(-1, 8, col_count)
+    pieces = lax.all_to_all(pieces, AXES, 0, 0, axis_index_groups=second_groups())
+    share = jnp.sum(pieces, axis=0)
+    full = lax.all_to_all(jnp.broadcast_to(share[None], (groups, 8, col_count)), "grp", 0, 0)
+    return full.reshape(groups * 8, col_count)
 
 
 def solution(mesh):

time: 72 us -> 66.8 us (0.928)
  the two profiles are of different devices: /device:TPU:56 before, /device:TPU:2 now
where the time goes in v3:
time: 66.8 us; the launch traced here: 66.5 us
  blocking collectives  46.2 us (69%)
  Pallas kernels  7.9 us (12%)
  waiting for transfers between devices  7.18 us (11%)
  starting transfers between devices  3.69 us (6%)
  local copies, waits for them, and re-layouts  1.37 us (2%)
    all_to_all x1, blocking collectives, body(): lax.all_to_all(jnp.broadcast_to(mine[None], (devs, 2, units)), 'row', 0, 0)  20.1 us
    all_to_all x1, blocking collectives, body(): lax.all_to_all(pieces, AXES, 0, 0, axis_index_groups=second_groups())  15.8 us
    all_to_all x1, blocking collectives, body(): lax.all_to_all(jnp.broadcast_to(share[None], (groups, 8, col_count)), 'gr...  10.3 us
    ppermute x3, waiting for transfers between devices, first_shift(): return lax.ppermute(value, AXES, pairs)  7.17 us
    pallas_call x1, Pallas kernels, transform(): pl.pallas_call(transform_kernel, in_specs=[pl.BlockSpec(memory_space=pltp...  4.86 us
    ppermute x3, starting transfers between devices, first_shift(): return lax.ppermute(value, AXES, pairs)  3.6 us
    pallas_call x1, Pallas kernels, mix(): pl.pallas_call(functools.partial(mix_kernel, scale, near), in_specs=[pl.B...  3.04 us
    unnamed x7, local copies, waits for them, and re-layouts  1.35 us
  transfers between devices with their start and end apart: 4, of which 3 were waited for; matrix products, arithmetic and copies ran while one was open for 0% of the time, Pallas kernels for 0%

profile of v3, /device:TPU:2, one launch (start us, length us, event | category | flops | bytes accessed | tf_op | source)
XLA Modules:
  0.0 66.5 jit_solution(16778745889105254040)
XLA Ops:
  0.0 0.0 copy-start
  0.0 0.7 %copy-done = s32[4096]{0:T(1024)S(1)} copy-done((s32[4096]{0:T(1024)S(1)}, s32[4096]{0:T(1024)}, u32[]{:S(2)}) %copy-start) | copy-done | bytes 16408
  0.7 0.0 copy-start.1
  0.7 0.0 copy-start.2
  0.7 4.9 %transform.1 = (f32[32,64,256]{2,1,0:T(8,128)S(1)}, f32[32,64,256]{2,1,0:T(8,128)S(1)}) custom-call(s32[1]{0:T(128)} %bitcast.place_ref, f32[32,128,256]{2,1,0:T(8,128)} %bitcast.8, s32[32,128]{1,0:T(8,128)S(1)} %bitcast.7), custom_call_target="tpu_custom_call" | custom-call | flops 536870912 | bytes 8388608 | tf_op jit(solution)/shard_map/transform/pallas_call | solution.py:74
  5.6 0.1 collective-permute-start
  5.7 0.0 copy-done.1
  5.7 0.0 copy-done.2
  5.7 20.1 %all_to_all.15.meta_ref = s32[32,2,32]{2,1,0:T(2,128)S(1)} all-to-all(s32[32,2,32]{2,1,0:T(2,128)S(1)} %broadcast_in_dim.4), channel_id=1, replica_groups=mesh['grp'=8,'row'=32] {'row'}, dimensions={0} | all-to-all | bytes 16384 | tf_op jit(solution)/shard_map/all_to_all | solution.py:202
  25.9 0.0 collective-permute-done.other_ref
  25.9 3.0 %mix.1 = (f32[4,2,4,8,256]{4,3,2,1,0:T(8,128)S(1)}, f32[4,2,4,8,256]{4,3,2,1,0:T(8,128)S(1)}, f32[4,2,4,8,256]{4,3,2,1,0:T(8,128)S(1)}, f32[4,2,4,8,256]{4,3,2,1,0:T(8,128)S(1)}) custom-call(s32[1]{0:T(128)} %bitcast.place_ref, s32[32,2,32]{2,1,0:T(2,128)S(1)} %all_to_all.15.meta_ref, f32[32,64,256]{2,1,0:T(8,128)S(1)} %get-tuple-element.11.own_ref, ...), custom_call_target="tpu_custom_call" | custom-call | flops 805306368 | bytes 5242880 | tf_op jit(solution)/shard_map/mix/pallas_call | solution.py:148
  28.9 1.6 %collective-permute-start.1 = (f32[4,2,4,8,256]{4,3,2,1,0:T(8,128)S(1)}, f32[4,2,4,8,256]{4,3,2,1,0:T(8,128)S(1)}, u32[]{:S(2)}, u32[]{:S(2)}) collective-permute-start(f32[4,2,4,8,256]{4,3,2,1,0:T(8,128)S(1)} %get-tuple-element.14), channel_id=1, source_target_pairs={{0,4},{1,129},{2,6},{3,131},{4,0},{5,133},{6,2},{7,135},{8,12},{9,... | collective-permute-start | bytes 786440 | tf_op jit(solution)/shard_map/ppermute | solution.py:175
  30.5 1.5 %collective-permute-start.2 = (f32[4,2,4,8,256]{4,3,2,1,0:T(8,128)S(1)}, f32[4,2,4,8,256]{4,3,2,1,0:T(8,128)S(1)}, u32[]{:S(2)}, u32[]{:S(2)}) collective-permute-start(f32[4,2,4,8,256]{4,3,2,1,0:T(8,128)S(1)} %get-tuple-element.15), channel_id=1, source_target_pairs={{0,2},{1,65},{2,4},{3,67},{4,6},{5,69},{6,0},{7,71},{8,10},{9,73},... | collective-permute-start | bytes 786440 | tf_op jit(solution)/shard_map/ppermute | solution.py:175
  31.9 0.6 collective-permute-start.3
  32.5 4.5 %collective-permute-done.1 = f32[4,2,4,8,256]{4,3,2,1,0:T(8,128)S(1)} collective-permute-done((f32[4,2,4,8,256]{4,3,2,1,0:T(8,128)S(1)}, f32[4,2,4,8,256]{4,3,2,1,0:T(8,128)S(1)}, u32[]{:S(2)}, u32[]{:S(2)}) %collective-permute-start.1) | collective-permute-done | bytes 262176 | tf_op jit(solution)/shard_map/ppermute | solution.py:175
  37.0 1.8 %collective-permute-done.2 = f32[4,2,4,8,256]{4,3,2,1,0:T(8,128)S(1)} collective-permute-done((f32[4,2,4,8,256]{4,3,2,1,0:T(8,128)S(1)}, f32[4,2,4,8,256]{4,3,2,1,0:T(8,128)S(1)}, u32[]{:S(2)}, u32[]{:S(2)}) %collective-permute-start.2) | collective-permute-done | bytes 262176 | tf_op jit(solution)/shard_map/ppermute | solution.py:175
  38.8 0.9 %collective-permute-done.3 = f32[4,2,4,8,256]{4,3,2,1,0:T(8,128)S(1)} collective-permute-done((f32[4,2,4,8,256]{4,3,2,1,0:T(8,128)S(1)}, f32[4,2,4,8,256]{4,3,2,1,0:T(8,128)S(1)}, u32[]{:S(2)}, u32[]{:S(2)}) %collective-permute-start.3) | collective-permute-done | bytes 262176 | tf_op jit(solution)/shard_map/ppermute | solution.py:175
  39.7 0.1 add_add_fusion
  39.8 15.8 %all_to_all.16 = f32[32,8,256]{2,1,0:T(8,128)S(1)} all-to-all(f32[32,8,256]{2,1,0:T(8,128)S(1)} %bitcast.9), channel_id=1, replica_groups={{0,8,16,24,32,40,48,56,64,72,80,88,96,104,112,120,128,136,144,152,160,1..., dimensions={0} | all-to-all | bytes 524288 | tf_op jit(solution)/shard_map/all_to_all | solution.py:210
  55.6 10.3 %all_to_all.17 = f32[8,8,256]{2,1,0:T(8,128)S(1)} all-to-all(f32[8,8,256]{2,1,0:T(8,128)S(1)} %broadcast_in_dim.5), channel_id=1, replica_groups=mesh['grp'=8,'row'=32] {'grp'}, dimensions={0} | all-to-all | bytes 131072 | tf_op jit(solution)/shard_map/all_to_all | solution.py:212
  65.9 0.6 copy.6
  (4 shorter events, 0.1 us)
Async XLA Ops:
  0.0 0.7 %copy-start = (s32[4096]{0:T(1024)S(1)}, s32[4096]{0:T(1024)}, u32[]{:S(2)}) copy-start(s32[4096]{0:T(1024)} %param.5) | copy-start | bytes 49156
  0.7 5.0 %copy-start.1 = (s32[32]{0:T(128)S(1)}, s32[32]{0:T(128)}, u32[]{:S(2)}) copy-start(s32[32]{0:T(128)} %param.7) | copy-start | bytes 388
  0.7 5.0 %copy-start.2 = (s32[32]{0:T(128)S(1)}, s32[32]{0:T(128)}, u32[]{:S(2)}) copy-start(s32[32]{0:T(128)} %param.6) | copy-start | bytes 388
  5.6 20.3 %collective-permute-start = (f32[32,64,256]{2,1,0:T(8,128)S(1)}, f32[32,64,256]{2,1,0:T(8,128)S(1)}, u32[]{:S(2)}, u32[]{:S(2)}) collective-permute-start(f32[32,64,256]{2,1,0:T(8,128)S(1)} %get-tuple-element.12), channel_id=1, source_target_pairs={{0,1},{1,0},{2,3},{3,2},{4,5},{5,4},{6,7},{7,6},{8,9},{9,8},{10,11... | collective-permute-start | bytes 6291464 | tf_op jit(solution)/shard_map/ppermute | solution.py:204
  28.9 8.1 %collective-permute-start.1 = (f32[4,2,4,8,256]{4,3,2,1,0:T(8,128)S(1)}, f32[4,2,4,8,256]{4,3,2,1,0:T(8,128)S(1)}, u32[]{:S(2)}, u32[]{:S(2)}) collective-permute-start(f32[4,2,4,8,256]{4,3,2,1,0:T(8,128)S(1)} %get-tuple-element.14), channel_id=1, source_target_pairs={{0,4},{1,129},{2,6},{3,131},{4,0},{5,133},{6,2},{7,135},{8,12},{9,... | collective-permute-start | bytes 786440 | tf_op jit(solution)/shard_map/ppermute | solution.py:175
  30.5 8.3 %collective-permute-start.2 = (f32[4,2,4,8,256]{4,3,2,1,0:T(8,128)S(1)}, f32[4,2,4,8,256]{4,3,2,1,0:T(8,128)S(1)}, u32[]{:S(2)}, u32[]{:S(2)}) collective-permute-start(f32[4,2,4,8,256]{4,3,2,1,0:T(8,128)S(1)} %get-tuple-element.15), channel_id=1, source_target_pairs={{0,2},{1,65},{2,4},{3,67},{4,6},{5,69},{6,0},{7,71},{8,10},{9,73},... | collective-permute-start | bytes 786440 | tf_op jit(solution)/shard_map/ppermute | solution.py:175
  31.9 7.8 %collective-permute-start.3 = (f32[4,2,4,8,256]{4,3,2,1,0:T(8,128)S(1)}, f32[4,2,4,8,256]{4,3,2,1,0:T(8,128)S(1)}, u32[]{:S(2)}, u32[]{:S(2)}) collective-permute-start(f32[4,2,4,8,256]{4,3,2,1,0:T(8,128)S(1)} %get-tuple-element.16), channel_id=1, source_target_pairs={{0,6},{1,193},{2,0},{3,195},{4,2},{5,197},{6,4},{7,199},{8,14},{9,... | collective-permute-start | bytes 786440 | tf_op jit(solution)/shard_map/ppermute | solution.py:175

commit v4 on v1

v4 whole, which is shorter than its diff:
```python
import functools
import itertools
import math

import jax
import jax.numpy as jnp
from jax import lax
from jax.experimental import pallas as pl
from jax.experimental.pallas import tpu as pltpu
from jax.sharding import PartitionSpec as P

SKETCH = 2048
MIB = 1 << 20
OWN = 400
AXES = ("grp", "row")


def parity(bits):
    for shift in (8, 4, 2, 1):
        bits = bits ^ bits >> shift
    return bits & 1


def hadamard_sign(rows, cols):
    return (1 - 2 * parity(rows & cols)).astype(jnp.float32)


def two_parts(value):
    high = value.astype(jnp.bfloat16)
    low = (value - high.astype(jnp.float32)).astype(jnp.bfloat16)
    return high, low


def transform_kernel(other, place_ref, matrix_ref, signs_ref, out_ref):
    count, block, cols = matrix_ref.shape
    half = block // 2
    side = (place_ref[0] & 1) ^ other
    out_row = lax.broadcasted_iota(jnp.int32, (half, block), 0) + side * half
    in_row = lax.broadcasted_iota(jnp.int32, (half, block), 1)
    hadamard = hadamard_sign(out_row, in_row)
    for unit in range(count):
        high, low = two_parts(matrix_ref[unit])
        signed = (hadamard * signs_ref[pl.ds(unit, 1), :].astype(jnp.float32)).astype(jnp.bfloat16)
        out_ref[unit] = jnp.dot(
            jnp.concatenate([signed, signed], axis=1),
            jnp.concatenate([high, low], axis=0),
            preferred_element_type=jnp.float32,
        )


def transform(other, place, matrix, row_signs):
    count, block, cols = matrix.shape
    step = 8
    return pl.pallas_call(
        functools.partial(transform_kernel, other),
        grid_spec=pltpu.PrefetchScalarGridSpec(
            num_scalar_prefetch=1,
            grid=(count // step,),
            in_specs=[
                pl.BlockSpec((step, block, cols), lambda i, place: (i, 0, 0)),
                pl.BlockSpec((step, block), lambda i, place: (i, 0)),
            ],
            out_specs=pl.BlockSpec((step, block // 2, cols), lambda i, place: (i, 0, 0)),
        ),
        out_shape=jax.ShapeDtypeStruct((count, block // 2, cols), jnp.float32),
        compiler_params=pltpu.CompilerParams(vmem_limit_bytes=16 * MIB),
        cost_estimate=pl.CostEstimate(flops=10**9, bytes_accessed=6 * MIB, transcendentals=0),
        name="transform_other" if other else "transform_own",
    )(place, matrix, row_signs)


def add_products(place, left, half_ref, base_ref, out_ref):
    near, _, low_count, far, rows, cols = out_ref.shape
    wide = half_ref.shape[0] * rows
    core, first_y = place
    for step, low_z in itertools.product(range(near), range(low_count)):
        piece = (first_y + step) % near * low_count + low_z
        high, low = two_parts(half_ref[:, pl.ds(pl.multiple_of(piece * rows, rows), rows), :].reshape(wide, cols))
        result = jnp.dot(left, jnp.concatenate([high, low, high], axis=0), preferred_element_type=jnp.float32)
        result = result.reshape(near, far, rows, cols)
        for turn in range(near):
            to = (jnp.where(core == 0, turn, step), jnp.where(core == 0, step, turn), low_z)
            out_ref[to] = result[turn] if base_ref is None else base_ref[to] + result[turn]


def placing(place_ref, near, low_count, sources):
    me = place_ref[0] % sources
    core = me & 1
    first_x = jnp.where(core == 0, me >> 1, 0)
    first_y = jnp.where(core == 0, 0, place_ref[0] // sources // low_count)
    return me, core, first_x, first_y


def mix_own_kernel(scale, place_ref, meta_ref, own_ref, out_ref, left_ref):
    near, _, low_count, far, rows, _ = out_ref.shape
    sources, _, units = meta_ref.shape
    targets = near * far
    me, core, first_x, first_y = placing(place_ref, near, low_count, sources)
    index = lax.broadcasted_iota(jnp.int32, (targets, units), 0)
    target = index % far * near + (index // far + first_x) % near
    sums = [jnp.zeros((targets, units), jnp.float32) for _ in range(2)]
    for source in range(sources):
        flip = 1 - 2 * parity((me >> 1) & (source >> 1))
        dests = meta_ref[source, 0:1, :]
        signs = meta_ref[source, 1:2, :] * flip
        routed = jnp.where(dests == target, signs.astype(jnp.float32), 0.0)
        sums[source & 1] = sums[source & 1] + routed
    side = (1 - 2 * core).astype(jnp.float32)
    tall, wide = targets * rows, units * rows
    unit_row = lax.broadcasted_iota(jnp.int32, (units, wide), 0)
    unit_col = lax.broadcasted_iota(jnp.int32, (units, wide), 1)
    spread = (hadamard_sign(unit_row, unit_col // rows) * scale).astype(jnp.bfloat16)
    keep = lax.broadcasted_iota(jnp.int32, (tall, wide), 0) % rows == lax.broadcasted_iota(jnp.int32, (tall, wide), 1) % rows
    lefts = []
    for total in (sums[0] + side * sums[1], sums[0] - side * sums[1]):
        total = jnp.broadcast_to(total[:, None, :], (targets, rows, units)).reshape(tall, units)
        weights = jnp.dot(total.astype(jnp.bfloat16), spread, preferred_element_type=jnp.float32)
        high, low = two_parts(jnp.where(keep, weights, 0.0))
        lefts.append(jnp.concatenate([high, high, low], axis=1))
    left_ref[...] = lefts[1]
    add_products((core, first_y), lefts[0], own_ref, None, out_ref)


def mix_other_kernel(sources, place_ref, left_ref, other_ref, base_ref, out_ref):
    near, _, low_count = out_ref.shape[:3]
    _, core, _, first_y = placing(place_ref, near, low_count, sources)
    add_products((core, first_y), left_ref[...], other_ref, base_ref, out_ref)


def mix_own(scale, place, meta, own, near, low_count, far):
    units, half, cols = own.shape
    rows = half // (near * low_count)
    vmem = pl.BlockSpec(memory_space=pltpu.VMEM)
    return pl.pallas_call(
        functools.partial(mix_own_kernel, scale),
        in_specs=[pl.BlockSpec(memory_space=pltpu.SMEM), vmem, vmem],
        out_specs=[vmem, vmem],
        out_shape=[
            jax.ShapeDtypeStruct((near, near, low_count, far, rows, cols), jnp.float32),
            jax.ShapeDtypeStruct((near * far * rows, 3 * units * rows), jnp.bfloat16),
        ],
        compiler_params=pltpu.CompilerParams(vmem_limit_bytes=16 * MIB),
        cost_estimate=pl.CostEstimate(flops=OWN * 10**9, bytes_accessed=3 * MIB, transcendentals=0),
        name="mix_own",
    )(place, meta, own)


def mix_other(sources, place, left, other, base):
    vmem = pl.BlockSpec(memory_space=pltpu.VMEM)
    return pl.pallas_call(
        functools.partial(mix_other_kernel, sources),
        in_specs=[pl.BlockSpec(memory_space=pltpu.SMEM), vmem, vmem, vmem],
        out_specs=vmem,
        out_shape=jax.ShapeDtypeStruct(base.shape, jnp.float32),
        compiler_params=pltpu.CompilerParams(vmem_limit_bytes=16 * MIB),
        cost_estimate=pl.CostEstimate(flops=10**9, bytes_accessed=4 * MIB, transcendentals=0),
        name="mix_other",
    )(place, left, other, base)


Y, Z_LOW, Z_HIGH, X, CORE = 4, 2, 4, 4, 2


def flat_index(y, z_low, z_high, x, core):
    return (((y % Y * Z_LOW + z_low) * Z_HIGH + z_high) * X + x % X) * CORE + core


def places():
    return itertools.product(range(Y), range(Z_LOW), range(Z_HIGH), range(X), range(CORE))


def first_shift(value, step):
    pairs = []
    for y, z_low, z_high, x, core in places():
        to = (y, z_low, z_high, x + step, core) if core == 0 else (y + step, z_low, z_high, x, core)
        pairs.append((flat_index(y, z_low, z_high, x, core), flat_index(*to)))
    return lax.ppermute(value, AXES, pairs)


def second_groups():
    groups = []
    for core, fixed in itertools.product(range(CORE), range(X)):
        members = itertools.product(range(Y), range(Z_LOW), range(Z_HIGH))
        groups.append(
            [
                flat_index(free, z_low, z_high, fixed, core) if core == 0 else flat_index(fixed, z_low, z_high, free, core)
                for free, z_low, z_high in members
            ]
        )
    return groups


def body(matrix, row_signs, block_dest, block_signs):
    row_count, col_count = matrix.shape
    units = block_dest.shape[0]
    block = row_count // units
    groups = lax.axis_size("grp")
    devs = lax.axis_size("row")
    total_rows = row_count * devs * groups
    scale = math.sqrt(SKETCH / total_rows) / math.sqrt(row_count * devs)
    place = lax.axis_index(AXES).astype(jnp.int32).reshape(1)

    mine = jnp.stack([block_dest, block_signs])
    meta = lax.all_to_all(jnp.broadcast_to(mine[None], (devs, 2, units)), "row", 0, 0)
    matrix = matrix.reshape(units, block, col_count)
    row_signs = row_signs.reshape(units, block)
    own, send = (transform(other, place, matrix, row_signs) for other in range(2))
    other = lax.ppermute(send, "row", [(i, i ^ 1) for i in range(devs)])
    base, left = mix_own(scale, place, meta, own, X, Z_LOW, Z_HIGH)
    parts = mix_other(devs, place, left, other, base)

    got = {step: first_shift(parts[step], step) for step in (2, 1, 3)}
    part = (parts[0] + got[2]) + (got[1] + got[3])
    pieces = part.reshape(-1, 8, col_count)
    pieces = lax.all_to_all(pieces, AXES, 0, 0, axis_index_groups=second_groups())
    share = jnp.sum(pieces, axis=0)
    full = lax.all_to_all(jnp.broadcast_to(share[None], (groups, 8, col_count)), "grp", 0, 0)
    return full.reshape(groups * 8, col_count)


def solution(mesh):
    return jax.shard_map(
        body,
        mesh=mesh,
        in_specs=(P(AXES, None), P(AXES), P(AXES), P(AXES)),
        out_specs=P("row", None),
        check_vma=False,
    )
```

time: 75.1 us -> 68 us (0.905)
  blocking collectives: 68.1 us -> 30.8 us
  starting transfers between devices: 0.09 us -> 15.9 us
  waiting for transfers between devices: 0.01 us -> 8.87 us
  Pallas kernels: 2.81 us -> 6.99 us
    all_to_all x2 -> x1, blocking collectives: 59.2 us -> 20.3 us  [body(): lax.all_to_all(pieces, AXES, 0, 0, axis_index_groups=second_groups())]
    all_to_all x0 -> x1, starting transfers between devices: none -> 11.6 us  [body(): lax.all_to_all(jnp.broadcast_to(mine[None], (devs, 2, units)), 'row', 0, 0)]
    ppermute x0 -> x3, waiting for transfers between devices: none -> 6.64 us  [first_shift(): return lax.ppermute(value, AXES, pairs)]
    ppermute x0 -> x3, starting transfers between devices: none -> 4.18 us  [first_shift(): return lax.ppermute(value, AXES, pairs)]
    pallas_call x2 -> x4, Pallas kernels: 2.81 us -> 6.99 us  [the longest x2 3.87 us: transform(): pl.pallas_call(functools.partial(transform_kernel, other), grid_spec=pltp...]
    all_to_all x0 -> x1, waiting for transfers between devices: none -> 1.68 us  [body(): lax.all_to_all(jnp.broadcast_to(mine[None], (devs, 2, units)), 'row', 0, 0)]
    all_to_all x1, blocking collectives: 8.9 us -> 10.5 us  [body(): lax.all_to_all(jnp.broadcast_to(share[None], (groups, 8, col_count)), 'gr...]
    unnamed x9 -> x5, local copies, waits for them, and re-layouts: 3.54 us -> 3.53 us
  transfers between devices with their start and end apart: 1 -> 5, of which waited for: 0 -> 4; matrix products, arithmetic and copies ran while one was open for 0% -> 0% of each run, Pallas kernels for 0% -> 7%
where the time goes in v4:
time: 68 us; the launch traced here: 67.7 us
  blocking collectives  30.8 us (45%)
  starting transfers between devices  15.9 us (23%)
  waiting for transfers between devices  8.87 us (13%)
  Pallas kernels  6.99 us (10%)
  local copies, waits for them, and re-layouts  4.22 us (6%)
  other arithmetic  0.79 us (1%)
    all_to_all x1, blocking collectives, body(): lax.all_to_all(pieces, AXES, 0, 0, axis_index_groups=second_groups())  20.3 us
    all_to_all x1, starting transfers between devices, body(): lax.all_to_all(jnp.broadcast_to(mine[None], (devs, 2, units)), 'row', 0, 0)  11.6 us
    all_to_all x1, blocking collectives, body(): lax.all_to_all(jnp.broadcast_to(share[None], (groups, 8, col_count)), 'gr...  10.5 us
    ppermute x3, waiting for transfers between devices, first_shift(): return lax.ppermute(value, AXES, pairs)  6.64 us
    ppermute x3, starting transfers between devices, first_shift(): return lax.ppermute(value, AXES, pairs)  4.18 us
    pallas_call x2, Pallas kernels, transform(): pl.pallas_call(functools.partial(transform_kernel, other), grid_spec=pltp...  3.87 us
    unnamed x5, local copies, waits for them, and re-layouts  3.53 us
    pallas_call x1, Pallas kernels, mix_other(): pl.pallas_call(functools.partial(mix_other_kernel, sources), in_specs=[pl...  2.33 us
  transfers between devices with their start and end apart: 5, of which 4 were waited for; matrix products, arithmetic and copies ran while one was open for 0% of the time, Pallas kernels for 7%

profile of v4, /device:TPU:2, one launch (start us, length us, event | category | flops | bytes accessed | tf_op | source)
XLA Modules:
  0.0 67.7 jit_solution(702763434262521892)
XLA Ops:
  0.0 0.7 %pad_add_fusion = s32[2,32]{1,0:T(2,128)S(1)} fusion(s32[1,32]{1,0:T(1,128)} %bitcast.25, s32[1,32]{1,0:T(1,128)} %bitcast.26), kind=kLoop, calls=%fused_computation.6 | loop fusion | flops 64 | bytes 512 | tf_op jit(solution)/shard_map/stack | solution.py:203
  0.7 0.6 broadcast_in_dim.4
  1.3 11.6 %all-to-all-start = ((s32[32,2,32]{2,1,0:T(2,128)}), s32[32,2,32]{2,1,0:T(2,128)S(1)}, u32[]{:S(2)}, u32[]{:S(2)}) async-start(s32[32,2,32]{2,1,0:T(2,128)} %broadcast_in_dim.4), calls=%async_computation | async-start | bytes 65536 | tf_op jit(solution)/shard_map/all_to_all | solution.py:204
  12.9 0.0 copy-start
  12.9 2.2 %copy-done = f32[4096,256]{1,0:T(8,128)S(1)} copy-done((f32[4096,256]{1,0:T(8,128)S(1)}, f32[4096,256]{1,0:T(8,128)}, u32[]{:S(2)}) %copy-start) | copy-done | bytes 4194328
  15.1 0.0 copy-start.1
  15.1 0.7 %copy-done.1 = s32[4096]{0:T(1024)S(1)} copy-done((s32[4096]{0:T(1024)S(1)}, s32[4096]{0:T(1024)}, u32[]{:S(2)}) %copy-start.1) | copy-done | bytes 16408
  15.8 2.6 %transform_other.1 = f32[32,64,256]{2,1,0:T(8,128)} custom-call(s32[1]{0:T(128)} %bitcast.place_ref, f32[32,128,256]{2,1,0:T(8,128)S(1)} %bitcast.19, s32[32,128]{1,0:T(8,128)S(1)} %bitcast.21), custom_call_target="tpu_custom_call" | custom-call | flops 1000000000 | bytes 6291456 | tf_op jit(solution)/shard_map/transform_other/pallas_call | solution.py:54
  18.4 0.1 collective-permute-start
  18.5 1.3 %transform_own.1.own_ref = f32[32,64,256]{2,1,0:T(8,128)S(1)} custom-call(s32[1]{0:T(128)} %bitcast.place_ref, f32[32,128,256]{2,1,0:T(8,128)S(1)} %bitcast.20, s32[32,128]{1,0:T(8,128)S(1)} %bitcast.22), custom_call_target="tpu_custom_call" | custom-call | flops 1000000000 | bytes 6291456 | tf_op jit(solution)/shard_map/transform_own/pallas_call | solution.py:54
  19.9 1.7 %all-to-all-done.meta_ref = s32[32,2,32]{2,1,0:T(2,128)S(1)} async-done(((s32[32,2,32]{2,1,0:T(2,128)}), s32[32,2,32]{2,1,0:T(2,128)S(1)}, u32[]{:S(2)}, u32[]{:S(2)}) %all-to-all-start) | async-done | bytes 8224 | tf_op jit(solution)/shard_map/all_to_all | solution.py:204
  21.6 0.8 %mix_own.1 = (f32[4,4,2,4,8,256]{5,4,3,2,1,0:T(8,128)S(1)}, bf16[128,768]{1,0:T(8,128)(2,1)S(1)}) custom-call(s32[1]{0:T(128)} %bitcast.place_ref, s32[32,2,32]{2,1,0:T(2,128)S(1)} %all-to-all-done.meta_ref, f32[32,64,256]{2,1,0:T(8,128)S(1)} %transform_own.1.own_ref), custom_call_target="tpu_custom_call" | custom-call | flops 399999991808 | bytes 3145728 | tf_op jit(solution)/shard_map/mix_own/pallas_call | solution.py:134
  22.4 0.5 collective-permute-done.other_ref
  22.9 2.3 %mix_other.1 = f32[4,4,2,4,8,256]{5,4,3,2,1,0:T(8,128)S(1)} custom-call(s32[1]{0:T(128)} %bitcast.place_ref, bf16[128,768]{1,0:T(8,128)(2,1)S(1)} %get-tuple-element.7.left_ref, f32[32,64,256]{2,1,0:T(8,128)} %collective-permute-done.other_ref, f32[4,4,2,4,8,256]{5,4,3,2,1,0:T(8,128)S(1)} %get-tuple-element.8.base_ref), custom_call_target="tpu_custom_call" | custom-call | flops 1000000000 | bytes 4194304 | tf_op jit(solution)/shard_map/mix_other/pallas_call | solution.py:150
  25.2 0.1 slice_bitcast_fusion
  25.3 2.2 %collective-permute-start.1 = (f32[4,2,4,8,256]{4,3,2,1,0:T(8,128)S(1)}, f32[4,2,4,8,256]{4,3,2,1,0:T(8,128)S(1)}, u32[]{:S(2)}, u32[]{:S(2)}) collective-permute-start(f32[4,2,4,8,256]{4,3,2,1,0:T(8,128)S(1)} %get-tuple-element.11), channel_id=1, source_target_pairs={{0,4},{1,129},{2,6},{3,131},{4,0},{5,133},{6,2},{7,135},{8,12},{9,... | collective-permute-start | bytes 786440 | tf_op jit(solution)/shard_map/ppermute | solution.py:177
  27.5 0.3 collective-permute-start.2
  27.8 1.7 %collective-permute-start.3 = (f32[4,2,4,8,256]{4,3,2,1,0:T(8,128)S(1)}, f32[4,2,4,8,256]{4,3,2,1,0:T(8,128)S(1)}, u32[]{:S(2)}, u32[]{:S(2)}) collective-permute-start(f32[4,2,4,8,256]{4,3,2,1,0:T(8,128)S(1)} %get-tuple-element.9), channel_id=1, source_target_pairs={{0,6},{1,193},{2,0},{3,195},{4,2},{5,197},{6,4},{7,199},{8,14},{9,... | collective-permute-start | bytes 786440 | tf_op jit(solution)/shard_map/ppermute | solution.py:177
  29.5 3.9 %collective-permute-done.1 = f32[4,2,4,8,256]{4,3,2,1,0:T(8,128)S(1)} collective-permute-done((f32[4,2,4,8,256]{4,3,2,1,0:T(8,128)S(1)}, f32[4,2,4,8,256]{4,3,2,1,0:T(8,128)S(1)}, u32[]{:S(2)}, u32[]{:S(2)}) %collective-permute-start.1) | collective-permute-done | bytes 262176 | tf_op jit(solution)/shard_map/ppermute | solution.py:177
  33.4 2.8 %collective-permute-done.2 = f32[4,2,4,8,256]{4,3,2,1,0:T(8,128)S(1)} collective-permute-done((f32[4,2,4,8,256]{4,3,2,1,0:T(8,128)S(1)}, f32[4,2,4,8,256]{4,3,2,1,0:T(8,128)S(1)}, u32[]{:S(2)}, u32[]{:S(2)}) %collective-permute-start.2) | collective-permute-done | bytes 262176 | tf_op jit(solution)/shard_map/ppermute | solution.py:177
  36.1 0.0 collective-permute-done.3
  36.1 0.1 fusion.1
  36.2 20.3 %all_to_all.15 = f32[32,8,256]{2,1,0:T(8,128)S(1)} all-to-all(f32[32,8,256]{2,1,0:T(8,128)S(1)} %bitcast.23), channel_id=1, replica_groups={{0,8,16,24,32,40,48,56,64,72,80,88,96,104,112,120,128,136,144,152,160,1..., dimensions={0} | all-to-all | bytes 524288 | tf_op jit(solution)/shard_map/all_to_all | solution.py:215
  56.5 10.5 %all_to_all.16 = f32[8,8,256]{2,1,0:T(8,128)S(1)} all-to-all(f32[8,8,256]{2,1,0:T(8,128)S(1)} %broadcast_in_dim.5), channel_id=1, replica_groups=mesh['grp'=8,'row'=32] {'grp'}, dimensions={0} | all-to-all | bytes 131072 | tf_op jit(solution)/shard_map/all_to_all | solution.py:217
  67.1 0.6 copy.6
  (2 shorter events, 0.0 us)
Async XLA Ops:
  1.3 20.2 %all-to-all-start = ((s32[32,2,32]{2,1,0:T(2,128)}), s32[32,2,32]{2,1,0:T(2,128)S(1)}, u32[]{:S(2)}, u32[]{:S(2)}) async-start(s32[32,2,32]{2,1,0:T(2,128)} %broadcast_in_dim.4), calls=%async_computation | async-start | bytes 65536 | tf_op jit(solution)/shard_map/all_to_all | solution.py:204
  12.9 2.2 %copy-start = (f32[4096,256]{1,0:T(8,128)S(1)}, f32[4096,256]{1,0:T(8,128)}, u32[]{:S(2)}) copy-start(f32[4096,256]{1,0:T(8,128)} %param.4) | copy-start | bytes 12582916
  15.1 0.7 %copy-start.1 = (s32[4096]{0:T(1024)S(1)}, s32[4096]{0:T(1024)}, u32[]{:S(2)}) copy-start(s32[4096]{0:T(1024)} %param.5) | copy-start | bytes 49156
  18.4 4.5 %collective-permute-start = (f32[32,64,256]{2,1,0:T(8,128)}, f32[32,64,256]{2,1,0:T(8,128)}, u32[]{:S(2)}, u32[]{:S(2)}) collective-permute-start(f32[32,64,256]{2,1,0:T(8,128)} %transform_other.1), channel_id=1, source_target_pairs={{0,1},{1,0},{2,3},{3,2},{4,5},{5,4},{6,7},{7,6},{8,9},{9,8},{10,11... | collective-permute-start | bytes 6291464 | tf_op jit(solution)/shard_map/ppermute | solution.py:208
  25.3 8.1 %collective-permute-start.1 = (f32[4,2,4,8,256]{4,3,2,1,0:T(8,128)S(1)}, f32[4,2,4,8,256]{4,3,2,1,0:T(8,128)S(1)}, u32[]{:S(2)}, u32[]{:S(2)}) collective-permute-start(f32[4,2,4,8,256]{4,3,2,1,0:T(8,128)S(1)} %get-tuple-element.11), channel_id=1, source_target_pairs={{0,4},{1,129},{2,6},{3,131},{4,0},{5,133},{6,2},{7,135},{8,12},{9,... | collective-permute-start | bytes 786440 | tf_op jit(solution)/shard_map/ppermute | solution.py:177
  27.5 8.7 %collective-permute-start.2 = (f32[4,2,4,8,256]{4,3,2,1,0:T(8,128)S(1)}, f32[4,2,4,8,256]{4,3,2,1,0:T(8,128)S(1)}, u32[]{:S(2)}, u32[]{:S(2)}) collective-permute-start(f32[4,2,4,8,256]{4,3,2,1,0:T(8,128)S(1)} %get-tuple-element.10), channel_id=1, source_target_pairs={{0,2},{1,65},{2,4},{3,67},{4,6},{5,69},{6,0},{7,71},{8,10},{9,73},... | collective-permute-start | bytes 786440 | tf_op jit(solution)/shard_map/ppermute | solution.py:177
  27.8 8.3 %collective-permute-start.3 = (f32[4,2,4,8,256]{4,3,2,1,0:T(8,128)S(1)}, f32[4,2,4,8,256]{4,3,2,1,0:T(8,128)S(1)}, u32[]{:S(2)}, u32[]{:S(2)}) collective-permute-start(f32[4,2,4,8,256]{4,3,2,1,0:T(8,128)S(1)} %get-tuple-element.9), channel_id=1, source_target_pairs={{0,6},{1,193},{2,0},{3,195},{4,2},{5,197},{6,4},{7,199},{8,14},{9,... | collective-permute-start | bytes 786440 | tf_op jit(solution)/shard_map/ppermute | solution.py:177

commit v5 on v1

v5 whole, which is shorter than its diff:
```python
import functools
import itertools
import math

import jax
import jax.numpy as jnp
from jax import lax
from jax.experimental import pallas as pl
from jax.experimental.pallas import tpu as pltpu
from jax.sharding import PartitionSpec as P

SKETCH = 2048
MIB = 1 << 20
AXES = ("grp", "row")


def parity(bits):
    for shift in (8, 4, 2, 1):
        bits = bits ^ bits >> shift
    return bits & 1


def hadamard_sign(rows, cols):
    return (1 - 2 * parity(rows & cols)).astype(jnp.float32)


def two_parts(value):
    high = value.astype(jnp.bfloat16)
    low = (value - high.astype(jnp.float32)).astype(jnp.bfloat16)
    return high, low


def transform_kernel(place_ref, matrix_ref, signs_ref, own_ref, send_ref):
    count, block, cols = matrix_ref.shape
    half = block // 2
    core = place_ref[0] & 1
    out_row = lax.broadcasted_iota(jnp.int32, (block, block), 0)
    in_row = lax.broadcasted_iota(jnp.int32, (block, block), 1)
    hadamard = hadamard_sign(out_row ^ core * half, in_row)
    for unit in range(count):
        high, low = two_parts(matrix_ref[unit])
        signed = (hadamard * signs_ref[pl.ds(unit, 1), :].astype(jnp.float32)).astype(jnp.bfloat16)
        result = jnp.dot(
            jnp.concatenate([signed, signed], axis=1),
            jnp.concatenate([high, low], axis=0),
            preferred_element_type=jnp.float32,
        )
        own_ref[unit] = result[:half]
        send_ref[unit] = result[half:]


def transform(place, matrix, row_signs):
    count, block, cols = matrix.shape
    step = 8
    half = jax.ShapeDtypeStruct((count, block // 2, cols), jnp.float32)
    return pl.pallas_call(
        transform_kernel,
        grid_spec=pltpu.PrefetchScalarGridSpec(
            num_scalar_prefetch=1,
            grid=(count // step,),
            in_specs=[
                pl.BlockSpec((step, block, cols), lambda i, place: (i, 0, 0)),
                pl.BlockSpec((step, block), lambda i, place: (i, 0)),
            ],
            out_specs=[
                pl.BlockSpec((step, block // 2, cols), lambda i, place: (i, 0, 0)),
                pl.BlockSpec((step, block // 2, cols), lambda i, place: (i, 0, 0)),
            ],
        ),
        out_shape=[half, half],
        compiler_params=pltpu.CompilerParams(vmem_limit_bytes=16 * MIB),
        cost_estimate=pl.CostEstimate(flops=2 * 2 * 128 * 128 * 256 * 32, bytes_accessed=8 * MIB, transcendentals=0),
        name="transform",
    )(place, matrix, row_signs)


def mix_kernel(scale, place_ref, meta_ref, own_ref, other_ref, out_ref):
    near, _, low_count, far, rows, cols = out_ref.shape
    sources, _, units = meta_ref.shape
    targets = near * far
    me = place_ref[0] % sources
    core = me & 1
    first_x = jnp.where(core == 0, me >> 1, 0)
    first_y = jnp.where(core == 0, 0, place_ref[0] // sources // low_count)
    index = lax.broadcasted_iota(jnp.int32, (targets, units), 0)
    target = index % far * near + (index // far + first_x) % near
    sums = [jnp.zeros((targets, units), jnp.float32) for _ in range(2)]
    for source in range(sources):
        flip = 1 - 2 * parity((me >> 1) & (source >> 1))
        dests = meta_ref[source, 0:1, :]
        signs = meta_ref[source, 1:2, :] * flip
        routed = jnp.where(dests == target, signs.astype(jnp.float32), 0.0)
        sums[source & 1] = sums[source & 1] + routed
    side = (1 - 2 * core).astype(jnp.float32)
    tall, wide = targets * rows, units * rows
    unit_row = lax.broadcasted_iota(jnp.int32, (units, wide), 0)
    unit_col = lax.broadcasted_iota(jnp.int32, (units, wide), 1)
    spread = (hadamard_sign(unit_row, unit_col // rows) * scale).astype(jnp.bfloat16)
    keep = lax.broadcasted_iota(jnp.int32, (tall, wide), 0) % rows == lax.broadcasted_iota(jnp.int32, (tall, wide), 1) % rows
    highs, lows = [], []
    for total in (sums[0] + side * sums[1], sums[0] - side * sums[1]):
        total = jnp.broadcast_to(total[:, None, :], (targets, rows, units)).reshape(tall, units)
        weights = jnp.dot(total.astype(jnp.bfloat16), spread, preferred_element_type=jnp.float32)
        high, low = two_parts(jnp.where(keep, weights, 0.0))
        highs.append(high)
        lows.append(low)
    left = jnp.concatenate(highs + highs + lows, axis=1)
    for step, low_z in itertools.product(range(near), range(low_count)):
        piece = (first_y + step) % near * low_count + low_z
        span = pl.ds(pl.multiple_of(piece * rows, rows), rows)
        parts = [two_parts(ref[:, span, :].reshape(wide, cols)) for ref in (own_ref, other_ref)]
        high = [part[0] for part in parts]
        low = [part[1] for part in parts]
        result = jnp.dot(left, jnp.concatenate(high + low + high, axis=0), preferred_element_type=jnp.float32)
        result = result.reshape(near, far, rows, cols)
        for turn in range(near):
            out_ref[jnp.where(core == 0, turn, step), jnp.where(core == 0, step, turn), low_z] = result[turn]


def mix(scale, place, meta, own, other, near, low_count, far):
    units, half, cols = own.shape
    rows = half // (near * low_count)
    vmem = pl.BlockSpec(memory_space=pltpu.VMEM)
    return pl.pallas_call(
        functools.partial(mix_kernel, scale),
        in_specs=[pl.BlockSpec(memory_space=pltpu.SMEM), vmem, vmem, vmem],
        out_specs=vmem,
        out_shape=jax.ShapeDtypeStruct((near, near, low_count, far, rows, cols), jnp.float32),
        compiler_params=pltpu.CompilerParams(vmem_limit_bytes=24 * MIB),
        cost_estimate=pl.CostEstimate(flops=2 * 3 * 128 * 512 * 256 * 8, bytes_accessed=5 * MIB, transcendentals=0),
        name="mix",
    )(place, meta, own, other)


Y, Z_LOW, Z_HIGH, X, CORE = 4, 2, 4, 4, 2


def flat_index(y, z_low, z_high, x, core):
    return (((y % Y * Z_LOW + z_low) * Z_HIGH + z_high) * X + x % X) * CORE + core


def places():
    return itertools.product(range(Y), range(Z_LOW), range(Z_HIGH), range(X), range(CORE))


def first_shift(value, step):
    pairs = []
    for y, z_low, z_high, x, core in places():
        to = (y, z_low, z_high, x + step, core) if core == 0 else (y + step, z_low, z_high, x, core)
        pairs.append((flat_index(y, z_low, z_high, x, core), flat_index(*to)))
    return lax.ppermute(value, AXES, pairs)


def second_groups():
    groups = []
    for core, fixed in itertools.product(range(CORE), range(X)):
        members = itertools.product(range(Y), range(Z_LOW), range(Z_HIGH))
        groups.append(
            [
                flat_index(free, z_low, z_high, fixed, core) if core == 0 else flat_index(fixed, z_low, z_high, free, core)
                for free, z_low, z_high in members
            ]
        )
    return groups


def body(matrix, row_signs, block_dest, block_signs):
    row_count, col_count = matrix.shape
    units = block_dest.shape[0]
    block = row_count // units
    groups = lax.axis_size("grp")
    devs = lax.axis_size("row")
    total_rows = row_count * devs * groups
    scale = math.sqrt(SKETCH / total_rows) / math.sqrt(row_count * devs)
    place = lax.axis_index(AXES).astype(jnp.int32).reshape(1)

    mine = jnp.stack([block_dest, block_signs])
    meta = lax.all_to_all(jnp.broadcast_to(mine[None], (devs, 2, units)), "row", 0, 0)
    matrix = matrix.reshape(units, block, col_count)
    row_signs = row_signs.reshape(units, block)
    own, send = transform(place, matrix, row_signs)
    other = lax.ppermute(send, "row", [(i, i ^ 1) for i in range(devs)])
    parts = mix(scale, place, meta, own, other, X, Z_LOW, Z_HIGH)

    got = {step: first_shift(parts[step], step) for step in (2, 1, 3)}
    part = (parts[0] + got[2]) + (got[1] + got[3])
    pieces = part.reshape(-1, 8, col_count)
    pieces = lax.all_to_all(pieces, AXES, 0, 0, axis_index_groups=second_groups())
    share = jnp.sum(pieces, axis=0)
    full = lax.all_to_all(jnp.broadcast_to(share[None], (groups, 8, col_count)), "grp", 0, 0)
    return full.reshape(groups * 8, col_count)


def solution(mesh):
    return jax.shard_map(
        body,
        mesh=mesh,
        in_specs=(P(AXES, None), P(AXES), P(AXES), P(AXES)),
        out_specs=P("row", None),
        check_vma=False,
    )
```

time: 75.1 us -> 64 us (0.85)
  blocking collectives: 68.1 us -> 46.2 us
  waiting for transfers between devices: 0.01 us -> 7.18 us
  starting transfers between devices: 0.09 us -> 3.69 us
    all_to_all x1, blocking collectives: 39.1 us -> 15.8 us  [body(): lax.all_to_all(pieces, AXES, 0, 0, axis_index_groups=second_groups())]
    ppermute x0 -> x3, waiting for transfers between devices: none -> 7.17 us  [first_shift(): return lax.ppermute(value, AXES, pairs)]
    ppermute x0 -> x3, starting transfers between devices: none -> 3.6 us  [first_shift(): return lax.ppermute(value, AXES, pairs)]
    all_to_all x1, blocking collectives: 8.9 us -> 10.3 us  [body(): lax.all_to_all(jnp.broadcast_to(share[None], (groups, 8, col_count)), 'gr...]
  transfers between devices with their start and end apart: 1 -> 4, of which waited for: 0 -> 3; matrix products, arithmetic and copies ran while one was open for 0% -> 0% of each run, Pallas kernels for 0% -> 0%
where the time goes in v5:
time: 64 us; the launch traced here: 63.7 us
  blocking collectives  46.2 us (72%)
  waiting for transfers between devices  7.18 us (11%)
  starting transfers between devices  3.69 us (6%)
  local copies, waits for them, and re-layouts  3.62 us (6%)
  Pallas kernels  2.89 us (5%)
    all_to_all x1, blocking collectives, body(): lax.all_to_all(jnp.broadcast_to(mine[None], (devs, 2, units)), 'row', 0, 0)  20.1 us
    all_to_all x1, blocking collectives, body(): lax.all_to_all(pieces, AXES, 0, 0, axis_index_groups=second_groups())  15.8 us
    all_to_all x1, blocking collectives, body(): lax.all_to_all(jnp.broadcast_to(share[None], (groups, 8, col_count)), 'gr...  10.3 us
    ppermute x3, waiting for transfers between devices, first_shift(): return lax.ppermute(value, AXES, pairs)  7.17 us
    ppermute x3, starting transfers between devices, first_shift(): return lax.ppermute(value, AXES, pairs)  3.6 us
    unnamed x9, local copies, waits for them, and re-layouts  3.54 us
    pallas_call x1, Pallas kernels, mix(): pl.pallas_call(functools.partial(mix_kernel, scale), in_specs=[pl.BlockSp...  1.46 us
    pallas_call x1, Pallas kernels, transform(): pl.pallas_call(transform_kernel, grid_spec=pltpu.PrefetchScalarGridSpec(n...  1.43 us
  transfers between devices with their start and end apart: 4, of which 3 were waited for; matrix products, arithmetic and copies ran while one was open for 0% of the time, Pallas kernels for 0%

profile of v5, /device:TPU:2, one launch (start us, length us, event | category | flops | bytes accessed | tf_op | source)
XLA Modules:
  0.0 63.7 jit_solution(10384140211454828416)
XLA Ops:
  0.0 0.0 copy-start
  0.0 2.2 %copy-done = f32[4096,256]{1,0:T(8,128)S(1)} copy-done((f32[4096,256]{1,0:T(8,128)S(1)}, f32[4096,256]{1,0:T(8,128)}, u32[]{:S(2)}) %copy-start) | copy-done | bytes 4194328
  2.2 0.0 copy-start.1
  2.2 0.7 %copy-done.1 = s32[4096]{0:T(1024)S(1)} copy-done((s32[4096]{0:T(1024)S(1)}, s32[4096]{0:T(1024)}, u32[]{:S(2)}) %copy-start.1) | copy-done | bytes 16408
  2.9 0.0 copy-start.2
  2.9 0.0 copy-start.3
  2.9 1.4 %transform.1 = (f32[32,64,256]{2,1,0:T(8,128)S(1)}, f32[32,64,256]{2,1,0:T(8,128)S(1)}) custom-call(s32[1]{0:T(128)} %bitcast.place_ref, f32[32,128,256]{2,1,0:T(8,128)S(1)} %bitcast.19, s32[32,128]{1,0:T(8,128)S(1)} %bitcast.20), custom_call_target="tpu_custom_call" | custom-call | flops 536870912 | bytes 8388608 | tf_op jit(solution)/shard_map/transform/pallas_call | solution.py:56
  4.3 0.1 collective-permute-start
  4.5 0.0 copy-done.2
  4.5 0.0 copy-done.3
  4.5 20.1 %all_to_all.15.meta_ref = s32[32,2,32]{2,1,0:T(2,128)S(1)} all-to-all(s32[32,2,32]{2,1,0:T(2,128)S(1)} %broadcast_in_dim.4), channel_id=1, replica_groups=mesh['grp'=8,'row'=32] {'row'}, dimensions={0} | all-to-all | bytes 16384 | tf_op jit(solution)/shard_map/all_to_all | solution.py:178
  24.6 0.0 collective-permute-done.other_ref
  24.6 1.5 %mix.1 = f32[4,4,2,4,8,256]{5,4,3,2,1,0:T(8,128)S(1)} custom-call(s32[1]{0:T(128)} %bitcast.place_ref, s32[32,2,32]{2,1,0:T(2,128)S(1)} %all_to_all.15.meta_ref, f32[32,64,256]{2,1,0:T(8,128)S(1)} %get-tuple-element.7.own_ref, f32[32,64,256]{2,1,0:T(8,128)S(1)} %collective-permute-done.other_ref), custom_call_target="tpu_custom_call" | custom-call | flops 805306368 | bytes 5242880 | tf_op jit(solution)/shard_map/mix/pallas_call | solution.py:124
  26.1 0.1 slice_bitcast_fusion
  26.2 1.6 %collective-permute-start.1 = (f32[4,2,4,8,256]{4,3,2,1,0:T(8,128)S(1)}, f32[4,2,4,8,256]{4,3,2,1,0:T(8,128)S(1)}, u32[]{:S(2)}, u32[]{:S(2)}) collective-permute-start(f32[4,2,4,8,256]{4,3,2,1,0:T(8,128)S(1)} %get-tuple-element.11), channel_id=1, source_target_pairs={{0,4},{1,129},{2,6},{3,131},{4,0},{5,133},{6,2},{7,135},{8,12},{9,... | collective-permute-start | bytes 786440 | tf_op jit(solution)/shard_map/ppermute | solution.py:151
  27.7 1.4 %collective-permute-start.2 = (f32[4,2,4,8,256]{4,3,2,1,0:T(8,128)S(1)}, f32[4,2,4,8,256]{4,3,2,1,0:T(8,128)S(1)}, u32[]{:S(2)}, u32[]{:S(2)}) collective-permute-start(f32[4,2,4,8,256]{4,3,2,1,0:T(8,128)S(1)} %get-tuple-element.10), channel_id=1, source_target_pairs={{0,2},{1,65},{2,4},{3,67},{4,6},{5,69},{6,0},{7,71},{8,10},{9,73},... | collective-permute-start | bytes 786440 | tf_op jit(solution)/shard_map/ppermute | solution.py:151
  29.2 0.6 collective-permute-start.3
  29.8 4.5 %collective-permute-done.1 = f32[4,2,4,8,256]{4,3,2,1,0:T(8,128)S(1)} collective-permute-done((f32[4,2,4,8,256]{4,3,2,1,0:T(8,128)S(1)}, f32[4,2,4,8,256]{4,3,2,1,0:T(8,128)S(1)}, u32[]{:S(2)}, u32[]{:S(2)}) %collective-permute-start.1) | collective-permute-done | bytes 262176 | tf_op jit(solution)/shard_map/ppermute | solution.py:151
  34.2 1.8 %collective-permute-done.2 = f32[4,2,4,8,256]{4,3,2,1,0:T(8,128)S(1)} collective-permute-done((f32[4,2,4,8,256]{4,3,2,1,0:T(8,128)S(1)}, f32[4,2,4,8,256]{4,3,2,1,0:T(8,128)S(1)}, u32[]{:S(2)}, u32[]{:S(2)}) %collective-permute-start.2) | collective-permute-done | bytes 262176 | tf_op jit(solution)/shard_map/ppermute | solution.py:151
  36.0 0.9 %collective-permute-done.3 = f32[4,2,4,8,256]{4,3,2,1,0:T(8,128)S(1)} collective-permute-done((f32[4,2,4,8,256]{4,3,2,1,0:T(8,128)S(1)}, f32[4,2,4,8,256]{4,3,2,1,0:T(8,128)S(1)}, u32[]{:S(2)}, u32[]{:S(2)}) %collective-permute-start.3) | collective-permute-done | bytes 262176 | tf_op jit(solution)/shard_map/ppermute | solution.py:151
  36.9 0.1 fusion.1
  37.0 15.8 %all_to_all.16 = f32[32,8,256]{2,1,0:T(8,128)S(1)} all-to-all(f32[32,8,256]{2,1,0:T(8,128)S(1)} %bitcast.21), channel_id=1, replica_groups={{0,8,16,24,32,40,48,56,64,72,80,88,96,104,112,120,128,136,144,152,160,1..., dimensions={0} | all-to-all | bytes 524288 | tf_op jit(solution)/shard_map/all_to_all | solution.py:188
  52.8 10.3 %all_to_all.17 = f32[8,8,256]{2,1,0:T(8,128)S(1)} all-to-all(f32[8,8,256]{2,1,0:T(8,128)S(1)} %broadcast_in_dim.5), channel_id=1, replica_groups=mesh['grp'=8,'row'=32] {'grp'}, dimensions={0} | all-to-all | bytes 131072 | tf_op jit(solution)/shard_map/all_to_all | solution.py:190
  63.1 0.6 copy.6
  (4 shorter events, 0.1 us)
Async XLA Ops:
  0.0 2.2 %copy-start = (f32[4096,256]{1,0:T(8,128)S(1)}, f32[4096,256]{1,0:T(8,128)}, u32[]{:S(2)}) copy-start(f32[4096,256]{1,0:T(8,128)} %param.4) | copy-start | bytes 12582916
  2.2 0.7 %copy-start.1 = (s32[4096]{0:T(1024)S(1)}, s32[4096]{0:T(1024)}, u32[]{:S(2)}) copy-start(s32[4096]{0:T(1024)} %param.5) | copy-start | bytes 49156
  2.9 1.5 %copy-start.2 = (s32[32]{0:T(128)S(1)}, s32[32]{0:T(128)}, u32[]{:S(2)}) copy-start(s32[32]{0:T(128)} %param.7) | copy-start | bytes 388
  2.9 1.6 %copy-start.3 = (s32[32]{0:T(128)S(1)}, s32[32]{0:T(128)}, u32[]{:S(2)}) copy-start(s32[32]{0:T(128)} %param.6) | copy-start | bytes 388
  4.3 20.3 %collective-permute-start = (f32[32,64,256]{2,1,0:T(8,128)S(1)}, f32[32,64,256]{2,1,0:T(8,128)S(1)}, u32[]{:S(2)}, u32[]{:S(2)}) collective-permute-start(f32[32,64,256]{2,1,0:T(8,128)S(1)} %get-tuple-element.8), channel_id=1, source_target_pairs={{0,1},{1,0},{2,3},{3,2},{4,5},{5,4},{6,7},{7,6},{8,9},{9,8},{10,11... | collective-permute-start | bytes 6291464 | tf_op jit(solution)/shard_map/ppermute | solution.py:182
  26.2 8.1 %collective-permute-start.1 = (f32[4,2,4,8,256]{4,3,2,1,0:T(8,128)S(1)}, f32[4,2,4,8,256]{4,3,2,1,0:T(8,128)S(1)}, u32[]{:S(2)}, u32[]{:S(2)}) collective-permute-start(f32[4,2,4,8,256]{4,3,2,1,0:T(8,128)S(1)} %get-tuple-element.11), channel_id=1, source_target_pairs={{0,4},{1,129},{2,6},{3,131},{4,0},{5,133},{6,2},{7,135},{8,12},{9,... | collective-permute-start | bytes 786440 | tf_op jit(solution)/shard_map/ppermute | solution.py:151
  27.7 8.3 %collective-permute-start.2 = (f32[4,2,4,8,256]{4,3,2,1,0:T(8,128)S(1)}, f32[4,2,4,8,256]{4,3,2,1,0:T(8,128)S(1)}, u32[]{:S(2)}, u32[]{:S(2)}) collective-permute-start(f32[4,2,4,8,256]{4,3,2,1,0:T(8,128)S(1)} %get-tuple-element.10), channel_id=1, source_target_pairs={{0,2},{1,65},{2,4},{3,67},{4,6},{5,69},{6,0},{7,71},{8,10},{9,73},... | collective-permute-start | bytes 786440 | tf_op jit(solution)/shard_map/ppermute | solution.py:151
  29.2 7.8 %collective-permute-start.3 = (f32[4,2,4,8,256]{4,3,2,1,0:T(8,128)S(1)}, f32[4,2,4,8,256]{4,3,2,1,0:T(8,128)S(1)}, u32[]{:S(2)}, u32[]{:S(2)}) collective-permute-start(f32[4,2,4,8,256]{4,3,2,1,0:T(8,128)S(1)} %get-tuple-element.9), channel_id=1, source_target_pairs={{0,6},{1,193},{2,0},{3,195},{4,2},{5,197},{6,4},{7,199},{8,14},{9,... | collective-permute-start | bytes 786440 | tf_op jit(solution)/shard_map/ppermute | solution.py:151

commit v6 on v5

--- a/solution.py
+++ b/solution.py
@@ -30,45 +30,49 @@
     return high, low
 
 
-def transform_kernel(place_ref, matrix_ref, signs_ref, own_ref, send_ref):
-    count, block, cols = matrix_ref.shape
+def transform_kernel(place_ref, matrix_hbm, signs_ref, own_ref, send_ref, matrix_ref, sems):
+    parts, step, block, _ = matrix_ref.shape
     half = block // 2
+    copies = [
+        pltpu.make_async_copy(matrix_hbm.at[pl.ds(part * step, step)], matrix_ref.at[part], sems.at[part])
+        for part in range(parts)
+    ]
+    for copy in copies:
+        copy.start()
     core = place_ref[0] & 1
     out_row = lax.broadcasted_iota(jnp.int32, (block, block), 0)
     in_row = lax.broadcasted_iota(jnp.int32, (block, block), 1)
     hadamard = hadamard_sign(out_row ^ core * half, in_row)
-    for unit in range(count):
-        high, low = two_parts(matrix_ref[unit])
-        signed = (hadamard * signs_ref[pl.ds(unit, 1), :].astype(jnp.float32)).astype(jnp.bfloat16)
-        result = jnp.dot(
-            jnp.concatenate([signed, signed], axis=1),
-            jnp.concatenate([high, low], axis=0),
-            preferred_element_type=jnp.float32,
-        )
-        own_ref[unit] = result[:half]
-        send_ref[unit] = result[half:]
+    for part in range(parts):
+        copies[part].wait()
+        for place in range(step):
+            unit = part * step + place
+            high, low = two_parts(matrix_ref[part, place])
+            signed = (hadamard * signs_ref[pl.ds(unit, 1), :].astype(jnp.float32)).astype(jnp.bfloat16)
+            result = jnp.dot(
+                jnp.concatenate([signed, signed], axis=1),
+                jnp.concatenate([high, low], axis=0),
+                preferred_element_type=jnp.float32,
+            )
+            own_ref[unit] = result[:half]
+            send_ref[unit] = result[half:]
 
 
 def transform(place, matrix, row_signs):
     count, block, cols = matrix.shape
-    step = 8
+    parts = 4
     half = jax.ShapeDtypeStruct((count, block // 2, cols), jnp.float32)
+    vmem = pl.BlockSpec(memory_space=pltpu.VMEM)
     return pl.pallas_call(
         transform_kernel,
-        grid_spec=pltpu.PrefetchScalarGridSpec(
-            num_scalar_prefetch=1,
-            grid=(count // step,),
-            in_specs=[
-                pl.BlockSpec((step, block, cols), lambda i, place: (i, 0, 0)),
-                pl.BlockSpec((step, block), lambda i, place: (i, 0)),
-            ],
-            out_specs=[
-                pl.BlockSpec((step, block // 2, cols), lambda i, place: (i, 0, 0)),
-                pl.BlockSpec((step, block // 2, cols), lambda i, place: (i, 0, 0)),
-            ],
-        ),
+        in_specs=[pl.BlockSpec(memory_space=pltpu.SMEM), pl.BlockSpec(memory_space=pltpu.HBM), vmem],
+        out_specs=[vmem, vmem],
         out_shape=[half, half],
-        compiler_params=pltpu.CompilerParams(vmem_limit_bytes=16 * MIB),
+        scratch_shapes=[
+            pltpu.VMEM((parts, count // parts, block, cols), jnp.float32),
+            pltpu.SemaphoreType.DMA((parts,)),
+        ],
+        compiler_params=pltpu.CompilerParams(vmem_limit_bytes=46 * MIB),
         cost_estimate=pl.CostEstimate(flops=2 * 2 * 128 * 128 * 256 * 32, bytes_accessed=8 * MIB, transcendentals=0),
         name="transform",
     )(place, matrix, row_signs)

time: 64 us -> 62.9 us (0.983)
  local copies, waits for them, and re-layouts: 3.62 us -> 1.43 us
  Pallas kernels: 2.89 us -> 4.03 us
    unnamed x9 -> x7, local copies, waits for them, and re-layouts: 3.54 us -> 1.35 us
    pallas_call x1, Pallas kernels: 1.43 us -> 2.57 us  [transform(): pl.pallas_call(transform_kernel, in_specs=[pl.BlockSpec(memory_space=pltp...]
where the time goes in v6:
time: 62.9 us; the launch traced here: 62.7 us
  blocking collectives  46.2 us (73%)
  waiting for transfers between devices  7.18 us (11%)
  Pallas kernels  4.03 us (6%)
  starting transfers between devices  3.69 us (6%)
  local copies, waits for them, and re-layouts  1.43 us (2%)
    all_to_all x1, blocking collectives, body(): lax.all_to_all(jnp.broadcast_to(mine[None], (devs, 2, units)), 'row', 0, 0)  20.1 us
    all_to_all x1, blocking collectives, body(): lax.all_to_all(pieces, AXES, 0, 0, axis_index_groups=second_groups())  15.8 us
    all_to_all x1, blocking collectives, body(): lax.all_to_all(jnp.broadcast_to(share[None], (groups, 8, col_count)), 'gr...  10.3 us
    ppermute x3, waiting for transfers between devices, first_shift(): return lax.ppermute(value, AXES, pairs)  7.17 us
    ppermute x3, starting transfers between devices, first_shift(): return lax.ppermute(value, AXES, pairs)  3.6 us
    pallas_call x1, Pallas kernels, transform(): pl.pallas_call(transform_kernel, in_specs=[pl.BlockSpec(memory_space=pltp...  2.57 us
    pallas_call x1, Pallas kernels, mix(): pl.pallas_call(functools.partial(mix_kernel, scale), in_specs=[pl.BlockSp...  1.46 us
    unnamed x7, local copies, waits for them, and re-layouts  1.35 us
  transfers between devices with their start and end apart: 4, of which 3 were waited for; matrix products, arithmetic and copies ran while one was open for 0% of the time, Pallas kernels for 0%

profile of v6, /device:TPU:2, one launch (start us, length us, event | category | flops | bytes accessed | tf_op | source)
XLA Modules:
  0.0 62.7 jit_solution(11276150777105309643)
XLA Ops:
  0.0 0.0 copy-start
  0.0 0.7 %copy-done = s32[4096]{0:T(1024)S(1)} copy-done((s32[4096]{0:T(1024)S(1)}, s32[4096]{0:T(1024)}, u32[]{:S(2)}) %copy-start) | copy-done | bytes 16408
  0.7 0.0 copy-start.1
  0.7 0.0 copy-start.2
  0.7 2.6 %transform.1 = (f32[32,64,256]{2,1,0:T(8,128)S(1)}, f32[32,64,256]{2,1,0:T(8,128)S(1)}) custom-call(s32[1]{0:T(128)} %bitcast.place_ref, f32[32,128,256]{2,1,0:T(8,128)} %bitcast.20, s32[32,128]{1,0:T(8,128)S(1)} %bitcast.19), custom_call_target="tpu_custom_call" | custom-call | flops 536870912 | bytes 8388608 | tf_op jit(solution)/shard_map/transform/pallas_call | solution.py:66
  3.3 0.1 collective-permute-start
  3.4 0.0 copy-done.1
  3.4 0.0 copy-done.2
  3.5 20.1 %all_to_all.15.meta_ref = s32[32,2,32]{2,1,0:T(2,128)S(1)} all-to-all(s32[32,2,32]{2,1,0:T(2,128)S(1)} %broadcast_in_dim.4), channel_id=1, replica_groups=mesh['grp'=8,'row'=32] {'row'}, dimensions={0} | all-to-all | bytes 16384 | tf_op jit(solution)/shard_map/all_to_all | solution.py:182
  23.6 0.0 collective-permute-done.other_ref
  23.6 1.5 %mix.1 = f32[4,4,2,4,8,256]{5,4,3,2,1,0:T(8,128)S(1)} custom-call(s32[1]{0:T(128)} %bitcast.place_ref, s32[32,2,32]{2,1,0:T(2,128)S(1)} %all_to_all.15.meta_ref, f32[32,64,256]{2,1,0:T(8,128)S(1)} %get-tuple-element.7.own_ref, f32[32,64,256]{2,1,0:T(8,128)S(1)} %collective-permute-done.other_ref), custom_call_target="tpu_custom_call" | custom-call | flops 805306368 | bytes 5242880 | tf_op jit(solution)/shard_map/mix/pallas_call | solution.py:128
  25.0 0.1 slice_bitcast_fusion
  25.1 1.6 %collective-permute-start.1 = (f32[4,2,4,8,256]{4,3,2,1,0:T(8,128)S(1)}, f32[4,2,4,8,256]{4,3,2,1,0:T(8,128)S(1)}, u32[]{:S(2)}, u32[]{:S(2)}) collective-permute-start(f32[4,2,4,8,256]{4,3,2,1,0:T(8,128)S(1)} %get-tuple-element.11), channel_id=1, source_target_pairs={{0,4},{1,129},{2,6},{3,131},{4,0},{5,133},{6,2},{7,135},{8,12},{9,... | collective-permute-start | bytes 786440 | tf_op jit(solution)/shard_map/ppermute | solution.py:155
  26.7 1.4 %collective-permute-start.2 = (f32[4,2,4,8,256]{4,3,2,1,0:T(8,128)S(1)}, f32[4,2,4,8,256]{4,3,2,1,0:T(8,128)S(1)}, u32[]{:S(2)}, u32[]{:S(2)}) collective-permute-start(f32[4,2,4,8,256]{4,3,2,1,0:T(8,128)S(1)} %get-tuple-element.10), channel_id=1, source_target_pairs={{0,2},{1,65},{2,4},{3,67},{4,6},{5,69},{6,0},{7,71},{8,10},{9,73},... | collective-permute-start | bytes 786440 | tf_op jit(solution)/shard_map/ppermute | solution.py:155
  28.1 0.6 collective-permute-start.3
  28.7 4.5 %collective-permute-done.1 = f32[4,2,4,8,256]{4,3,2,1,0:T(8,128)S(1)} collective-permute-done((f32[4,2,4,8,256]{4,3,2,1,0:T(8,128)S(1)}, f32[4,2,4,8,256]{4,3,2,1,0:T(8,128)S(1)}, u32[]{:S(2)}, u32[]{:S(2)}) %collective-permute-start.1) | collective-permute-done | bytes 262176 | tf_op jit(solution)/shard_map/ppermute | solution.py:155
  33.2 1.8 %collective-permute-done.2 = f32[4,2,4,8,256]{4,3,2,1,0:T(8,128)S(1)} collective-permute-done((f32[4,2,4,8,256]{4,3,2,1,0:T(8,128)S(1)}, f32[4,2,4,8,256]{4,3,2,1,0:T(8,128)S(1)}, u32[]{:S(2)}, u32[]{:S(2)}) %collective-permute-start.2) | collective-permute-done | bytes 262176 | tf_op jit(solution)/shard_map/ppermute | solution.py:155
  35.0 0.9 %collective-permute-done.3 = f32[4,2,4,8,256]{4,3,2,1,0:T(8,128)S(1)} collective-permute-done((f32[4,2,4,8,256]{4,3,2,1,0:T(8,128)S(1)}, f32[4,2,4,8,256]{4,3,2,1,0:T(8,128)S(1)}, u32[]{:S(2)}, u32[]{:S(2)}) %collective-permute-start.3) | collective-permute-done | bytes 262176 | tf_op jit(solution)/shard_map/ppermute | solution.py:155
  35.9 0.1 fusion.1
  36.0 15.8 %all_to_all.16 = f32[32,8,256]{2,1,0:T(8,128)S(1)} all-to-all(f32[32,8,256]{2,1,0:T(8,128)S(1)} %bitcast.21), channel_id=1, replica_groups={{0,8,16,24,32,40,48,56,64,72,80,88,96,104,112,120,128,136,144,152,160,1..., dimensions={0} | all-to-all | bytes 524288 | tf_op jit(solution)/shard_map/all_to_all | solution.py:192
  51.8 10.3 %all_to_all.17 = f32[8,8,256]{2,1,0:T(8,128)S(1)} all-to-all(f32[8,8,256]{2,1,0:T(8,128)S(1)} %broadcast_in_dim.5), channel_id=1, replica_groups=mesh['grp'=8,'row'=32] {'grp'}, dimensions={0} | all-to-all | bytes 131072 | tf_op jit(solution)/shard_map/all_to_all | solution.py:194
  62.0 0.6 %copy.6 = f32[64,256]{1,0:T(8,128)} copy(f32[64,256]{1,0:T(8,128)S(1)} %bitcast.22) | data formatting | bytes 131072
  (4 shorter events, 0.1 us)
Async XLA Ops:
  0.0 0.7 %copy-start = (s32[4096]{0:T(1024)S(1)}, s32[4096]{0:T(1024)}, u32[]{:S(2)}) copy-start(s32[4096]{0:T(1024)} %param.5) | copy-start | bytes 49156
  0.7 2.7 %copy-start.1 = (s32[32]{0:T(128)S(1)}, s32[32]{0:T(128)}, u32[]{:S(2)}) copy-start(s32[32]{0:T(128)} %param.7) | copy-start | bytes 388
  0.7 2.7 %copy-start.2 = (s32[32]{0:T(128)S(1)}, s32[32]{0:T(128)}, u32[]{:S(2)}) copy-start(s32[32]{0:T(128)} %param.6) | copy-start | bytes 388
  3.3 20.3 %collective-permute-start = (f32[32,64,256]{2,1,0:T(8,128)S(1)}, f32[32,64,256]{2,1,0:T(8,128)S(1)}, u32[]{:S(2)}, u32[]{:S(2)}) collective-permute-start(f32[32,64,256]{2,1,0:T(8,128)S(1)} %get-tuple-element.8), channel_id=1, source_target_pairs={{0,1},{1,0},{2,3},{3,2},{4,5},{5,4},{6,7},{7,6},{8,9},{9,8},{10,11... | collective-permute-start | bytes 6291464 | tf_op jit(solution)/shard_map/ppermute | solution.py:186
  25.1 8.1 %collective-permute-start.1 = (f32[4,2,4,8,256]{4,3,2,1,0:T(8,128)S(1)}, f32[4,2,4,8,256]{4,3,2,1,0:T(8,128)S(1)}, u32[]{:S(2)}, u32[]{:S(2)}) collective-permute-start(f32[4,2,4,8,256]{4,3,2,1,0:T(8,128)S(1)} %get-tuple-element.11), channel_id=1, source_target_pairs={{0,4},{1,129},{2,6},{3,131},{4,0},{5,133},{6,2},{7,135},{8,12},{9,... | collective-permute-start | bytes 786440 | tf_op jit(solution)/shard_map/ppermute | solution.py:155
  26.7 8.3 %collective-permute-start.2 = (f32[4,2,4,8,256]{4,3,2,1,0:T(8,128)S(1)}, f32[4,2,4,8,256]{4,3,2,1,0:T(8,128)S(1)}, u32[]{:S(2)}, u32[]{:S(2)}) collective-permute-start(f32[4,2,4,8,256]{4,3,2,1,0:T(8,128)S(1)} %get-tuple-element.10), channel_id=1, source_target_pairs={{0,2},{1,65},{2,4},{3,67},{4,6},{5,69},{6,0},{7,71},{8,10},{9,73},... | collective-permute-start | bytes 786440 | tf_op jit(solution)/shard_map/ppermute | solution.py:155
  28.1 7.8 %collective-permute-start.3 = (f32[4,2,4,8,256]{4,3,2,1,0:T(8,128)S(1)}, f32[4,2,4,8,256]{4,3,2,1,0:T(8,128)S(1)}, u32[]{:S(2)}, u32[]{:S(2)}) collective-permute-start(f32[4,2,4,8,256]{4,3,2,1,0:T(8,128)S(1)} %get-tuple-element.9), channel_id=1, source_target_pairs={{0,6},{1,193},{2,0},{3,195},{4,2},{5,197},{6,4},{7,199},{8,14},{9,... | collective-permute-start | bytes 786440 | tf_op jit(solution)/shard_map/ppermute | solution.py:155

commit v7 on v6

--- a/solution.py
+++ b/solution.py
@@ -30,9 +30,11 @@
     return high, low
 
 
-def transform_kernel(place_ref, matrix_hbm, signs_ref, own_ref, send_ref, matrix_ref, sems):
+def transform_kernel(place_ref, matrix_hbm, signs_hbm, own_ref, send_ref, matrix_ref, signs_ref, sems, signs_sem):
     parts, step, block, _ = matrix_ref.shape
     half = block // 2
+    signs_copy = pltpu.make_async_copy(signs_hbm, signs_ref, signs_sem)
+    signs_copy.start()
     copies = [
         pltpu.make_async_copy(matrix_hbm.at[pl.ds(part * step, step)], matrix_ref.at[part], sems.at[part])
         for part in range(parts)
@@ -43,6 +45,7 @@
     out_row = lax.broadcasted_iota(jnp.int32, (block, block), 0)
     in_row = lax.broadcasted_iota(jnp.int32, (block, block), 1)
     hadamard = hadamard_sign(out_row ^ core * half, in_row)
+    signs_copy.wait()
     for part in range(parts):
         copies[part].wait()
         for place in range(step):
@@ -62,20 +65,23 @@
     count, block, cols = matrix.shape
     parts = 4
     half = jax.ShapeDtypeStruct((count, block // 2, cols), jnp.float32)
+    hbm = pl.BlockSpec(memory_space=pltpu.HBM)
     vmem = pl.BlockSpec(memory_space=pltpu.VMEM)
     return pl.pallas_call(
         transform_kernel,
-        in_specs=[pl.BlockSpec(memory_space=pltpu.SMEM), pl.BlockSpec(memory_space=pltpu.HBM), vmem],
+        in_specs=[pl.BlockSpec(memory_space=pltpu.SMEM), hbm, hbm],
         out_specs=[vmem, vmem],
         out_shape=[half, half],
         scratch_shapes=[
             pltpu.VMEM((parts, count // parts, block, cols), jnp.float32),
+            pltpu.VMEM((count, block), jnp.int32),
             pltpu.SemaphoreType.DMA((parts,)),
+            pltpu.SemaphoreType.DMA,
         ],
-        compiler_params=pltpu.CompilerParams(vmem_limit_bytes=46 * MIB),
+        compiler_params=pltpu.CompilerParams(vmem_limit_bytes=16 * MIB),
         cost_estimate=pl.CostEstimate(flops=2 * 2 * 128 * 128 * 256 * 32, bytes_accessed=8 * MIB, transcendentals=0),
         name="transform",
-    )(place, matrix, row_signs)
+    )(place, pltpu.with_memory_space_constraint(matrix, pltpu.HBM), pltpu.with_memory_space_constraint(row_signs, pltpu.HBM))
 
 
 def mix_kernel(scale, place_ref, meta_ref, own_ref, other_ref, out_ref):

time: 62.9 us -> 62.6 us (level)
  local copies, waits for them, and re-layouts: 1.43 us -> 0.71 us
    unnamed x7 -> x5, local copies, waits for them, and re-layouts: 1.35 us -> 0.64 us
where the time goes in v7:
time: 62.6 us; the launch traced here: 62.4 us
  blocking collectives  46.2 us (74%)
  waiting for transfers between devices  7.18 us (11%)
  Pallas kernels  4.47 us (7%)
  starting transfers between devices  3.69 us (6%)
  local copies, waits for them, and re-layouts  0.71 us (1%)
    all_to_all x1, blocking collectives, body(): lax.all_to_all(jnp.broadcast_to(mine[None], (devs, 2, units)), 'row', 0, 0)  20.1 us
    all_to_all x1, blocking collectives, body(): lax.all_to_all(pieces, AXES, 0, 0, axis_index_groups=second_groups())  15.8 us
    all_to_all x1, blocking collectives, body(): lax.all_to_all(jnp.broadcast_to(share[None], (groups, 8, col_count)), 'gr...  10.3 us
    ppermute x3, waiting for transfers between devices, first_shift(): return lax.ppermute(value, AXES, pairs)  7.17 us
    ppermute x3, starting transfers between devices, first_shift(): return lax.ppermute(value, AXES, pairs)  3.6 us
    pallas_call x1, Pallas kernels, transform(): pl.pallas_call(transform_kernel, in_specs=[pl.BlockSpec(memory_space=pltp...  3.01 us
    pallas_call x1, Pallas kernels, mix(): pl.pallas_call(functools.partial(mix_kernel, scale), in_specs=[pl.BlockSp...  1.46 us
  transfers between devices with their start and end apart: 4, of which 3 were waited for; matrix products, arithmetic and copies ran while one was open for 0% of the time, Pallas kernels for 0%

profile of v7, /device:TPU:2, one launch (start us, length us, event | category | flops | bytes accessed | tf_op | source)
XLA Modules:
  0.0 62.4 jit_solution(16805562816675412585)
XLA Ops:
  0.0 0.0 copy-start
  0.0 0.0 copy-start.1
  0.0 3.0 %transform.1 = (f32[32,64,256]{2,1,0:T(8,128)S(1)}, f32[32,64,256]{2,1,0:T(8,128)S(1)}) custom-call(s32[1]{0:T(128)} %bitcast.place_ref, f32[32,128,256]{2,1,0:T(8,128)} %bitcast.19, s32[32,128]{1,0:T(8,128)} %bitcast.22), custom_call_target="tpu_custom_call" | custom-call | flops 536870912 | bytes 8388608 | tf_op jit(solution)/shard_map/transform/pallas_call | solution.py:70
  3.0 0.1 collective-permute-start
  3.1 0.0 copy-done
  3.1 0.0 copy-done.1
  3.2 20.1 %all_to_all.15.meta_ref = s32[32,2,32]{2,1,0:T(2,128)S(1)} all-to-all(s32[32,2,32]{2,1,0:T(2,128)S(1)} %broadcast_in_dim.4), channel_id=1, replica_groups=mesh['grp'=8,'row'=32] {'row'}, dimensions={0} | all-to-all | bytes 16384 | tf_op jit(solution)/shard_map/all_to_all | solution.py:188
  23.3 0.0 collective-permute-done.other_ref
  23.3 1.5 %mix.1 = f32[4,4,2,4,8,256]{5,4,3,2,1,0:T(8,128)S(1)} custom-call(s32[1]{0:T(128)} %bitcast.place_ref, s32[32,2,32]{2,1,0:T(2,128)S(1)} %all_to_all.15.meta_ref, f32[32,64,256]{2,1,0:T(8,128)S(1)} %get-tuple-element.7.own_ref, f32[32,64,256]{2,1,0:T(8,128)S(1)} %collective-permute-done.other_ref), custom_call_target="tpu_custom_call" | custom-call | flops 805306368 | bytes 5242880 | tf_op jit(solution)/shard_map/mix/pallas_call | solution.py:134
  24.8 0.1 slice_bitcast_fusion
  24.8 1.6 %collective-permute-start.1 = (f32[4,2,4,8,256]{4,3,2,1,0:T(8,128)S(1)}, f32[4,2,4,8,256]{4,3,2,1,0:T(8,128)S(1)}, u32[]{:S(2)}, u32[]{:S(2)}) collective-permute-start(f32[4,2,4,8,256]{4,3,2,1,0:T(8,128)S(1)} %get-tuple-element.11), channel_id=1, source_target_pairs={{0,4},{1,129},{2,6},{3,131},{4,0},{5,133},{6,2},{7,135},{8,12},{9,... | collective-permute-start | bytes 786440 | tf_op jit(solution)/shard_map/ppermute | solution.py:161
  26.4 1.5 %collective-permute-start.2 = (f32[4,2,4,8,256]{4,3,2,1,0:T(8,128)S(1)}, f32[4,2,4,8,256]{4,3,2,1,0:T(8,128)S(1)}, u32[]{:S(2)}, u32[]{:S(2)}) collective-permute-start(f32[4,2,4,8,256]{4,3,2,1,0:T(8,128)S(1)} %get-tuple-element.10), channel_id=1, source_target_pairs={{0,2},{1,65},{2,4},{3,67},{4,6},{5,69},{6,0},{7,71},{8,10},{9,73},... | collective-permute-start | bytes 786440 | tf_op jit(solution)/shard_map/ppermute | solution.py:161
  27.8 0.6 collective-permute-start.3
  28.4 4.5 %collective-permute-done.1 = f32[4,2,4,8,256]{4,3,2,1,0:T(8,128)S(1)} collective-permute-done((f32[4,2,4,8,256]{4,3,2,1,0:T(8,128)S(1)}, f32[4,2,4,8,256]{4,3,2,1,0:T(8,128)S(1)}, u32[]{:S(2)}, u32[]{:S(2)}) %collective-permute-start.1) | collective-permute-done | bytes 262176 | tf_op jit(solution)/shard_map/ppermute | solution.py:161
  32.9 1.8 %collective-permute-done.2 = f32[4,2,4,8,256]{4,3,2,1,0:T(8,128)S(1)} collective-permute-done((f32[4,2,4,8,256]{4,3,2,1,0:T(8,128)S(1)}, f32[4,2,4,8,256]{4,3,2,1,0:T(8,128)S(1)}, u32[]{:S(2)}, u32[]{:S(2)}) %collective-permute-start.2) | collective-permute-done | bytes 262176 | tf_op jit(solution)/shard_map/ppermute | solution.py:161
  34.7 0.9 %collective-permute-done.3 = f32[4,2,4,8,256]{4,3,2,1,0:T(8,128)S(1)} collective-permute-done((f32[4,2,4,8,256]{4,3,2,1,0:T(8,128)S(1)}, f32[4,2,4,8,256]{4,3,2,1,0:T(8,128)S(1)}, u32[]{:S(2)}, u32[]{:S(2)}) %collective-permute-start.3) | collective-permute-done | bytes 262176 | tf_op jit(solution)/shard_map/ppermute | solution.py:161
  35.6 0.1 fusion.1
  35.7 15.8 %all_to_all.16 = f32[32,8,256]{2,1,0:T(8,128)S(1)} all-to-all(f32[32,8,256]{2,1,0:T(8,128)S(1)} %bitcast.20), channel_id=1, replica_groups={{0,8,16,24,32,40,48,56,64,72,80,88,96,104,112,120,128,136,144,152,160,1..., dimensions={0} | all-to-all | bytes 524288 | tf_op jit(solution)/shard_map/all_to_all | solution.py:198
  51.5 10.3 %all_to_all.17 = f32[8,8,256]{2,1,0:T(8,128)S(1)} all-to-all(f32[8,8,256]{2,1,0:T(8,128)S(1)} %broadcast_in_dim.5), channel_id=1, replica_groups=mesh['grp'=8,'row'=32] {'grp'}, dimensions={0} | all-to-all | bytes 131072 | tf_op jit(solution)/shard_map/all_to_all | solution.py:200
  61.8 0.6 %copy.6 = f32[64,256]{1,0:T(8,128)} copy(f32[64,256]{1,0:T(8,128)S(1)} %bitcast.21) | data formatting | bytes 131072
  (4 shorter events, 0.1 us)
Async XLA Ops:
  0.0 3.1 %copy-start = (s32[32]{0:T(128)S(1)}, s32[32]{0:T(128)}, u32[]{:S(2)}) copy-start(s32[32]{0:T(128)} %param.7) | copy-start | bytes 388
  0.0 3.1 %copy-start.1 = (s32[32]{0:T(128)S(1)}, s32[32]{0:T(128)}, u32[]{:S(2)}) copy-start(s32[32]{0:T(128)} %param.6) | copy-start | bytes 388
  3.0 20.3 %collective-permute-start = (f32[32,64,256]{2,1,0:T(8,128)S(1)}, f32[32,64,256]{2,1,0:T(8,128)S(1)}, u32[]{:S(2)}, u32[]{:S(2)}) collective-permute-start(f32[32,64,256]{2,1,0:T(8,128)S(1)} %get-tuple-element.8), channel_id=1, source_target_pairs={{0,1},{1,0},{2,3},{3,2},{4,5},{5,4},{6,7},{7,6},{8,9},{9,8},{10,11... | collective-permute-start | bytes 6291464 | tf_op jit(solution)/shard_map/ppermute | solution.py:192
  24.8 8.1 %collective-permute-start.1 = (f32[4,2,4,8,256]{4,3,2,1,0:T(8,128)S(1)}, f32[4,2,4,8,256]{4,3,2,1,0:T(8,128)S(1)}, u32[]{:S(2)}, u32[]{:S(2)}) collective-permute-start(f32[4,2,4,8,256]{4,3,2,1,0:T(8,128)S(1)} %get-tuple-element.11), channel_id=1, source_target_pairs={{0,4},{1,129},{2,6},{3,131},{4,0},{5,133},{6,2},{7,135},{8,12},{9,... | collective-permute-start | bytes 786440 | tf_op jit(solution)/shard_map/ppermute | solution.py:161
  26.4 8.3 %collective-permute-start.2 = (f32[4,2,4,8,256]{4,3,2,1,0:T(8,128)S(1)}, f32[4,2,4,8,256]{4,3,2,1,0:T(8,128)S(1)}, u32[]{:S(2)}, u32[]{:S(2)}) collective-permute-start(f32[4,2,4,8,256]{4,3,2,1,0:T(8,128)S(1)} %get-tuple-element.10), channel_id=1, source_target_pairs={{0,2},{1,65},{2,4},{3,67},{4,6},{5,69},{6,0},{7,71},{8,10},{9,73},... | collective-permute-start | bytes 786440 | tf_op jit(solution)/shard_map/ppermute | solution.py:161
  27.8 7.8 %collective-permute-start.3 = (f32[4,2,4,8,256]{4,3,2,1,0:T(8,128)S(1)}, f32[4,2,4,8,256]{4,3,2,1,0:T(8,128)S(1)}, u32[]{:S(2)}, u32[]{:S(2)}) collective-permute-start(f32[4,2,4,8,256]{4,3,2,1,0:T(8,128)S(1)} %get-tuple-element.9), channel_id=1, source_target_pairs={{0,6},{1,193},{2,0},{3,195},{4,2},{5,197},{6,4},{7,199},{8,14},{9,... | collective-permute-start | bytes 786440 | tf_op jit(solution)/shard_map/ppermute | solution.py:161

commit v8 on v7

--- a/solution.py
+++ b/solution.py
@@ -63,7 +63,7 @@
 
 def transform(place, matrix, row_signs):
     count, block, cols = matrix.shape
-    parts = 4
+    parts = 8
     half = jax.ShapeDtypeStruct((count, block // 2, cols), jnp.float32)
     hbm = pl.BlockSpec(memory_space=pltpu.HBM)
     vmem = pl.BlockSpec(memory_space=pltpu.VMEM)
@@ -114,14 +114,15 @@
         high, low = two_parts(jnp.where(keep, weights, 0.0))
         highs.append(high)
         lows.append(low)
-    left = jnp.concatenate(highs + highs + lows, axis=1)
+    left = jnp.concatenate(highs, axis=1)
+    stacked = jnp.concatenate([left, jnp.concatenate(lows, axis=1)], axis=0)
     for step, low_z in itertools.product(range(near), range(low_count)):
         piece = (first_y + step) % near * low_count + low_z
         span = pl.ds(pl.multiple_of(piece * rows, rows), rows)
         parts = [two_parts(ref[:, span, :].reshape(wide, cols)) for ref in (own_ref, other_ref)]
-        high = [part[0] for part in parts]
-        low = [part[1] for part in parts]
-        result = jnp.dot(left, jnp.concatenate(high + low + high, axis=0), preferred_element_type=jnp.float32)
+        high, low = (jnp.concatenate(each, axis=0) for each in zip(*parts))
+        both = jnp.dot(stacked, high, preferred_element_type=jnp.float32)
+        result = jnp.dot(left, low, preferred_element_type=jnp.float32) + (both[:tall] + both[tall:])
         result = result.reshape(near, far, rows, cols)
         for turn in range(near):
             out_ref[jnp.where(core == 0, turn, step), jnp.where(core == 0, step, turn), low_z] = result[turn]

time: 62.6 us -> 63.3 us (1.011)
  Pallas kernels: 4.47 us -> 5.14 us
    pallas_call x1, Pallas kernels: 3.01 us -> 3.86 us  [transform(): pl.pallas_call(transform_kernel, in_specs=[pl.BlockSpec(memory_space=pltp...]
where the time goes in v8:
time: 63.3 us; the launch traced here: 63.1 us
  blocking collectives  46.2 us (73%)
  waiting for transfers between devices  7.18 us (11%)
  Pallas kernels  5.14 us (8%)
  starting transfers between devices  3.68 us (6%)
  local copies, waits for them, and re-layouts  0.71 us (1%)
    all_to_all x1, blocking collectives, body(): lax.all_to_all(jnp.broadcast_to(mine[None], (devs, 2, units)), 'row', 0, 0)  20.1 us
    all_to_all x1, blocking collectives, body(): lax.all_to_all(pieces, AXES, 0, 0, axis_index_groups=second_groups())  15.8 us
    all_to_all x1, blocking collectives, body(): lax.all_to_all(jnp.broadcast_to(share[None], (groups, 8, col_count)), 'gr...  10.3 us
    ppermute x3, waiting for transfers between devices, first_shift(): return lax.ppermute(value, AXES, pairs)  7.18 us
    pallas_call x1, Pallas kernels, transform(): pl.pallas_call(transform_kernel, in_specs=[pl.BlockSpec(memory_space=pltp...  3.86 us
    ppermute x3, starting transfers between devices, first_shift(): return lax.ppermute(value, AXES, pairs)  3.59 us
    pallas_call x1, Pallas kernels, mix(): pl.pallas_call(functools.partial(mix_kernel, scale), in_specs=[pl.BlockSp...  1.28 us
  transfers between devices with their start and end apart: 4, of which 3 were waited for; matrix products, arithmetic and copies ran while one was open for 0% of the time, Pallas kernels for 0%

profile of v8, /device:TPU:2, one launch (start us, length us, event | category | flops | bytes accessed | tf_op | source)
XLA Modules:
  0.0 63.1 jit_solution(17118120410495184333)
XLA Ops:
  0.0 0.0 copy-start
  0.0 0.0 copy-start.1
  0.0 3.9 %transform.1 = (f32[32,64,256]{2,1,0:T(8,128)S(1)}, f32[32,64,256]{2,1,0:T(8,128)S(1)}) custom-call(s32[1]{0:T(128)} %bitcast.place_ref, f32[32,128,256]{2,1,0:T(8,128)} %bitcast.19, s32[32,128]{1,0:T(8,128)} %bitcast.22), custom_call_target="tpu_custom_call" | custom-call | flops 536870912 | bytes 8388608 | tf_op jit(solution)/shard_map/transform/pallas_call | solution.py:70
  3.9 0.1 collective-permute-start
  4.0 0.0 copy-done
  4.0 0.0 copy-done.1
  4.0 20.1 %all_to_all.15.meta_ref = s32[32,2,32]{2,1,0:T(2,128)S(1)} all-to-all(s32[32,2,32]{2,1,0:T(2,128)S(1)} %broadcast_in_dim.4), channel_id=1, replica_groups=mesh['grp'=8,'row'=32] {'row'}, dimensions={0} | all-to-all | bytes 16384 | tf_op jit(solution)/shard_map/all_to_all | solution.py:189
  24.1 0.0 collective-permute-done.other_ref
  24.1 1.3 %mix.1 = f32[4,4,2,4,8,256]{5,4,3,2,1,0:T(8,128)S(1)} custom-call(s32[1]{0:T(128)} %bitcast.place_ref, s32[32,2,32]{2,1,0:T(2,128)S(1)} %all_to_all.15.meta_ref, f32[32,64,256]{2,1,0:T(8,128)S(1)} %get-tuple-element.7.own_ref, f32[32,64,256]{2,1,0:T(8,128)S(1)} %collective-permute-done.other_ref), custom_call_target="tpu_custom_call" | custom-call | flops 805306368 | bytes 5242880 | tf_op jit(solution)/shard_map/mix/pallas_call | solution.py:135
  25.4 0.1 slice_bitcast_fusion
  25.5 1.6 %collective-permute-start.1 = (f32[4,2,4,8,256]{4,3,2,1,0:T(8,128)S(1)}, f32[4,2,4,8,256]{4,3,2,1,0:T(8,128)S(1)}, u32[]{:S(2)}, u32[]{:S(2)}) collective-permute-start(f32[4,2,4,8,256]{4,3,2,1,0:T(8,128)S(1)} %get-tuple-element.11), channel_id=1, source_target_pairs={{0,4},{1,129},{2,6},{3,131},{4,0},{5,133},{6,2},{7,135},{8,12},{9,... | collective-permute-start | bytes 786440 | tf_op jit(solution)/shard_map/ppermute | solution.py:162
  27.1 1.5 %collective-permute-start.2 = (f32[4,2,4,8,256]{4,3,2,1,0:T(8,128)S(1)}, f32[4,2,4,8,256]{4,3,2,1,0:T(8,128)S(1)}, u32[]{:S(2)}, u32[]{:S(2)}) collective-permute-start(f32[4,2,4,8,256]{4,3,2,1,0:T(8,128)S(1)} %get-tuple-element.10), channel_id=1, source_target_pairs={{0,2},{1,65},{2,4},{3,67},{4,6},{5,69},{6,0},{7,71},{8,10},{9,73},... | collective-permute-start | bytes 786440 | tf_op jit(solution)/shard_map/ppermute | solution.py:162
  28.5 0.6 collective-permute-start.3
  29.1 4.5 %collective-permute-done.1 = f32[4,2,4,8,256]{4,3,2,1,0:T(8,128)S(1)} collective-permute-done((f32[4,2,4,8,256]{4,3,2,1,0:T(8,128)S(1)}, f32[4,2,4,8,256]{4,3,2,1,0:T(8,128)S(1)}, u32[]{:S(2)}, u32[]{:S(2)}) %collective-permute-start.1) | collective-permute-done | bytes 262176 | tf_op jit(solution)/shard_map/ppermute | solution.py:162
  33.6 1.8 %collective-permute-done.2 = f32[4,2,4,8,256]{4,3,2,1,0:T(8,128)S(1)} collective-permute-done((f32[4,2,4,8,256]{4,3,2,1,0:T(8,128)S(1)}, f32[4,2,4,8,256]{4,3,2,1,0:T(8,128)S(1)}, u32[]{:S(2)}, u32[]{:S(2)}) %collective-permute-start.2) | collective-permute-done | bytes 262176 | tf_op jit(solution)/shard_map/ppermute | solution.py:162
  35.4 0.9 %collective-permute-done.3 = f32[4,2,4,8,256]{4,3,2,1,0:T(8,128)S(1)} collective-permute-done((f32[4,2,4,8,256]{4,3,2,1,0:T(8,128)S(1)}, f32[4,2,4,8,256]{4,3,2,1,0:T(8,128)S(1)}, u32[]{:S(2)}, u32[]{:S(2)}) %collective-permute-start.3) | collective-permute-done | bytes 262176 | tf_op jit(solution)/shard_map/ppermute | solution.py:162
  36.3 0.1 fusion.1
  36.3 15.8 %all_to_all.16 = f32[32,8,256]{2,1,0:T(8,128)S(1)} all-to-all(f32[32,8,256]{2,1,0:T(8,128)S(1)} %bitcast.20), channel_id=1, replica_groups={{0,8,16,24,32,40,48,56,64,72,80,88,96,104,112,120,128,136,144,152,160,1..., dimensions={0} | all-to-all | bytes 524288 | tf_op jit(solution)/shard_map/all_to_all | solution.py:199
  52.2 10.3 %all_to_all.17 = f32[8,8,256]{2,1,0:T(8,128)S(1)} all-to-all(f32[8,8,256]{2,1,0:T(8,128)S(1)} %broadcast_in_dim.5), channel_id=1, replica_groups=mesh['grp'=8,'row'=32] {'grp'}, dimensions={0} | all-to-all | bytes 131072 | tf_op jit(solution)/shard_map/all_to_all | solution.py:201
  62.4 0.6 copy.6
  (4 shorter events, 0.1 us)
Async XLA Ops:
  0.0 4.0 %copy-start = (s32[32]{0:T(128)S(1)}, s32[32]{0:T(128)}, u32[]{:S(2)}) copy-start(s32[32]{0:T(128)} %param.7) | copy-start | bytes 388
  0.0 4.0 %copy-start.1 = (s32[32]{0:T(128)S(1)}, s32[32]{0:T(128)}, u32[]{:S(2)}) copy-start(s32[32]{0:T(128)} %param.6) | copy-start | bytes 388
  3.9 20.3 %collective-permute-start = (f32[32,64,256]{2,1,0:T(8,128)S(1)}, f32[32,64,256]{2,1,0:T(8,128)S(1)}, u32[]{:S(2)}, u32[]{:S(2)}) collective-permute-start(f32[32,64,256]{2,1,0:T(8,128)S(1)} %get-tuple-element.8), channel_id=1, source_target_pairs={{0,1},{1,0},{2,3},{3,2},{4,5},{5,4},{6,7},{7,6},{8,9},{9,8},{10,11... | collective-permute-start | bytes 6291464 | tf_op jit(solution)/shard_map/ppermute | solution.py:193
  25.5 8.1 %collective-permute-start.1 = (f32[4,2,4,8,256]{4,3,2,1,0:T(8,128)S(1)}, f32[4,2,4,8,256]{4,3,2,1,0:T(8,128)S(1)}, u32[]{:S(2)}, u32[]{:S(2)}) collective-permute-start(f32[4,2,4,8,256]{4,3,2,1,0:T(8,128)S(1)} %get-tuple-element.11), channel_id=1, source_target_pairs={{0,4},{1,129},{2,6},{3,131},{4,0},{5,133},{6,2},{7,135},{8,12},{9,... | collective-permute-start | bytes 786440 | tf_op jit(solution)/shard_map/ppermute | solution.py:162
  27.1 8.3 %collective-permute-start.2 = (f32[4,2,4,8,256]{4,3,2,1,0:T(8,128)S(1)}, f32[4,2,4,8,256]{4,3,2,1,0:T(8,128)S(1)}, u32[]{:S(2)}, u32[]{:S(2)}) collective-permute-start(f32[4,2,4,8,256]{4,3,2,1,0:T(8,128)S(1)} %get-tuple-element.10), channel_id=1, source_target_pairs={{0,2},{1,65},{2,4},{3,67},{4,6},{5,69},{6,0},{7,71},{8,10},{9,73},... | collective-permute-start | bytes 786440 | tf_op jit(solution)/shard_map/ppermute | solution.py:162
  28.5 7.8 %collective-permute-start.3 = (f32[4,2,4,8,256]{4,3,2,1,0:T(8,128)S(1)}, f32[4,2,4,8,256]{4,3,2,1,0:T(8,128)S(1)}, u32[]{:S(2)}, u32[]{:S(2)}) collective-permute-start(f32[4,2,4,8,256]{4,3,2,1,0:T(8,128)S(1)} %get-tuple-element.9), channel_id=1, source_target_pairs={{0,6},{1,193},{2,0},{3,195},{4,2},{5,197},{6,4},{7,199},{8,14},{9,... | collective-permute-start | bytes 786440 | tf_op jit(solution)/shard_map/ppermute | solution.py:162

commit v9 on v8

--- a/solution.py
+++ b/solution.py
@@ -63,7 +63,7 @@
 
 def transform(place, matrix, row_signs):
     count, block, cols = matrix.shape
-    parts = 8
+    parts = 4
     half = jax.ShapeDtypeStruct((count, block // 2, cols), jnp.float32)
     hbm = pl.BlockSpec(memory_space=pltpu.HBM)
     vmem = pl.BlockSpec(memory_space=pltpu.VMEM)

time: 63.3 us -> 62.4 us (0.986)
  Pallas kernels: 5.14 us -> 4.28 us
    pallas_call x1, Pallas kernels: 3.86 us -> 3.01 us  [transform(): pl.pallas_call(transform_kernel, in_specs=[pl.BlockSpec(memory_space=pltp...]
where the time goes in v9:
time: 62.4 us; the launch traced here: 62.2 us
  blocking collectives  46.2 us (74%)
  waiting for transfers between devices  7.17 us (11%)
  Pallas kernels  4.28 us (7%)
  starting transfers between devices  3.7 us (6%)
  local copies, waits for them, and re-layouts  0.71 us (1%)
    all_to_all x1, blocking collectives, body(): lax.all_to_all(jnp.broadcast_to(mine[None], (devs, 2, units)), 'row', 0, 0)  20.1 us
    all_to_all x1, blocking collectives, body(): lax.all_to_all(pieces, AXES, 0, 0, axis_index_groups=second_groups())  15.8 us
    all_to_all x1, blocking collectives, body(): lax.all_to_all(jnp.broadcast_to(share[None], (groups, 8, col_count)), 'gr...  10.3 us
    ppermute x3, waiting for transfers between devices, first_shift(): return lax.ppermute(value, AXES, pairs)  7.17 us
    ppermute x3, starting transfers between devices, first_shift(): return lax.ppermute(value, AXES, pairs)  3.6 us
    pallas_call x1, Pallas kernels, transform(): pl.pallas_call(transform_kernel, in_specs=[pl.BlockSpec(memory_space=pltp...  3.01 us
    pallas_call x1, Pallas kernels, mix(): pl.pallas_call(functools.partial(mix_kernel, scale), in_specs=[pl.BlockSp...  1.28 us
  transfers between devices with their start and end apart: 4, of which 3 were waited for; matrix products, arithmetic and copies ran while one was open for 0% of the time, Pallas kernels for 0%

profile of v9, /device:TPU:2, one launch (start us, length us, event | category | flops | bytes accessed | tf_op | source)
XLA Modules:
  0.0 62.2 jit_solution(3018316131253595035)
XLA Ops:
  0.0 0.0 copy-start
  0.0 0.0 copy-start.1
  0.0 3.0 %transform.1 = (f32[32,64,256]{2,1,0:T(8,128)S(1)}, f32[32,64,256]{2,1,0:T(8,128)S(1)}) custom-call(s32[1]{0:T(128)} %bitcast.place_ref, f32[32,128,256]{2,1,0:T(8,128)} %bitcast.19, s32[32,128]{1,0:T(8,128)} %bitcast.22), custom_call_target="tpu_custom_call" | custom-call | flops 536870912 | bytes 8388608 | tf_op jit(solution)/shard_map/transform/pallas_call | solution.py:70
  3.0 0.1 collective-permute-start
  3.1 0.0 copy-done
  3.1 0.0 copy-done.1
  3.2 20.1 %all_to_all.15.meta_ref = s32[32,2,32]{2,1,0:T(2,128)S(1)} all-to-all(s32[32,2,32]{2,1,0:T(2,128)S(1)} %broadcast_in_dim.4), channel_id=1, replica_groups=mesh['grp'=8,'row'=32] {'row'}, dimensions={0} | all-to-all | bytes 16384 | tf_op jit(solution)/shard_map/all_to_all | solution.py:189
  23.3 0.0 collective-permute-done.other_ref
  23.3 1.3 %mix.1 = f32[4,4,2,4,8,256]{5,4,3,2,1,0:T(8,128)S(1)} custom-call(s32[1]{0:T(128)} %bitcast.place_ref, s32[32,2,32]{2,1,0:T(2,128)S(1)} %all_to_all.15.meta_ref, f32[32,64,256]{2,1,0:T(8,128)S(1)} %get-tuple-element.7.own_ref, f32[32,64,256]{2,1,0:T(8,128)S(1)} %collective-permute-done.other_ref), custom_call_target="tpu_custom_call" | custom-call | flops 805306368 | bytes 5242880 | tf_op jit(solution)/shard_map/mix/pallas_call | solution.py:135
  24.6 0.1 slice_bitcast_fusion
  24.6 1.6 %collective-permute-start.1 = (f32[4,2,4,8,256]{4,3,2,1,0:T(8,128)S(1)}, f32[4,2,4,8,256]{4,3,2,1,0:T(8,128)S(1)}, u32[]{:S(2)}, u32[]{:S(2)}) collective-permute-start(f32[4,2,4,8,256]{4,3,2,1,0:T(8,128)S(1)} %get-tuple-element.11), channel_id=1, source_target_pairs={{0,4},{1,129},{2,6},{3,131},{4,0},{5,133},{6,2},{7,135},{8,12},{9,... | collective-permute-start | bytes 786440 | tf_op jit(solution)/shard_map/ppermute | solution.py:162
  26.2 1.4 %collective-permute-start.2 = (f32[4,2,4,8,256]{4,3,2,1,0:T(8,128)S(1)}, f32[4,2,4,8,256]{4,3,2,1,0:T(8,128)S(1)}, u32[]{:S(2)}, u32[]{:S(2)}) collective-permute-start(f32[4,2,4,8,256]{4,3,2,1,0:T(8,128)S(1)} %get-tuple-element.10), channel_id=1, source_target_pairs={{0,2},{1,65},{2,4},{3,67},{4,6},{5,69},{6,0},{7,71},{8,10},{9,73},... | collective-permute-start | bytes 786440 | tf_op jit(solution)/shard_map/ppermute | solution.py:162
  27.7 0.6 collective-permute-start.3
  28.3 4.5 %collective-permute-done.1 = f32[4,2,4,8,256]{4,3,2,1,0:T(8,128)S(1)} collective-permute-done((f32[4,2,4,8,256]{4,3,2,1,0:T(8,128)S(1)}, f32[4,2,4,8,256]{4,3,2,1,0:T(8,128)S(1)}, u32[]{:S(2)}, u32[]{:S(2)}) %collective-permute-start.1) | collective-permute-done | bytes 262176 | tf_op jit(solution)/shard_map/ppermute | solution.py:162
  32.7 1.8 %collective-permute-done.2 = f32[4,2,4,8,256]{4,3,2,1,0:T(8,128)S(1)} collective-permute-done((f32[4,2,4,8,256]{4,3,2,1,0:T(8,128)S(1)}, f32[4,2,4,8,256]{4,3,2,1,0:T(8,128)S(1)}, u32[]{:S(2)}, u32[]{:S(2)}) %collective-permute-start.2) | collective-permute-done | bytes 262176 | tf_op jit(solution)/shard_map/ppermute | solution.py:162
  34.5 0.9 %collective-permute-done.3 = f32[4,2,4,8,256]{4,3,2,1,0:T(8,128)S(1)} collective-permute-done((f32[4,2,4,8,256]{4,3,2,1,0:T(8,128)S(1)}, f32[4,2,4,8,256]{4,3,2,1,0:T(8,128)S(1)}, u32[]{:S(2)}, u32[]{:S(2)}) %collective-permute-start.3) | collective-permute-done | bytes 262176 | tf_op jit(solution)/shard_map/ppermute | solution.py:162
  35.4 0.1 fusion.1
  35.5 15.8 %all_to_all.16 = f32[32,8,256]{2,1,0:T(8,128)S(1)} all-to-all(f32[32,8,256]{2,1,0:T(8,128)S(1)} %bitcast.20), channel_id=1, replica_groups={{0,8,16,24,32,40,48,56,64,72,80,88,96,104,112,120,128,136,144,152,160,1..., dimensions={0} | all-to-all | bytes 524288 | tf_op jit(solution)/shard_map/all_to_all | solution.py:199
  51.3 10.3 %all_to_all.17 = f32[8,8,256]{2,1,0:T(8,128)S(1)} all-to-all(f32[8,8,256]{2,1,0:T(8,128)S(1)} %broadcast_in_dim.5), channel_id=1, replica_groups=mesh['grp'=8,'row'=32] {'grp'}, dimensions={0} | all-to-all | bytes 131072 | tf_op jit(solution)/shard_map/all_to_all | solution.py:201
  61.6 0.6 %copy.6 = f32[64,256]{1,0:T(8,128)} copy(f32[64,256]{1,0:T(8,128)S(1)} %bitcast.21) | data formatting | bytes 131072
  (4 shorter events, 0.1 us)
Async XLA Ops:
  0.0 3.1 %copy-start = (s32[32]{0:T(128)S(1)}, s32[32]{0:T(128)}, u32[]{:S(2)}) copy-start(s32[32]{0:T(128)} %param.7) | copy-start | bytes 388
  0.0 3.1 %copy-start.1 = (s32[32]{0:T(128)S(1)}, s32[32]{0:T(128)}, u32[]{:S(2)}) copy-start(s32[32]{0:T(128)} %param.6) | copy-start | bytes 388
  3.0 20.3 %collective-permute-start = (f32[32,64,256]{2,1,0:T(8,128)S(1)}, f32[32,64,256]{2,1,0:T(8,128)S(1)}, u32[]{:S(2)}, u32[]{:S(2)}) collective-permute-start(f32[32,64,256]{2,1,0:T(8,128)S(1)} %get-tuple-element.8), channel_id=1, source_target_pairs={{0,1},{1,0},{2,3},{3,2},{4,5},{5,4},{6,7},{7,6},{8,9},{9,8},{10,11... | collective-permute-start | bytes 6291464 | tf_op jit(solution)/shard_map/ppermute | solution.py:193
  24.6 8.1 %collective-permute-start.1 = (f32[4,2,4,8,256]{4,3,2,1,0:T(8,128)S(1)}, f32[4,2,4,8,256]{4,3,2,1,0:T(8,128)S(1)}, u32[]{:S(2)}, u32[]{:S(2)}) collective-permute-start(f32[4,2,4,8,256]{4,3,2,1,0:T(8,128)S(1)} %get-tuple-element.11), channel_id=1, source_target_pairs={{0,4},{1,129},{2,6},{3,131},{4,0},{5,133},{6,2},{7,135},{8,12},{9,... | collective-permute-start | bytes 786440 | tf_op jit(solution)/shard_map/ppermute | solution.py:162
  26.2 8.3 %collective-permute-start.2 = (f32[4,2,4,8,256]{4,3,2,1,0:T(8,128)S(1)}, f32[4,2,4,8,256]{4,3,2,1,0:T(8,128)S(1)}, u32[]{:S(2)}, u32[]{:S(2)}) collective-permute-start(f32[4,2,4,8,256]{4,3,2,1,0:T(8,128)S(1)} %get-tuple-element.10), channel_id=1, source_target_pairs={{0,2},{1,65},{2,4},{3,67},{4,6},{5,69},{6,0},{7,71},{8,10},{9,73},... | collective-permute-start | bytes 786440 | tf_op jit(solution)/shard_map/ppermute | solution.py:162
  27.7 7.7 %collective-permute-start.3 = (f32[4,2,4,8,256]{4,3,2,1,0:T(8,128)S(1)}, f32[4,2,4,8,256]{4,3,2,1,0:T(8,128)S(1)}, u32[]{:S(2)}, u32[]{:S(2)}) collective-permute-start(f32[4,2,4,8,256]{4,3,2,1,0:T(8,128)S(1)} %get-tuple-element.9), channel_id=1, source_target_pairs={{0,6},{1,193},{2,0},{3,195},{4,2},{5,197},{6,4},{7,199},{8,14},{9,... | collective-permute-start | bytes 786440 | tf_op jit(solution)/shard_map/ppermute | solution.py:162

commit v10 on v9

--- a/solution.py
+++ b/solution.py
@@ -30,28 +30,26 @@
     return high, low
 
 
-def transform_kernel(place_ref, matrix_hbm, signs_hbm, own_ref, send_ref, matrix_ref, signs_ref, sems, signs_sem):
-    parts, step, block, _ = matrix_ref.shape
+def transform_kernel(cuts, place_ref, matrix_hbm, signs_hbm, own_ref, send_ref, matrix_ref, signs_ref, sems, signs_sem):
+    block = matrix_ref.shape[1]
     half = block // 2
     signs_copy = pltpu.make_async_copy(signs_hbm, signs_ref, signs_sem)
     signs_copy.start()
-    copies = [
-        pltpu.make_async_copy(matrix_hbm.at[pl.ds(part * step, step)], matrix_ref.at[part], sems.at[part])
-        for part in range(parts)
-    ]
-    for copy in copies:
-        copy.start()
+    copies = []
+    for part, (first, last) in enumerate(itertools.pairwise(cuts)):
+        span = pl.ds(first, last - first)
+        copies.append(pltpu.make_async_copy(matrix_hbm.at[span], matrix_ref.at[span], sems.at[part]))
+        copies[-1].start()
     core = place_ref[0] & 1
     out_row = lax.broadcasted_iota(jnp.int32, (block, block), 0)
     in_row = lax.broadcasted_iota(jnp.int32, (block, block), 1)
-    hadamard = hadamard_sign(out_row ^ core * half, in_row)
+    hadamard = hadamard_sign(out_row ^ core * half, in_row).astype(jnp.bfloat16)
     signs_copy.wait()
-    for part in range(parts):
-        copies[part].wait()
-        for place in range(step):
-            unit = part * step + place
-            high, low = two_parts(matrix_ref[part, place])
-            signed = (hadamard * signs_ref[pl.ds(unit, 1), :].astype(jnp.float32)).astype(jnp.bfloat16)
+    for copy, (first, last) in zip(copies, itertools.pairwise(cuts)):
+        copy.wait()
+        for unit in range(first, last):
+            high, low = two_parts(matrix_ref[unit])
+            signed = hadamard * signs_ref[pl.ds(unit, 1), :].astype(jnp.float32).astype(jnp.bfloat16)
             result = jnp.dot(
                 jnp.concatenate([signed, signed], axis=1),
                 jnp.concatenate([high, low], axis=0),
@@ -63,25 +61,29 @@
 
 def transform(place, matrix, row_signs):
     count, block, cols = matrix.shape
-    parts = 4
+    cuts = (0, count // 4, count * 5 // 8, count)
     half = jax.ShapeDtypeStruct((count, block // 2, cols), jnp.float32)
     hbm = pl.BlockSpec(memory_space=pltpu.HBM)
     vmem = pl.BlockSpec(memory_space=pltpu.VMEM)
     return pl.pallas_call(
-        transform_kernel,
+        functools.partial(transform_kernel, cuts),
         in_specs=[pl.BlockSpec(memory_space=pltpu.SMEM), hbm, hbm],
         out_specs=[vmem, vmem],
         out_shape=[half, half],
         scratch_shapes=[
-            pltpu.VMEM((parts, count // parts, block, cols), jnp.float32),
+            pltpu.VMEM(matrix.shape, jnp.float32),
             pltpu.VMEM((count, block), jnp.int32),
-            pltpu.SemaphoreType.DMA((parts,)),
+            pltpu.SemaphoreType.DMA((len(cuts) - 1,)),
             pltpu.SemaphoreType.DMA,
         ],
         compiler_params=pltpu.CompilerParams(vmem_limit_bytes=16 * MIB),
         cost_estimate=pl.CostEstimate(flops=2 * 2 * 128 * 128 * 256 * 32, bytes_accessed=8 * MIB, transcendentals=0),
         name="transform",
-    )(place, pltpu.with_memory_space_constraint(matrix, pltpu.HBM), pltpu.with_memory_space_constraint(row_signs, pltpu.HBM))
+    )(
+        place,
+        pltpu.with_memory_space_constraint(matrix, pltpu.HBM),
+        pltpu.with_memory_space_constraint(row_signs, pltpu.HBM),
+    )
 
 
 def mix_kernel(scale, place_ref, meta_ref, own_ref, other_ref, out_ref):

time: 62.4 us -> 62.1 us (level)
  no operation moved by 1% of the time
where the time goes in v10:
time: 62.1 us; the launch traced here: 61.9 us
  blocking collectives  46.2 us (74%)
  waiting for transfers between devices  7.17 us (12%)
  Pallas kernels  3.94 us (6%)
  starting transfers between devices  3.7 us (6%)
  local copies, waits for them, and re-layouts  0.71 us (1%)
    all_to_all x1, blocking collectives, body(): lax.all_to_all(jnp.broadcast_to(mine[None], (devs, 2, units)), 'row', 0, 0)  20.1 us
    all_to_all x1, blocking collectives, body(): lax.all_to_all(pieces, AXES, 0, 0, axis_index_groups=second_groups())  15.8 us
    all_to_all x1, blocking collectives, body(): lax.all_to_all(jnp.broadcast_to(share[None], (groups, 8, col_count)), 'gr...  10.3 us
    ppermute x3, waiting for transfers between devices, first_shift(): return lax.ppermute(value, AXES, pairs)  7.17 us
    ppermute x3, starting transfers between devices, first_shift(): return lax.ppermute(value, AXES, pairs)  3.6 us
    pallas_call x1, Pallas kernels, transform(): pl.pallas_call(functools.partial(transform_kernel, cuts), in_specs=[pl.Bl...  2.66 us
    pallas_call x1, Pallas kernels, mix(): pl.pallas_call(functools.partial(mix_kernel, scale), in_specs=[pl.BlockSp...  1.28 us
  transfers between devices with their start and end apart: 4, of which 3 were waited for; matrix products, arithmetic and copies ran while one was open for 0% of the time, Pallas kernels for 0%

profile of v10, /device:TPU:2, one launch (start us, length us, event | category | flops | bytes accessed | tf_op | source)
XLA Modules:
  0.0 61.9 jit_solution(2145015950325949735)
XLA Ops:
  0.0 0.0 copy-start
  0.0 0.0 copy-start.1
  0.0 2.7 %transform.1 = (f32[32,64,256]{2,1,0:T(8,128)S(1)}, f32[32,64,256]{2,1,0:T(8,128)S(1)}) custom-call(s32[1]{0:T(128)} %bitcast.place_ref, f32[32,128,256]{2,1,0:T(8,128)} %bitcast.19, s32[32,128]{1,0:T(8,128)} %bitcast.22), custom_call_target="tpu_custom_call" | custom-call | flops 536870912 | bytes 8388608 | tf_op jit(solution)/shard_map/transform/pallas_call | solution.py:68
  2.7 0.1 collective-permute-start
  2.8 0.0 copy-done
  2.8 0.0 copy-done.1
  2.8 20.1 %all_to_all.15.meta_ref = s32[32,2,32]{2,1,0:T(2,128)S(1)} all-to-all(s32[32,2,32]{2,1,0:T(2,128)S(1)} %broadcast_in_dim.4), channel_id=1, replica_groups=mesh['grp'=8,'row'=32] {'row'}, dimensions={0} | all-to-all | bytes 16384 | tf_op jit(solution)/shard_map/all_to_all | solution.py:191
  22.9 0.0 collective-permute-done.other_ref
  23.0 1.3 %mix.1 = f32[4,4,2,4,8,256]{5,4,3,2,1,0:T(8,128)S(1)} custom-call(s32[1]{0:T(128)} %bitcast.place_ref, s32[32,2,32]{2,1,0:T(2,128)S(1)} %all_to_all.15.meta_ref, f32[32,64,256]{2,1,0:T(8,128)S(1)} %get-tuple-element.7.own_ref, f32[32,64,256]{2,1,0:T(8,128)S(1)} %collective-permute-done.other_ref), custom_call_target="tpu_custom_call" | custom-call | flops 805306368 | bytes 5242880 | tf_op jit(solution)/shard_map/mix/pallas_call | solution.py:137
  24.2 0.1 slice_bitcast_fusion
  24.3 1.6 %collective-permute-start.1 = (f32[4,2,4,8,256]{4,3,2,1,0:T(8,128)S(1)}, f32[4,2,4,8,256]{4,3,2,1,0:T(8,128)S(1)}, u32[]{:S(2)}, u32[]{:S(2)}) collective-permute-start(f32[4,2,4,8,256]{4,3,2,1,0:T(8,128)S(1)} %get-tuple-element.11), channel_id=1, source_target_pairs={{0,4},{1,129},{2,6},{3,131},{4,0},{5,133},{6,2},{7,135},{8,12},{9,... | collective-permute-start | bytes 786440 | tf_op jit(solution)/shard_map/ppermute | solution.py:164
  25.9 1.4 %collective-permute-start.2 = (f32[4,2,4,8,256]{4,3,2,1,0:T(8,128)S(1)}, f32[4,2,4,8,256]{4,3,2,1,0:T(8,128)S(1)}, u32[]{:S(2)}, u32[]{:S(2)}) collective-permute-start(f32[4,2,4,8,256]{4,3,2,1,0:T(8,128)S(1)} %get-tuple-element.10), channel_id=1, source_target_pairs={{0,2},{1,65},{2,4},{3,67},{4,6},{5,69},{6,0},{7,71},{8,10},{9,73},... | collective-permute-start | bytes 786440 | tf_op jit(solution)/shard_map/ppermute | solution.py:164
  27.3 0.6 collective-permute-start.3
  27.9 4.5 %collective-permute-done.1 = f32[4,2,4,8,256]{4,3,2,1,0:T(8,128)S(1)} collective-permute-done((f32[4,2,4,8,256]{4,3,2,1,0:T(8,128)S(1)}, f32[4,2,4,8,256]{4,3,2,1,0:T(8,128)S(1)}, u32[]{:S(2)}, u32[]{:S(2)}) %collective-permute-start.1) | collective-permute-done | bytes 262176 | tf_op jit(solution)/shard_map/ppermute | solution.py:164
  32.4 1.8 %collective-permute-done.2 = f32[4,2,4,8,256]{4,3,2,1,0:T(8,128)S(1)} collective-permute-done((f32[4,2,4,8,256]{4,3,2,1,0:T(8,128)S(1)}, f32[4,2,4,8,256]{4,3,2,1,0:T(8,128)S(1)}, u32[]{:S(2)}, u32[]{:S(2)}) %collective-permute-start.2) | collective-permute-done | bytes 262176 | tf_op jit(solution)/shard_map/ppermute | solution.py:164
  34.2 0.9 %collective-permute-done.3 = f32[4,2,4,8,256]{4,3,2,1,0:T(8,128)S(1)} collective-permute-done((f32[4,2,4,8,256]{4,3,2,1,0:T(8,128)S(1)}, f32[4,2,4,8,256]{4,3,2,1,0:T(8,128)S(1)}, u32[]{:S(2)}, u32[]{:S(2)}) %collective-permute-start.3) | collective-permute-done | bytes 262176 | tf_op jit(solution)/shard_map/ppermute | solution.py:164
  35.1 0.1 fusion.1
  35.1 15.8 %all_to_all.16 = f32[32,8,256]{2,1,0:T(8,128)S(1)} all-to-all(f32[32,8,256]{2,1,0:T(8,128)S(1)} %bitcast.20), channel_id=1, replica_groups={{0,8,16,24,32,40,48,56,64,72,80,88,96,104,112,120,128,136,144,152,160,1..., dimensions={0} | all-to-all | bytes 524288 | tf_op jit(solution)/shard_map/all_to_all | solution.py:201
  51.0 10.3 %all_to_all.17 = f32[8,8,256]{2,1,0:T(8,128)S(1)} all-to-all(f32[8,8,256]{2,1,0:T(8,128)S(1)} %broadcast_in_dim.5), channel_id=1, replica_groups=mesh['grp'=8,'row'=32] {'grp'}, dimensions={0} | all-to-all | bytes 131072 | tf_op jit(solution)/shard_map/all_to_all | solution.py:203
  61.2 0.6 %copy.6 = f32[64,256]{1,0:T(8,128)} copy(f32[64,256]{1,0:T(8,128)S(1)} %bitcast.21) | data formatting | bytes 131072
  (4 shorter events, 0.1 us)
Async XLA Ops:
  0.0 2.8 %copy-start = (s32[32]{0:T(128)S(1)}, s32[32]{0:T(128)}, u32[]{:S(2)}) copy-start(s32[32]{0:T(128)} %param.7) | copy-start | bytes 388
  0.0 2.8 %copy-start.1 = (s32[32]{0:T(128)S(1)}, s32[32]{0:T(128)}, u32[]{:S(2)}) copy-start(s32[32]{0:T(128)} %param.6) | copy-start | bytes 388
  2.7 20.3 %collective-permute-start = (f32[32,64,256]{2,1,0:T(8,128)S(1)}, f32[32,64,256]{2,1,0:T(8,128)S(1)}, u32[]{:S(2)}, u32[]{:S(2)}) collective-permute-start(f32[32,64,256]{2,1,0:T(8,128)S(1)} %get-tuple-element.8), channel_id=1, source_target_pairs={{0,1},{1,0},{2,3},{3,2},{4,5},{5,4},{6,7},{7,6},{8,9},{9,8},{10,11... | collective-permute-start | bytes 6291464 | tf_op jit(solution)/shard_map/ppermute | solution.py:195
  24.3 8.1 %collective-permute-start.1 = (f32[4,2,4,8,256]{4,3,2,1,0:T(8,128)S(1)}, f32[4,2,4,8,256]{4,3,2,1,0:T(8,128)S(1)}, u32[]{:S(2)}, u32[]{:S(2)}) collective-permute-start(f32[4,2,4,8,256]{4,3,2,1,0:T(8,128)S(1)} %get-tuple-element.11), channel_id=1, source_target_pairs={{0,4},{1,129},{2,6},{3,131},{4,0},{5,133},{6,2},{7,135},{8,12},{9,... | collective-permute-start | bytes 786440 | tf_op jit(solution)/shard_map/ppermute | solution.py:164
  25.9 8.3 %collective-permute-start.2 = (f32[4,2,4,8,256]{4,3,2,1,0:T(8,128)S(1)}, f32[4,2,4,8,256]{4,3,2,1,0:T(8,128)S(1)}, u32[]{:S(2)}, u32[]{:S(2)}) collective-permute-start(f32[4,2,4,8,256]{4,3,2,1,0:T(8,128)S(1)} %get-tuple-element.10), channel_id=1, source_target_pairs={{0,2},{1,65},{2,4},{3,67},{4,6},{5,69},{6,0},{7,71},{8,10},{9,73},... | collective-permute-start | bytes 786440 | tf_op jit(solution)/shard_map/ppermute | solution.py:164
  27.3 7.7 %collective-permute-start.3 = (f32[4,2,4,8,256]{4,3,2,1,0:T(8,128)S(1)}, f32[4,2,4,8,256]{4,3,2,1,0:T(8,128)S(1)}, u32[]{:S(2)}, u32[]{:S(2)}) collective-permute-start(f32[4,2,4,8,256]{4,3,2,1,0:T(8,128)S(1)} %get-tuple-element.9), channel_id=1, source_target_pairs={{0,6},{1,193},{2,0},{3,195},{4,2},{5,197},{6,4},{7,199},{8,14},{9,... | collective-permute-start | bytes 786440 | tf_op jit(solution)/shard_map/ppermute | solution.py:164

commit v11 on v5

v11 whole, which is shorter than its diff:
```python
import functools
import itertools
import math

import jax
import jax.numpy as jnp
from jax import lax
from jax.experimental import pallas as pl
from jax.experimental.pallas import tpu as pltpu
from jax.sharding import PartitionSpec as P

SKETCH = 2048
MIB = 1 << 20
AXES = ("grp", "row")


def parity(bits):
    for shift in (8, 4, 2, 1):
        bits = bits ^ bits >> shift
    return bits & 1


def hadamard_sign(rows, cols):
    return (1 - 2 * parity(rows & cols)).astype(jnp.float32)


def two_parts(value):
    high = value.astype(jnp.bfloat16)
    low = (value - high.astype(jnp.float32)).astype(jnp.bfloat16)
    return high, low


def mix_kernel(
    scale, place_ref, meta_ref, matrix_hbm, signs_hbm, other_hbm, other_signs_ref, out_ref, rows_ref, factor_ref, signs_ref, sems, signs_sem
):
    near, _, low_count, far, rows, cols = out_ref.shape
    sources, _, units = meta_ref.shape
    half = rows_ref.shape[2]
    targets = near * far
    me = place_ref[0] % sources
    core = me & 1
    first_row = pl.multiple_of(core * half, half)
    signs_copy = pltpu.make_async_copy(signs_hbm, signs_ref, signs_sem)
    signs_copy.start()
    first_x = jnp.where(core == 0, me >> 1, 0)
    first_y = jnp.where(core == 0, 0, place_ref[0] // sources // low_count)
    copies = []
    for step in range(near):
        first = pl.multiple_of((first_y + step) % near * low_count * rows, low_count * rows)
        for turn, ref in enumerate((matrix_hbm, other_hbm)):
            copies.append(
                pltpu.make_async_copy(
                    ref.at[:, pl.ds(pl.multiple_of(first_row + first, low_count * rows), low_count * rows), :],
                    rows_ref.at[turn, :, pl.ds(first, low_count * rows), :],
                    sems.at[step, turn],
                )
            )
            copies[-1].start()
    index = lax.broadcasted_iota(jnp.int32, (targets, units), 0)
    target = index % far * near + (index // far + first_x) % near
    sums = [jnp.zeros((targets, units), jnp.float32) for _ in range(2)]
    for source in range(sources):
        flip = 1 - 2 * parity((me >> 1) & (source >> 1))
        dests = meta_ref[source, 0:1, :]
        signs = meta_ref[source, 1:2, :] * flip
        routed = jnp.where(dests == target, signs.astype(jnp.float32), 0.0)
        sums[source & 1] = sums[source & 1] + routed
    side = (1 - 2 * core).astype(jnp.float32)
    tall, wide = targets * rows, units * rows
    unit_row = lax.broadcasted_iota(jnp.int32, (units, wide), 0)
    unit_col = lax.broadcasted_iota(jnp.int32, (units, wide), 1) // rows
    spread = (hadamard_sign(unit_row, unit_col) * scale).astype(jnp.bfloat16)
    repeat = (unit_row == unit_col).astype(jnp.bfloat16)
    keep = lax.broadcasted_iota(jnp.int32, (tall, wide), 0) % rows == lax.broadcasted_iota(jnp.int32, (tall, wide), 1) % rows
    signs_copy.wait()
    highs, lows = [], []
    for turn, (total, ref) in enumerate(
        ((sums[0] + side * sums[1], signs_ref), (sums[0] - side * sums[1], other_signs_ref))
    ):
        total = jnp.broadcast_to(total[:, None, :], (targets, rows, units)).reshape(tall, units)
        weights = jnp.dot(total.astype(jnp.bfloat16), spread, preferred_element_type=jnp.float32)
        high, low = two_parts(jnp.where(keep, weights, 0.0))
        highs.append(high)
        lows.append(low)
        factor_ref[:, pl.ds(turn * wide, wide)] = lax.dot_general(
            ref[...].astype(jnp.float32).astype(jnp.bfloat16),
            repeat,
            (((0,), (0,)), ((), ())),
            preferred_element_type=jnp.float32,
        )
    stacked = jnp.concatenate([jnp.concatenate(highs, axis=1), jnp.concatenate(lows, axis=1)], axis=0)
    for step, low_z in itertools.product(range(near), range(low_count)):
        if low_z == 0 and step % 2 == 0:
            for copy in copies[2 * step : 2 * step + 4]:
                copy.wait()
        piece = (first_y + step) % near * low_count + low_z
        span = pl.ds(pl.multiple_of(piece * rows, rows), rows)
        far_span = pl.ds(pl.multiple_of(first_row + piece * rows, rows), rows)
        factor = factor_ref[far_span, :]
        factor = jnp.concatenate([factor, factor], axis=0).astype(jnp.bfloat16)
        left = (stacked.reshape(tall // rows, 2 * rows, 2 * wide) * factor[None]).reshape(2 * tall, 2 * wide)
        parts = [two_parts(rows_ref[turn, :, span, :].reshape(wide, cols)) for turn in range(2)]
        high, low = (jnp.concatenate(each, axis=0) for each in zip(*parts))
        both = jnp.dot(left, high, preferred_element_type=jnp.float32)
        result = jnp.dot(left[:tall], low, preferred_element_type=jnp.float32) + (both[:tall] + both[tall:])
        result = result.reshape(near, far, rows, cols)
        for turn in range(near):
            out_ref[jnp.where(core == 0, turn, step), jnp.where(core == 0, step, turn), low_z] = result[turn]


def mix(scale, place, meta, matrix, signs, other, other_signs, near, low_count, far):
    units, block, cols = matrix.shape
    half = block // 2
    rows = half // (near * low_count)
    hbm = pl.BlockSpec(memory_space=pltpu.HBM)
    vmem = pl.BlockSpec(memory_space=pltpu.VMEM)
    return pl.pallas_call(
        functools.partial(mix_kernel, scale),
        in_specs=[pl.BlockSpec(memory_space=pltpu.SMEM), vmem, hbm, hbm, hbm, vmem],
        out_specs=vmem,
        out_shape=jax.ShapeDtypeStruct((near, near, low_count, far, rows, cols), jnp.float32),
        scratch_shapes=[
            pltpu.VMEM((2, units, half, cols), jnp.float32),
            pltpu.VMEM((block, 2 * units * rows), jnp.float32),
            pltpu.VMEM(signs.shape, jnp.int32),
            pltpu.SemaphoreType.DMA((near, 2)),
            pltpu.SemaphoreType.DMA,
        ],
        compiler_params=pltpu.CompilerParams(vmem_limit_bytes=24 * MIB),
        cost_estimate=pl.CostEstimate(flops=2 * 3 * 128 * 512 * 256 * 8, bytes_accessed=5 * MIB, transcendentals=0),
        name="mix",
    )(place, meta, *(pltpu.with_memory_space_constraint(value, pltpu.HBM) for value in (matrix, signs, other)), other_signs)


def finish_kernel(place_ref, mixed_ref, out_ref):
    block = mixed_ref.shape[0]
    half = block // 2
    row = lax.broadcasted_iota(jnp.int32, (half, block), 0) + (place_ref[0] & 1) * half
    hadamard = hadamard_sign(row, lax.broadcasted_iota(jnp.int32, (half, block), 1)).astype(jnp.bfloat16)
    value = mixed_ref[...]
    high = value.astype(jnp.bfloat16)
    middle, low = two_parts(value - high.astype(jnp.float32))
    out_ref[...] = jnp.dot(
        jnp.concatenate([hadamard] * 3, axis=1),
        jnp.concatenate([high, middle, low], axis=0),
        preferred_element_type=jnp.float32,
    )


def finish(place, mixed):
    vmem = pl.BlockSpec(memory_space=pltpu.VMEM)
    return pl.pallas_call(
        finish_kernel,
        in_specs=[pl.BlockSpec(memory_space=pltpu.SMEM), vmem],
        out_specs=vmem,
        out_shape=jax.ShapeDtypeStruct((mixed.shape[0] // 2, mixed.shape[1]), jnp.float32),
        compiler_params=pltpu.CompilerParams(vmem_limit_bytes=8 * MIB),
        name="finish",
    )(place, mixed)


Y, Z_LOW, Z_HIGH, X, CORE = 4, 2, 4, 4, 2


def flat_index(y, z_low, z_high, x, core):
    return (((y % Y * Z_LOW + z_low) * Z_HIGH + z_high) * X + x % X) * CORE + core


def places():
    return itertools.product(range(Y), range(Z_LOW), range(Z_HIGH), range(X), range(CORE))


def first_shift(value, step):
    pairs = []
    for y, z_low, z_high, x, core in places():
        to = (y, z_low, z_high, x + step, core) if core == 0 else (y + step, z_low, z_high, x, core)
        pairs.append((flat_index(y, z_low, z_high, x, core), flat_index(*to)))
    return lax.ppermute(value, AXES, pairs)


def second_groups():
    groups = []
    for core, fixed in itertools.product(range(CORE), range(X)):
        members = itertools.product(range(Y), range(Z_LOW), range(Z_HIGH))
        groups.append(
            [
                flat_index(free, z_low, z_high, fixed, core) if core == 0 else flat_index(fixed, z_low, z_high, free, core)
                for free, z_low, z_high in members
            ]
        )
    return groups


def last_groups():
    return [
        [flat_index(y, z_low, z_high, x, core) for core in range(CORE) for y in range(Y) for z_low in range(Z_LOW)]
        for z_high in range(Z_HIGH)
        for x in range(X)
    ]


def body(matrix, row_signs, block_dest, block_signs):
    row_count, col_count = matrix.shape
    units = block_dest.shape[0]
    block = row_count // units
    groups = lax.axis_size("grp")
    devs = lax.axis_size("row")
    total_rows = row_count * devs * groups
    scale = math.sqrt(SKETCH / total_rows) / math.sqrt(row_count * devs)
    place = lax.axis_index(AXES).astype(jnp.int32).reshape(1)

    mine, place = lax.optimization_barrier((jnp.stack([block_dest, block_signs]), place))
    meta = lax.all_to_all(jnp.broadcast_to(mine[None], (devs, 2, units)), "row", 0, 0)
    matrix = matrix.reshape(units, block, col_count)
    row_signs = row_signs.reshape(units, block)
    other, other_signs = (lax.ppermute(value, "row", [(i, i ^ 1) for i in range(devs)]) for value in (matrix, row_signs))
    parts = mix(scale, place, meta, matrix, row_signs, other, other_signs, X, Z_LOW, Z_HIGH)

    got = {step: first_shift(parts[step], step) for step in (2, 1, 3)}
    part = (parts[0] + got[2]) + (got[1] + got[3])
    pieces = part.reshape(-1, 8, col_count)
    pieces = lax.all_to_all(pieces, AXES, 0, 0, axis_index_groups=second_groups())
    share = jnp.sum(pieces, axis=0)
    full = jnp.broadcast_to(share[None], (CORE * groups, *share.shape))
    full = lax.all_to_all(full, AXES, 0, 0, axis_index_groups=last_groups())
    return finish(place, full.reshape(block, col_count))


def solution(mesh):
    return jax.shard_map(
        body,
        mesh=mesh,
        in_specs=(P(AXES, None), P(AXES), P(AXES), P(AXES)),
        out_specs=P("row", None),
        check_vma=False,
    )
```

time: 64 us -> 65.4 us (1.022)
  the two profiles are of different devices: /device:TPU:2 before, /device:TPU:1 now
where the time goes in v11:
time: 65.4 us; the launch traced here: 65.2 us
  blocking collectives  44.8 us (69%)
  starting transfers between devices  7.71 us (12%)
  waiting for transfers between devices  7.52 us (11%)
  Pallas kernels  4.21 us (6%)
  other arithmetic  0.79 us (1%)
    all_to_all x1, blocking collectives, body(): lax.all_to_all(jnp.broadcast_to(mine[None], (devs, 2, units)), 'row', 0, 0)  19.3 us
    all_to_all x1, blocking collectives, body(): lax.all_to_all(pieces, AXES, 0, 0, axis_index_groups=second_groups())  13.4 us
    all_to_all x1, blocking collectives, body(): full = lax.all_to_all(full, AXES, 0, 0, axis_index_groups=last_groups())  12.1 us
    ppermute x3, waiting for transfers between devices, first_shift(): return lax.ppermute(value, AXES, pairs)  7.51 us
    ppermute x3, starting transfers between devices, first_shift(): return lax.ppermute(value, AXES, pairs)  4.47 us
    pallas_call x1, Pallas kernels, mix(): pl.pallas_call(functools.partial(mix_kernel, scale), in_specs=[pl.BlockSp...  3.4 us
    ppermute x2, starting transfers between devices, body(): lax.ppermute(value, 'row', [(i, i ^ 1) for i in range(devs)])  3.24 us
  transfers between devices with their start and end apart: 5, of which 2 were waited for; matrix products, arithmetic and copies ran while one was open for 1% of the time, Pallas kernels for 0%

profile of v11, /device:TPU:1, one launch (start us, length us, event | category | flops | bytes accessed | tf_op | source)
XLA Modules:
  0.0 65.2 jit_solution(18340518115697263000)
XLA Ops:
  0.0 3.2 %collective-permute-start = (f32[32,128,256]{2,1,0:T(8,128)}, f32[32,128,256]{2,1,0:T(8,128)}, u32[]{:S(2)}, u32[]{:S(2)}) collective-permute-start(f32[32,128,256]{2,1,0:T(8,128)} %bitcast.20), channel_id=1, source_target_pairs={{0,1},{1,0},{2,3},{3,2},{4,5},{5,4},{6,7},{7,6},{8,9},{9,8},{10,11... | collective-permute-start | bytes 12582920 | tf_op jit(solution)/shard_map/ppermute | solution.py:216
  3.2 0.0 collective-permute-start.1
  3.2 0.7 %pad_add_fusion = s32[2,32]{1,0:T(2,128)S(1)} fusion(s32[1,32]{1,0:T(1,128)} %bitcast.25, s32[1,32]{1,0:T(1,128)} %bitcast.26), kind=kLoop, calls=%fused_computation.6 | loop fusion | flops 64 | bytes 512 | tf_op jit(solution)/shard_map/stack | solution.py:212
  3.9 19.3 %all_to_all.15.meta_ref = s32[32,2,32]{2,1,0:T(2,128)S(1)} all-to-all(s32[32,2,32]{2,1,0:T(2,128)S(1)} %broadcast_in_dim.4), channel_id=1, replica_groups=mesh['grp'=8,'row'=32] {'row'}, dimensions={0} | all-to-all | bytes 16384 | tf_op jit(solution)/shard_map/all_to_all | solution.py:213
  23.3 0.0 collective-permute-done.1.other_signs_ref
  23.3 0.0 collective-permute-done.other_hbm
  23.3 3.4 %mix.1 = f32[4,4,2,4,8,256]{5,4,3,2,1,0:T(8,128)S(1)} custom-call(s32[1]{0:T(128)} %bitcast.2.place_ref, s32[32,2,32]{2,1,0:T(2,128)S(1)} %all_to_all.15.meta_ref, f32[32,128,256]{2,1,0:T(8,128)} %bitcast.21, s32[32,128]{1,0:T(8,128)} %bitcast.24, f32[32,128,256]{2,1,0:T(8,128)} %collective-permute-done.other_hbm, ...), custom_call_target="tpu_custom_call" | custom-call | flops 805306368 | bytes 5242880 | tf_op jit(solution)/shard_map/mix/pallas_call | solution.py:117
  26.7 0.1 slice_bitcast_fusion
  26.8 2.7 %collective-permute-start.4 = (f32[4,2,4,8,256]{4,3,2,1,0:T(8,128)S(1)}, f32[4,2,4,8,256]{4,3,2,1,0:T(8,128)S(1)}, u32[]{:S(2)}, u32[]{:S(2)}) collective-permute-start(f32[4,2,4,8,256]{4,3,2,1,0:T(8,128)S(1)} %get-tuple-element.9), channel_id=1, source_target_pairs={{0,6},{1,193},{2,0},{3,195},{4,2},{5,197},{6,4},{7,199},{8,14},{9,... | collective-permute-start | bytes 786440 | tf_op jit(solution)/shard_map/ppermute | solution.py:178
  29.5 0.0 collective-permute-start.3
  29.5 1.7 %collective-permute-start.2 = (f32[4,2,4,8,256]{4,3,2,1,0:T(8,128)S(1)}, f32[4,2,4,8,256]{4,3,2,1,0:T(8,128)S(1)}, u32[]{:S(2)}, u32[]{:S(2)}) collective-permute-start(f32[4,2,4,8,256]{4,3,2,1,0:T(8,128)S(1)} %get-tuple-element.11), channel_id=1, source_target_pairs={{0,4},{1,129},{2,6},{3,131},{4,0},{5,133},{6,2},{7,135},{8,12},{9,... | collective-permute-start | bytes 786440 | tf_op jit(solution)/shard_map/ppermute | solution.py:178
  31.2 1.6 %collective-permute-done.4 = f32[4,2,4,8,256]{4,3,2,1,0:T(8,128)S(1)} collective-permute-done((f32[4,2,4,8,256]{4,3,2,1,0:T(8,128)S(1)}, f32[4,2,4,8,256]{4,3,2,1,0:T(8,128)S(1)}, u32[]{:S(2)}, u32[]{:S(2)}) %collective-permute-start.4) | collective-permute-done | bytes 262176 | tf_op jit(solution)/shard_map/ppermute | solution.py:178
  32.8 5.9 %collective-permute-done.3 = f32[4,2,4,8,256]{4,3,2,1,0:T(8,128)S(1)} collective-permute-done((f32[4,2,4,8,256]{4,3,2,1,0:T(8,128)S(1)}, f32[4,2,4,8,256]{4,3,2,1,0:T(8,128)S(1)}, u32[]{:S(2)}, u32[]{:S(2)}) %collective-permute-start.3) | collective-permute-done | bytes 262176 | tf_op jit(solution)/shard_map/ppermute | solution.py:178
  38.8 0.0 collective-permute-done.2
  38.8 0.1 fusion.1
  38.8 13.4 %all_to_all.16 = f32[32,8,256]{2,1,0:T(8,128)S(1)} all-to-all(f32[32,8,256]{2,1,0:T(8,128)S(1)} %bitcast.22), channel_id=1, replica_groups={{0,8,16,24,32,40,48,56,64,72,80,88,96,104,112,120,128,136,144,152,160,1..., dimensions={0} | all-to-all | bytes 524288 | tf_op jit(solution)/shard_map/all_to_all | solution.py:222
  52.3 12.1 %all_to_all.17 = f32[16,8,256]{2,1,0:T(8,128)S(1)} all-to-all(f32[16,8,256]{2,1,0:T(8,128)S(1)} %broadcast_in_dim.5), channel_id=1, replica_groups={{0,32,64,96,128,160,192,224,1,33,65,97,129,161,193,225},{2,34,66,98,130..., dimensions={0} | all-to-all | bytes 262144 | tf_op jit(solution)/shard_map/all_to_all | solution.py:225
  64.4 0.8 %finish.1 = f32[64,256]{1,0:T(8,128)} custom-call(s32[1]{0:T(128)} %bitcast.2.place_ref, f32[128,256]{1,0:T(8,128)S(1)} %bitcast.19), custom_call_target="tpu_custom_call" | custom-call | tf_op jit(solution)/shard_map/finish/pallas_call | solution.py:152
  (3 shorter events, 0.1 us)
Async XLA Ops:
  0.0 23.3 %collective-permute-start = (f32[32,128,256]{2,1,0:T(8,128)}, f32[32,128,256]{2,1,0:T(8,128)}, u32[]{:S(2)}, u32[]{:S(2)}) collective-permute-start(f32[32,128,256]{2,1,0:T(8,128)} %bitcast.20), channel_id=1, source_target_pairs={{0,1},{1,0},{2,3},{3,2},{4,5},{5,4},{6,7},{7,6},{8,9},{9,8},{10,11... | collective-permute-start | bytes 12582920 | tf_op jit(solution)/shard_map/ppermute | solution.py:216
  3.2 20.0 %collective-permute-start.1 = (s32[32,128]{1,0:T(8,128)}, s32[32,128]{1,0:T(8,128)S(1)}, u32[]{:S(2)}, u32[]{:S(2)}) collective-permute-start(s32[32,128]{1,0:T(8,128)} %bitcast.23), channel_id=1, source_target_pairs={{0,1},{1,0},{2,3},{3,2},{4,5},{5,4},{6,7},{7,6},{8,9},{9,8},{10,11... | collective-permute-start | bytes 49160 | tf_op jit(solution)/shard_map/ppermute | solution.py:216
  26.8 6.1 %collective-permute-start.4 = (f32[4,2,4,8,256]{4,3,2,1,0:T(8,128)S(1)}, f32[4,2,4,8,256]{4,3,2,1,0:T(8,128)S(1)}, u32[]{:S(2)}, u32[]{:S(2)}) collective-permute-start(f32[4,2,4,8,256]{4,3,2,1,0:T(8,128)S(1)} %get-tuple-element.9), channel_id=1, source_target_pairs={{0,6},{1,193},{2,0},{3,195},{4,2},{5,197},{6,4},{7,199},{8,14},{9,... | collective-permute-start | bytes 786440 | tf_op jit(solution)/shard_map/ppermute | solution.py:178
  29.5 9.2 %collective-permute-start.3 = (f32[4,2,4,8,256]{4,3,2,1,0:T(8,128)S(1)}, f32[4,2,4,8,256]{4,3,2,1,0:T(8,128)S(1)}, u32[]{:S(2)}, u32[]{:S(2)}) collective-permute-start(f32[4,2,4,8,256]{4,3,2,1,0:T(8,128)S(1)} %get-tuple-element.10), channel_id=1, source_target_pairs={{0,2},{1,65},{2,4},{3,67},{4,6},{5,69},{6,0},{7,71},{8,10},{9,73},... | collective-permute-start | bytes 786440 | tf_op jit(solution)/shard_map/ppermute | solution.py:178
  29.5 9.2 %collective-permute-start.2 = (f32[4,2,4,8,256]{4,3,2,1,0:T(8,128)S(1)}, f32[4,2,4,8,256]{4,3,2,1,0:T(8,128)S(1)}, u32[]{:S(2)}, u32[]{:S(2)}) collective-permute-start(f32[4,2,4,8,256]{4,3,2,1,0:T(8,128)S(1)} %get-tuple-element.11), channel_id=1, source_target_pairs={{0,4},{1,129},{2,6},{3,131},{4,0},{5,133},{6,2},{7,135},{8,12},{9,... | collective-permute-start | bytes 786440 | tf_op jit(solution)/shard_map/ppermute | solution.py:178

commit v12 on v10

--- a/solution.py
+++ b/solution.py
@@ -11,6 +11,7 @@
 
 SKETCH = 2048
 MIB = 1 << 20
+LANES = 128
 AXES = ("grp", "row")
 
 
@@ -88,7 +89,9 @@
 
 def mix_kernel(scale, place_ref, meta_ref, own_ref, other_ref, out_ref):
     near, _, low_count, far, rows, cols = out_ref.shape
-    sources, _, units = meta_ref.shape
+    chips = meta_ref.shape[0]
+    units = own_ref.shape[0]
+    sources = 2 * chips
     targets = near * far
     me = place_ref[0] % sources
     core = me & 1
@@ -96,13 +99,12 @@
     first_y = jnp.where(core == 0, 0, place_ref[0] // sources // low_count)
     index = lax.broadcasted_iota(jnp.int32, (targets, units), 0)
     target = index % far * near + (index // far + first_x) % near
-    sums = [jnp.zeros((targets, units), jnp.float32) for _ in range(2)]
-    for source in range(sources):
-        flip = 1 - 2 * parity((me >> 1) & (source >> 1))
-        dests = meta_ref[source, 0:1, :]
-        signs = meta_ref[source, 1:2, :] * flip
-        routed = jnp.where(dests == target, signs.astype(jnp.float32), 0.0)
-        sums[source & 1] = sums[source & 1] + routed
+    same, different = (jnp.zeros((targets, units), jnp.float32) for _ in range(2))
+    for source in range(chips):
+        flip = 1 - 2 * parity((me >> 1) & source)
+        dests, signs, other_dests, other_signs = (meta_ref[source, row : row + 1, :units] for row in range(4))
+        same = same + jnp.where(dests == target, (signs * flip).astype(jnp.float32), 0.0)
+        different = different + jnp.where(other_dests == target, (other_signs * flip).astype(jnp.float32), 0.0)
     side = (1 - 2 * core).astype(jnp.float32)
     tall, wide = targets * rows, units * rows
     unit_row = lax.broadcasted_iota(jnp.int32, (units, wide), 0)
@@ -110,7 +112,7 @@
     spread = (hadamard_sign(unit_row, unit_col // rows) * scale).astype(jnp.bfloat16)
     keep = lax.broadcasted_iota(jnp.int32, (tall, wide), 0) % rows == lax.broadcasted_iota(jnp.int32, (tall, wide), 1) % rows
     highs, lows = [], []
-    for total in (sums[0] + side * sums[1], sums[0] - side * sums[1]):
+    for total in (side * same + different, same - side * different):
         total = jnp.broadcast_to(total[:, None, :], (targets, rows, units)).reshape(tall, units)
         weights = jnp.dot(total.astype(jnp.bfloat16), spread, preferred_element_type=jnp.float32)
         high, low = two_parts(jnp.where(keep, weights, 0.0))
@@ -187,12 +189,17 @@
     scale = math.sqrt(SKETCH / total_rows) / math.sqrt(row_count * devs)
     place = lax.axis_index(AXES).astype(jnp.int32).reshape(1)
 
+    cores = [(i, i ^ 1) for i in range(devs)]
     mine = jnp.stack([block_dest, block_signs])
-    meta = lax.all_to_all(jnp.broadcast_to(mine[None], (devs, 2, units)), "row", 0, 0)
+    mine = jnp.concatenate([mine, lax.ppermute(mine, "row", cores)])
+    mine = jnp.pad(mine, ((0, 0), (0, LANES - units)))
+    same_core = [list(range(core, devs, CORE)) for core in range(CORE)]
     matrix = matrix.reshape(units, block, col_count)
-    row_signs = row_signs.reshape(units, block)
-    own, send = transform(place, matrix, row_signs)
-    other = lax.ppermute(send, "row", [(i, i ^ 1) for i in range(devs)])
+    own, send = transform(place, matrix, row_signs.reshape(units, block))
+    send, mine = lax.optimization_barrier((send, mine))
+    other = lax.ppermute(send, "row", cores)
+    meta = jnp.broadcast_to(mine[None], (devs // CORE, *mine.shape))
+    meta = lax.all_to_all(meta, "row", 0, 0, axis_index_groups=same_core)
     parts = mix(scale, place, meta, own, other, X, Z_LOW, Z_HIGH)
 
     got = {step: first_shift(parts[step], step) for step in (2, 1, 3)}

time: 62.1 us -> 63.1 us (1.016)
  other arithmetic: 0.12 us -> 0.8 us
    another operation x1, other arithmetic: 0.01 us -> 0.68 us  [body(): mine = jnp.stack([block_dest, block_signs])]
  transfers between devices with their start and end apart: 4 -> 5, of which waited for: 3 -> 3; matrix products, arithmetic and copies ran while one was open for 0% -> 0% of each run, Pallas kernels for 0% -> 4%
where the time goes in v12:
time: 63.1 us; the launch traced here: 62.9 us
  blocking collectives  46 us (73%)
  waiting for transfers between devices  7.16 us (11%)
  starting transfers between devices  4.19 us (7%)
  Pallas kernels  3.94 us (6%)
  other arithmetic  0.8 us (1%)
  local copies, waits for them, and re-layouts  0.72 us (1%)
    all_to_all x1, blocking collectives, body(): meta = lax.all_to_all(meta, 'row', 0, 0, axis_index_groups=same_core)  19.9 us
    all_to_all x1, blocking collectives, body(): lax.all_to_all(pieces, AXES, 0, 0, axis_index_groups=second_groups())  15.5 us
    all_to_all x1, blocking collectives, body(): lax.all_to_all(jnp.broadcast_to(share[None], (groups, 8, col_count)), 'gr...  10.5 us
    ppermute x3, waiting for transfers between devices, first_shift(): return lax.ppermute(value, AXES, pairs)  7.15 us
    ppermute x3, starting transfers between devices, first_shift(): return lax.ppermute(value, AXES, pairs)  3.62 us
    pallas_call x1, Pallas kernels, transform(): pl.pallas_call(functools.partial(transform_kernel, cuts), in_specs=[pl.Bl...  2.65 us
    pallas_call x1, Pallas kernels, mix(): pl.pallas_call(functools.partial(mix_kernel, scale), in_specs=[pl.BlockSp...  1.28 us
  transfers between devices with their start and end apart: 5, of which 3 were waited for; matrix products, arithmetic and copies ran while one was open for 0% of the time, Pallas kernels for 4%

profile of v12, /device:TPU:2, one launch (start us, length us, event | category | flops | bytes accessed | tf_op | source)
XLA Modules:
  0.0 62.9 jit_solution(11836269025591514918)
XLA Ops:
  0.0 0.7 %pad_add_fusion.1 = s32[2,32]{1,0:T(2,128)S(1)} fusion(s32[1,32]{1,0:T(1,128)} %bitcast.23, s32[1,32]{1,0:T(1,128)} %bitcast.25), kind=kLoop, calls=%fused_computation.7 | loop fusion | flops 64 | bytes 512 | tf_op jit(solution)/shard_map/stack | solution.py:193
  0.7 0.0 collective-permute-start
  0.7 0.0 copy-start
  0.7 0.0 copy-start.1
  0.7 2.7 %transform.1 = (f32[32,64,256]{2,1,0:T(8,128)S(1)}, f32[32,64,256]{2,1,0:T(8,128)S(1)}) custom-call(s32[1]{0:T(128)} %bitcast.place_ref, f32[32,128,256]{2,1,0:T(8,128)} %bitcast.19, s32[32,128]{1,0:T(8,128)} %bitcast.22), custom_call_target="tpu_custom_call" | custom-call | flops 536870912 | bytes 8388608 | tf_op jit(solution)/shard_map/transform/pallas_call | solution.py:69
  3.4 0.0 collective-permute-done
  3.4 0.0 copy-done
  3.4 0.0 copy-done.1
  3.4 0.6 collective-permute-start.1
  4.0 19.9 %all_to_all.15.meta_ref = s32[16,4,128]{2,1,0:T(4,128)S(1)} all-to-all(s32[16,4,128]{2,1,0:T(4,128)S(1)} %broadcast_in_dim.4), channel_id=1, replica_groups={{0,2,4,6,8,10,12,14,16,18,20,22,24,26,28,30},{1,3,5,7,9,11,13,15,17,19,..., dimensions={0} | all-to-all | bytes 65536 | tf_op jit(solution)/shard_map/all_to_all | solution.py:202
  23.9 0.0 collective-permute-done.1.other_ref
  24.0 1.3 %mix.1 = f32[4,4,2,4,8,256]{5,4,3,2,1,0:T(8,128)S(1)} custom-call(s32[1]{0:T(128)} %bitcast.place_ref, s32[16,4,128]{2,1,0:T(4,128)S(1)} %all_to_all.15.meta_ref, f32[32,64,256]{2,1,0:T(8,128)S(1)} %get-tuple-element.11.own_ref, f32[32,64,256]{2,1,0:T(8,128)S(1)} %collective-permute-done.1.other_ref), custom_call_target="tpu_custom_call" | custom-call | flops 805306368 | bytes 5242880 | tf_op jit(solution)/shard_map/mix/pallas_call | solution.py:139
  25.2 0.1 slice_bitcast_fusion
  25.3 1.6 %collective-permute-start.2 = (f32[4,2,4,8,256]{4,3,2,1,0:T(8,128)S(1)}, f32[4,2,4,8,256]{4,3,2,1,0:T(8,128)S(1)}, u32[]{:S(2)}, u32[]{:S(2)}) collective-permute-start(f32[4,2,4,8,256]{4,3,2,1,0:T(8,128)S(1)} %get-tuple-element.15), channel_id=1, source_target_pairs={{0,4},{1,129},{2,6},{3,131},{4,0},{5,133},{6,2},{7,135},{8,12},{9,... | collective-permute-start | bytes 786440 | tf_op jit(solution)/shard_map/ppermute | solution.py:166
  26.9 1.4 %collective-permute-start.3 = (f32[4,2,4,8,256]{4,3,2,1,0:T(8,128)S(1)}, f32[4,2,4,8,256]{4,3,2,1,0:T(8,128)S(1)}, u32[]{:S(2)}, u32[]{:S(2)}) collective-permute-start(f32[4,2,4,8,256]{4,3,2,1,0:T(8,128)S(1)} %get-tuple-element.14), channel_id=1, source_target_pairs={{0,2},{1,65},{2,4},{3,67},{4,6},{5,69},{6,0},{7,71},{8,10},{9,73},... | collective-permute-start | bytes 786440 | tf_op jit(solution)/shard_map/ppermute | solution.py:166
  28.3 0.6 collective-permute-start.4
  28.9 4.4 %collective-permute-done.2 = f32[4,2,4,8,256]{4,3,2,1,0:T(8,128)S(1)} collective-permute-done((f32[4,2,4,8,256]{4,3,2,1,0:T(8,128)S(1)}, f32[4,2,4,8,256]{4,3,2,1,0:T(8,128)S(1)}, u32[]{:S(2)}, u32[]{:S(2)}) %collective-permute-start.2) | collective-permute-done | bytes 262176 | tf_op jit(solution)/shard_map/ppermute | solution.py:166
  33.4 2.0 %collective-permute-done.3 = f32[4,2,4,8,256]{4,3,2,1,0:T(8,128)S(1)} collective-permute-done((f32[4,2,4,8,256]{4,3,2,1,0:T(8,128)S(1)}, f32[4,2,4,8,256]{4,3,2,1,0:T(8,128)S(1)}, u32[]{:S(2)}, u32[]{:S(2)}) %collective-permute-start.3) | collective-permute-done | bytes 262176 | tf_op jit(solution)/shard_map/ppermute | solution.py:166
  35.4 0.7 %collective-permute-done.4 = f32[4,2,4,8,256]{4,3,2,1,0:T(8,128)S(1)} collective-permute-done((f32[4,2,4,8,256]{4,3,2,1,0:T(8,128)S(1)}, f32[4,2,4,8,256]{4,3,2,1,0:T(8,128)S(1)}, u32[]{:S(2)}, u32[]{:S(2)}) %collective-permute-start.4) | collective-permute-done | bytes 262176 | tf_op jit(solution)/shard_map/ppermute | solution.py:166
  36.1 0.1 fusion.1
  36.2 15.5 %all_to_all.16 = f32[32,8,256]{2,1,0:T(8,128)S(1)} all-to-all(f32[32,8,256]{2,1,0:T(8,128)S(1)} %bitcast.20), channel_id=1, replica_groups={{0,8,16,24,32,40,48,56,64,72,80,88,96,104,112,120,128,136,144,152,160,1..., dimensions={0} | all-to-all | bytes 524288 | tf_op jit(solution)/shard_map/all_to_all | solution.py:208
  51.7 10.5 %all_to_all.17 = f32[8,8,256]{2,1,0:T(8,128)S(1)} all-to-all(f32[8,8,256]{2,1,0:T(8,128)S(1)} %broadcast_in_dim.5), channel_id=1, replica_groups=mesh['grp'=8,'row'=32] {'grp'}, dimensions={0} | all-to-all | bytes 131072 | tf_op jit(solution)/shard_map/all_to_all | solution.py:210
  62.2 0.6 %copy.6 = f32[64,256]{1,0:T(8,128)} copy(f32[64,256]{1,0:T(8,128)S(1)} %bitcast.21) | data formatting | bytes 131072
  (5 shorter events, 0.1 us)
Async XLA Ops:
  0.7 2.7 %collective-permute-start = (s32[2,32]{1,0:T(2,128)S(1)}, s32[2,32]{1,0:T(2,128)S(1)}, u32[]{:S(2)}, u32[]{:S(2)}) collective-permute-start(s32[2,32]{1,0:T(2,128)S(1)} %pad_add_fusion.1), channel_id=1, source_target_pairs={{0,1},{1,0},{2,3},{3,2},{4,5},{5,4},{6,7},{7,6},{8,9},{9,8},{10,11... | collective-permute-start | bytes 776 | tf_op jit(solution)/shard_map/ppermute | solution.py:194
  0.7 2.7 %copy-start = (s32[32]{0:T(128)S(1)}, s32[32]{0:T(128)}, u32[]{:S(2)}) copy-start(s32[32]{0:T(128)} %param.7) | copy-start | bytes 388
  0.7 2.7 %copy-start.1 = (s32[32]{0:T(128)S(1)}, s32[32]{0:T(128)}, u32[]{:S(2)}) copy-start(s32[32]{0:T(128)} %param.6) | copy-start | bytes 388
  3.4 20.5 %collective-permute-start.1 = (f32[32,64,256]{2,1,0:T(8,128)S(1)}, f32[32,64,256]{2,1,0:T(8,128)S(1)}, u32[]{:S(2)}, u32[]{:S(2)}) collective-permute-start(f32[32,64,256]{2,1,0:T(8,128)S(1)} %get-tuple-element.12), channel_id=1, source_target_pairs={{0,1},{1,0},{2,3},{3,2},{4,5},{5,4},{6,7},{7,6},{8,9},{9,8},{10,11... | collective-permute-start | bytes 6291464 | tf_op jit(solution)/shard_map/ppermute | solution.py:200
  25.3 8.1 %collective-permute-start.2 = (f32[4,2,4,8,256]{4,3,2,1,0:T(8,128)S(1)}, f32[4,2,4,8,256]{4,3,2,1,0:T(8,128)S(1)}, u32[]{:S(2)}, u32[]{:S(2)}) collective-permute-start(f32[4,2,4,8,256]{4,3,2,1,0:T(8,128)S(1)} %get-tuple-element.15), channel_id=1, source_target_pairs={{0,4},{1,129},{2,6},{3,131},{4,0},{5,133},{6,2},{7,135},{8,12},{9,... | collective-permute-start | bytes 786440 | tf_op jit(solution)/shard_map/ppermute | solution.py:166
  26.9 8.5 %collective-permute-start.3 = (f32[4,2,4,8,256]{4,3,2,1,0:T(8,128)S(1)}, f32[4,2,4,8,256]{4,3,2,1,0:T(8,128)S(1)}, u32[]{:S(2)}, u32[]{:S(2)}) collective-permute-start(f32[4,2,4,8,256]{4,3,2,1,0:T(8,128)S(1)} %get-tuple-element.14), channel_id=1, source_target_pairs={{0,2},{1,65},{2,4},{3,67},{4,6},{5,69},{6,0},{7,71},{8,10},{9,73},... | collective-permute-start | bytes 786440 | tf_op jit(solution)/shard_map/ppermute | solution.py:166
  28.3 7.8 %collective-permute-start.4 = (f32[4,2,4,8,256]{4,3,2,1,0:T(8,128)S(1)}, f32[4,2,4,8,256]{4,3,2,1,0:T(8,128)S(1)}, u32[]{:S(2)}, u32[]{:S(2)}) collective-permute-start(f32[4,2,4,8,256]{4,3,2,1,0:T(8,128)S(1)} %get-tuple-element.13), channel_id=1, source_target_pairs={{0,6},{1,193},{2,0},{3,195},{4,2},{5,197},{6,4},{7,199},{8,14},{9,... | collective-permute-start | bytes 786440 | tf_op jit(solution)/shard_map/ppermute | solution.py:166

commit v13 on v12

--- a/solution.py
+++ b/solution.py
@@ -190,9 +190,8 @@
     place = lax.axis_index(AXES).astype(jnp.int32).reshape(1)
 
     cores = [(i, i ^ 1) for i in range(devs)]
-    mine = jnp.stack([block_dest, block_signs])
-    mine = jnp.concatenate([mine, lax.ppermute(mine, "row", cores)])
-    mine = jnp.pad(mine, ((0, 0), (0, LANES - units)))
+    swapped = [lax.ppermute(value, "row", cores) for value in (block_dest, block_signs)]
+    mine = jnp.pad(jnp.stack([block_dest, block_signs, *swapped]), ((0, 0), (0, LANES - units)))
     same_core = [list(range(core, devs, CORE)) for core in range(CORE)]
     matrix = matrix.reshape(units, block, col_count)
     own, send = transform(place, matrix, row_signs.reshape(units, block))

time: 63.1 us -> 62.4 us (0.989)
  other arithmetic: 0.8 us -> 0.12 us
    another operation x1, other arithmetic: 0.68 us -> 0.01 us  [body(): jnp.stack([block_dest, block_signs, *swapped])]
  transfers between devices with their start and end apart: 5 -> 6, of which waited for: 3 -> 3; matrix products, arithmetic and copies ran while one was open for 0% -> 0% of each run, Pallas kernels for 4% -> 4%
where the time goes in v13:
time: 62.4 us; the launch traced here: 62.2 us
  blocking collectives  46 us (74%)
  waiting for transfers between devices  7.16 us (11%)
  starting transfers between devices  4.22 us (7%)
  Pallas kernels  3.94 us (6%)
  local copies, waits for them, and re-layouts  0.71 us (1%)
    all_to_all x1, blocking collectives, body(): meta = lax.all_to_all(meta, 'row', 0, 0, axis_index_groups=same_core)  19.9 us
    all_to_all x1, blocking collectives, body(): lax.all_to_all(pieces, AXES, 0, 0, axis_index_groups=second_groups())  15.5 us
    all_to_all x1, blocking collectives, body(): lax.all_to_all(jnp.broadcast_to(share[None], (groups, 8, col_count)), 'gr...  10.5 us
    ppermute x3, waiting for transfers between devices, first_shift(): return lax.ppermute(value, AXES, pairs)  7.15 us
    ppermute x3, starting transfers between devices, first_shift(): return lax.ppermute(value, AXES, pairs)  3.62 us
    pallas_call x1, Pallas kernels, transform(): pl.pallas_call(functools.partial(transform_kernel, cuts), in_specs=[pl.Bl...  2.66 us
    pallas_call x1, Pallas kernels, mix(): pl.pallas_call(functools.partial(mix_kernel, scale), in_specs=[pl.BlockSp...  1.28 us
  transfers between devices with their start and end apart: 6, of which 3 were waited for; matrix products, arithmetic and copies ran while one was open for 0% of the time, Pallas kernels for 4%

profile of v13, /device:TPU:2, one launch (start us, length us, event | category | flops | bytes accessed | tf_op | source)
XLA Modules:
  0.0 62.2 jit_solution(2289549116481901949)
XLA Ops:
  0.0 0.0 collective-permute-start
  0.0 0.5 collective-permute-start.1
  0.5 0.0 copy-start
  0.5 0.0 copy-start.1
  0.5 2.7 %transform.1 = (f32[32,64,256]{2,1,0:T(8,128)S(1)}, f32[32,64,256]{2,1,0:T(8,128)S(1)}) custom-call(s32[1]{0:T(128)} %bitcast.place_ref, f32[32,128,256]{2,1,0:T(8,128)} %bitcast.21, s32[32,128]{1,0:T(8,128)} %bitcast.24), custom_call_target="tpu_custom_call" | custom-call | flops 536870912 | bytes 8388608 | tf_op jit(solution)/shard_map/transform/pallas_call | solution.py:69
  3.2 0.0 collective-permute-done
  3.2 0.0 collective-permute-done.1
  3.2 0.0 copy-done
  3.2 0.0 copy-done.1
  3.3 0.1 collective-permute-start.2
  3.4 19.9 %all_to_all.15.meta_ref = s32[16,4,128]{2,1,0:T(4,128)S(1)} all-to-all(s32[16,4,128]{2,1,0:T(4,128)S(1)} %broadcast_in_dim.4), channel_id=1, replica_groups={{0,2,4,6,8,10,12,14,16,18,20,22,24,26,28,30},{1,3,5,7,9,11,13,15,17,19,..., dimensions={0} | all-to-all | bytes 65536 | tf_op jit(solution)/shard_map/all_to_all | solution.py:201
  23.3 0.0 collective-permute-done.2.other_ref
  23.3 1.3 %mix.1 = f32[4,4,2,4,8,256]{5,4,3,2,1,0:T(8,128)S(1)} custom-call(s32[1]{0:T(128)} %bitcast.place_ref, s32[16,4,128]{2,1,0:T(4,128)S(1)} %all_to_all.15.meta_ref, f32[32,64,256]{2,1,0:T(8,128)S(1)} %get-tuple-element.11.own_ref, f32[32,64,256]{2,1,0:T(8,128)S(1)} %collective-permute-done.2.other_ref), custom_call_target="tpu_custom_call" | custom-call | flops 805306368 | bytes 5242880 | tf_op jit(solution)/shard_map/mix/pallas_call | solution.py:139
  24.6 0.1 slice_bitcast_fusion
  24.7 1.6 %collective-permute-start.3 = (f32[4,2,4,8,256]{4,3,2,1,0:T(8,128)S(1)}, f32[4,2,4,8,256]{4,3,2,1,0:T(8,128)S(1)}, u32[]{:S(2)}, u32[]{:S(2)}) collective-permute-start(f32[4,2,4,8,256]{4,3,2,1,0:T(8,128)S(1)} %get-tuple-element.15), channel_id=1, source_target_pairs={{0,4},{1,129},{2,6},{3,131},{4,0},{5,133},{6,2},{7,135},{8,12},{9,... | collective-permute-start | bytes 786440 | tf_op jit(solution)/shard_map/ppermute | solution.py:166
  26.2 1.4 %collective-permute-start.4 = (f32[4,2,4,8,256]{4,3,2,1,0:T(8,128)S(1)}, f32[4,2,4,8,256]{4,3,2,1,0:T(8,128)S(1)}, u32[]{:S(2)}, u32[]{:S(2)}) collective-permute-start(f32[4,2,4,8,256]{4,3,2,1,0:T(8,128)S(1)} %get-tuple-element.14), channel_id=1, source_target_pairs={{0,2},{1,65},{2,4},{3,67},{4,6},{5,69},{6,0},{7,71},{8,10},{9,73},... | collective-permute-start | bytes 786440 | tf_op jit(solution)/shard_map/ppermute | solution.py:166
  27.7 0.6 collective-permute-start.5
  28.3 4.4 %collective-permute-done.3 = f32[4,2,4,8,256]{4,3,2,1,0:T(8,128)S(1)} collective-permute-done((f32[4,2,4,8,256]{4,3,2,1,0:T(8,128)S(1)}, f32[4,2,4,8,256]{4,3,2,1,0:T(8,128)S(1)}, u32[]{:S(2)}, u32[]{:S(2)}) %collective-permute-start.3) | collective-permute-done | bytes 262176 | tf_op jit(solution)/shard_map/ppermute | solution.py:166
  32.7 2.0 %collective-permute-done.4 = f32[4,2,4,8,256]{4,3,2,1,0:T(8,128)S(1)} collective-permute-done((f32[4,2,4,8,256]{4,3,2,1,0:T(8,128)S(1)}, f32[4,2,4,8,256]{4,3,2,1,0:T(8,128)S(1)}, u32[]{:S(2)}, u32[]{:S(2)}) %collective-permute-start.4) | collective-permute-done | bytes 262176 | tf_op jit(solution)/shard_map/ppermute | solution.py:166
  34.7 0.7 %collective-permute-done.5 = f32[4,2,4,8,256]{4,3,2,1,0:T(8,128)S(1)} collective-permute-done((f32[4,2,4,8,256]{4,3,2,1,0:T(8,128)S(1)}, f32[4,2,4,8,256]{4,3,2,1,0:T(8,128)S(1)}, u32[]{:S(2)}, u32[]{:S(2)}) %collective-permute-start.5) | collective-permute-done | bytes 262176 | tf_op jit(solution)/shard_map/ppermute | solution.py:166
  35.4 0.1 fusion.1
  35.5 15.5 %all_to_all.16 = f32[32,8,256]{2,1,0:T(8,128)S(1)} all-to-all(f32[32,8,256]{2,1,0:T(8,128)S(1)} %bitcast.22), channel_id=1, replica_groups={{0,8,16,24,32,40,48,56,64,72,80,88,96,104,112,120,128,136,144,152,160,1..., dimensions={0} | all-to-all | bytes 524288 | tf_op jit(solution)/shard_map/all_to_all | solution.py:207
  51.0 10.5 %all_to_all.17 = f32[8,8,256]{2,1,0:T(8,128)S(1)} all-to-all(f32[8,8,256]{2,1,0:T(8,128)S(1)} %broadcast_in_dim.5), channel_id=1, replica_groups=mesh['grp'=8,'row'=32] {'grp'}, dimensions={0} | all-to-all | bytes 131072 | tf_op jit(solution)/shard_map/all_to_all | solution.py:209
  61.6 0.6 %copy.6 = f32[64,256]{1,0:T(8,128)} copy(f32[64,256]{1,0:T(8,128)S(1)} %bitcast.23) | data formatting | bytes 131072
  (5 shorter events, 0.1 us)
Async XLA Ops:
  0.0 3.2 %collective-permute-start = (s32[32]{0:T(128)}, s32[32]{0:T(128)S(1)}, u32[]{:S(2)}, u32[]{:S(2)}) collective-permute-start(s32[32]{0:T(128)} %param.6), channel_id=1, source_target_pairs={{0,1},{1,0},{2,3},{3,2},{4,5},{5,4},{6,7},{7,6},{8,9},{9,8},{10,11... | collective-permute-start | bytes 392 | tf_op jit(solution)/shard_map/ppermute | solution.py:193
  0.0 3.2 %collective-permute-start.1 = (s32[32]{0:T(128)}, s32[32]{0:T(128)S(1)}, u32[]{:S(2)}, u32[]{:S(2)}) collective-permute-start(s32[32]{0:T(128)} %param.7), channel_id=1, source_target_pairs={{0,1},{1,0},{2,3},{3,2},{4,5},{5,4},{6,7},{7,6},{8,9},{9,8},{10,11... | collective-permute-start | bytes 392 | tf_op jit(solution)/shard_map/ppermute | solution.py:193
  0.5 2.7 %copy-start = (s32[32]{0:T(128)S(1)}, s32[32]{0:T(128)}, u32[]{:S(2)}) copy-start(s32[32]{0:T(128)} %param.7) | copy-start | bytes 388
  0.5 2.7 %copy-start.1 = (s32[32]{0:T(128)S(1)}, s32[32]{0:T(128)}, u32[]{:S(2)}) copy-start(s32[32]{0:T(128)} %param.6) | copy-start | bytes 388
  3.3 20.0 %collective-permute-start.2 = (f32[32,64,256]{2,1,0:T(8,128)S(1)}, f32[32,64,256]{2,1,0:T(8,128)S(1)}, u32[]{:S(2)}, u32[]{:S(2)}) collective-permute-start(f32[32,64,256]{2,1,0:T(8,128)S(1)} %get-tuple-element.12), channel_id=1, source_target_pairs={{0,1},{1,0},{2,3},{3,2},{4,5},{5,4},{6,7},{7,6},{8,9},{9,8},{10,11... | collective-permute-start | bytes 6291464 | tf_op jit(solution)/shard_map/ppermute | solution.py:199
  24.7 8.1 %collective-permute-start.3 = (f32[4,2,4,8,256]{4,3,2,1,0:T(8,128)S(1)}, f32[4,2,4,8,256]{4,3,2,1,0:T(8,128)S(1)}, u32[]{:S(2)}, u32[]{:S(2)}) collective-permute-start(f32[4,2,4,8,256]{4,3,2,1,0:T(8,128)S(1)} %get-tuple-element.15), channel_id=1, source_target_pairs={{0,4},{1,129},{2,6},{3,131},{4,0},{5,133},{6,2},{7,135},{8,12},{9,... | collective-permute-start | bytes 786440 | tf_op jit(solution)/shard_map/ppermute | solution.py:166
  26.2 8.5 %collective-permute-start.4 = (f32[4,2,4,8,256]{4,3,2,1,0:T(8,128)S(1)}, f32[4,2,4,8,256]{4,3,2,1,0:T(8,128)S(1)}, u32[]{:S(2)}, u32[]{:S(2)}) collective-permute-start(f32[4,2,4,8,256]{4,3,2,1,0:T(8,128)S(1)} %get-tuple-element.14), channel_id=1, source_target_pairs={{0,2},{1,65},{2,4},{3,67},{4,6},{5,69},{6,0},{7,71},{8,10},{9,73},... | collective-permute-start | bytes 786440 | tf_op jit(solution)/shard_map/ppermute | solution.py:166
  27.7 7.8 %collective-permute-start.5 = (f32[4,2,4,8,256]{4,3,2,1,0:T(8,128)S(1)}, f32[4,2,4,8,256]{4,3,2,1,0:T(8,128)S(1)}, u32[]{:S(2)}, u32[]{:S(2)}) collective-permute-start(f32[4,2,4,8,256]{4,3,2,1,0:T(8,128)S(1)} %get-tuple-element.13), channel_id=1, source_target_pairs={{0,6},{1,193},{2,0},{3,195},{4,2},{5,197},{6,4},{7,199},{8,14},{9,... | collective-permute-start | bytes 786440 | tf_op jit(solution)/shard_map/ppermute | solution.py:166

commit v14 on v13

--- a/solution.py
+++ b/solution.py
@@ -111,15 +111,12 @@
     unit_col = lax.broadcasted_iota(jnp.int32, (units, wide), 1)
     spread = (hadamard_sign(unit_row, unit_col // rows) * scale).astype(jnp.bfloat16)
     keep = lax.broadcasted_iota(jnp.int32, (tall, wide), 0) % rows == lax.broadcasted_iota(jnp.int32, (tall, wide), 1) % rows
-    highs, lows = [], []
-    for total in (side * same + different, same - side * different):
-        total = jnp.broadcast_to(total[:, None, :], (targets, rows, units)).reshape(tall, units)
-        weights = jnp.dot(total.astype(jnp.bfloat16), spread, preferred_element_type=jnp.float32)
-        high, low = two_parts(jnp.where(keep, weights, 0.0))
-        highs.append(high)
-        lows.append(low)
-    left = jnp.concatenate(highs, axis=1)
-    stacked = jnp.concatenate([left, jnp.concatenate(lows, axis=1)], axis=0)
+    totals = jnp.concatenate([side * same + different, same - side * different], axis=0)
+    totals = jnp.broadcast_to(totals[:, None, :], (2 * targets, rows, units)).reshape(2 * tall, units)
+    weights = jnp.dot(totals.astype(jnp.bfloat16), spread, preferred_element_type=jnp.float32)
+    weights = jnp.concatenate([jnp.where(keep, weights[:tall], 0.0), jnp.where(keep, weights[tall:], 0.0)], axis=1)
+    left, low_left = two_parts(weights)
+    stacked = jnp.concatenate([left, low_left], axis=0)
     for step, low_z in itertools.product(range(near), range(low_count)):
         piece = (first_y + step) % near * low_count + low_z
         span = pl.ds(pl.multiple_of(piece * rows, rows), rows)

time: 62.4 us -> 62.4 us (level)
  no operation moved by 1% of the time
where the time goes in v14:
time: 62.4 us; the launch traced here: 62.2 us
  blocking collectives  46 us (74%)
  waiting for transfers between devices  7.16 us (11%)
  starting transfers between devices  4.22 us (7%)
  Pallas kernels  3.94 us (6%)
  local copies, waits for them, and re-layouts  0.71 us (1%)
    all_to_all x1, blocking collectives, body(): meta = lax.all_to_all(meta, 'row', 0, 0, axis_index_groups=same_core)  19.9 us
    all_to_all x1, blocking collectives, body(): lax.all_to_all(pieces, AXES, 0, 0, axis_index_groups=second_groups())  15.5 us
    all_to_all x1, blocking collectives, body(): lax.all_to_all(jnp.broadcast_to(share[None], (groups, 8, col_count)), 'gr...  10.5 us
    ppermute x3, waiting for transfers between devices, first_shift(): return lax.ppermute(value, AXES, pairs)  7.15 us
    ppermute x3, starting transfers between devices, first_shift(): return lax.ppermute(value, AXES, pairs)  3.62 us
    pallas_call x1, Pallas kernels, transform(): pl.pallas_call(functools.partial(transform_kernel, cuts), in_specs=[pl.Bl...  2.66 us
    pallas_call x1, Pallas kernels, mix(): pl.pallas_call(functools.partial(mix_kernel, scale), in_specs=[pl.BlockSp...  1.28 us
  transfers between devices with their start and end apart: 6, of which 3 were waited for; matrix products, arithmetic and copies ran while one was open for 0% of the time, Pallas kernels for 4%

profile of v14, /device:TPU:2, one launch (start us, length us, event | category | flops | bytes accessed | tf_op | source)
XLA Modules:
  0.0 62.2 jit_solution(14578251986267719781)
XLA Ops:
  0.0 0.0 collective-permute-start
  0.0 0.5 collective-permute-start.1
  0.5 0.0 copy-start
  0.5 0.0 copy-start.1
  0.5 2.7 %transform.1 = (f32[32,64,256]{2,1,0:T(8,128)S(1)}, f32[32,64,256]{2,1,0:T(8,128)S(1)}) custom-call(s32[1]{0:T(128)} %bitcast.place_ref, f32[32,128,256]{2,1,0:T(8,128)} %bitcast.21, s32[32,128]{1,0:T(8,128)} %bitcast.24), custom_call_target="tpu_custom_call" | custom-call | flops 536870912 | bytes 8388608 | tf_op jit(solution)/shard_map/transform/pallas_call | solution.py:69
  3.2 0.0 collective-permute-done
  3.2 0.0 collective-permute-done.1
  3.2 0.0 copy-done
  3.2 0.0 copy-done.1
  3.3 0.1 collective-permute-start.2
  3.4 19.9 %all_to_all.15.meta_ref = s32[16,4,128]{2,1,0:T(4,128)S(1)} all-to-all(s32[16,4,128]{2,1,0:T(4,128)S(1)} %broadcast_in_dim.4), channel_id=1, replica_groups={{0,2,4,6,8,10,12,14,16,18,20,22,24,26,28,30},{1,3,5,7,9,11,13,15,17,19,..., dimensions={0} | all-to-all | bytes 65536 | tf_op jit(solution)/shard_map/all_to_all | solution.py:198
  23.3 0.0 collective-permute-done.2.other_ref
  23.3 1.3 %mix.1 = f32[4,4,2,4,8,256]{5,4,3,2,1,0:T(8,128)S(1)} custom-call(s32[1]{0:T(128)} %bitcast.place_ref, s32[16,4,128]{2,1,0:T(4,128)S(1)} %all_to_all.15.meta_ref, f32[32,64,256]{2,1,0:T(8,128)S(1)} %get-tuple-element.11.own_ref, f32[32,64,256]{2,1,0:T(8,128)S(1)} %collective-permute-done.2.other_ref), custom_call_target="tpu_custom_call" | custom-call | flops 805306368 | bytes 5242880 | tf_op jit(solution)/shard_map/mix/pallas_call | solution.py:136
  24.6 0.1 slice_bitcast_fusion
  24.7 1.6 %collective-permute-start.3 = (f32[4,2,4,8,256]{4,3,2,1,0:T(8,128)S(1)}, f32[4,2,4,8,256]{4,3,2,1,0:T(8,128)S(1)}, u32[]{:S(2)}, u32[]{:S(2)}) collective-permute-start(f32[4,2,4,8,256]{4,3,2,1,0:T(8,128)S(1)} %get-tuple-element.15), channel_id=1, source_target_pairs={{0,4},{1,129},{2,6},{3,131},{4,0},{5,133},{6,2},{7,135},{8,12},{9,... | collective-permute-start | bytes 786440 | tf_op jit(solution)/shard_map/ppermute | solution.py:163
  26.3 1.4 %collective-permute-start.4 = (f32[4,2,4,8,256]{4,3,2,1,0:T(8,128)S(1)}, f32[4,2,4,8,256]{4,3,2,1,0:T(8,128)S(1)}, u32[]{:S(2)}, u32[]{:S(2)}) collective-permute-start(f32[4,2,4,8,256]{4,3,2,1,0:T(8,128)S(1)} %get-tuple-element.14), channel_id=1, source_target_pairs={{0,2},{1,65},{2,4},{3,67},{4,6},{5,69},{6,0},{7,71},{8,10},{9,73},... | collective-permute-start | bytes 786440 | tf_op jit(solution)/shard_map/ppermute | solution.py:163
  27.7 0.6 collective-permute-start.5
  28.3 4.4 %collective-permute-done.3 = f32[4,2,4,8,256]{4,3,2,1,0:T(8,128)S(1)} collective-permute-done((f32[4,2,4,8,256]{4,3,2,1,0:T(8,128)S(1)}, f32[4,2,4,8,256]{4,3,2,1,0:T(8,128)S(1)}, u32[]{:S(2)}, u32[]{:S(2)}) %collective-permute-start.3) | collective-permute-done | bytes 262176 | tf_op jit(solution)/shard_map/ppermute | solution.py:163
  32.7 2.0 %collective-permute-done.4 = f32[4,2,4,8,256]{4,3,2,1,0:T(8,128)S(1)} collective-permute-done((f32[4,2,4,8,256]{4,3,2,1,0:T(8,128)S(1)}, f32[4,2,4,8,256]{4,3,2,1,0:T(8,128)S(1)}, u32[]{:S(2)}, u32[]{:S(2)}) %collective-permute-start.4) | collective-permute-done | bytes 262176 | tf_op jit(solution)/shard_map/ppermute | solution.py:163
  34.7 0.7 %collective-permute-done.5 = f32[4,2,4,8,256]{4,3,2,1,0:T(8,128)S(1)} collective-permute-done((f32[4,2,4,8,256]{4,3,2,1,0:T(8,128)S(1)}, f32[4,2,4,8,256]{4,3,2,1,0:T(8,128)S(1)}, u32[]{:S(2)}, u32[]{:S(2)}) %collective-permute-start.5) | collective-permute-done | bytes 262176 | tf_op jit(solution)/shard_map/ppermute | solution.py:163
  35.4 0.1 fusion.1
  35.5 15.5 %all_to_all.16 = f32[32,8,256]{2,1,0:T(8,128)S(1)} all-to-all(f32[32,8,256]{2,1,0:T(8,128)S(1)} %bitcast.22), channel_id=1, replica_groups={{0,8,16,24,32,40,48,56,64,72,80,88,96,104,112,120,128,136,144,152,160,1..., dimensions={0} | all-to-all | bytes 524288 | tf_op jit(solution)/shard_map/all_to_all | solution.py:204
  51.1 10.5 %all_to_all.17 = f32[8,8,256]{2,1,0:T(8,128)S(1)} all-to-all(f32[8,8,256]{2,1,0:T(8,128)S(1)} %broadcast_in_dim.5), channel_id=1, replica_groups=mesh['grp'=8,'row'=32] {'grp'}, dimensions={0} | all-to-all | bytes 131072 | tf_op jit(solution)/shard_map/all_to_all | solution.py:206
  61.6 0.6 %copy.6 = f32[64,256]{1,0:T(8,128)} copy(f32[64,256]{1,0:T(8,128)S(1)} %bitcast.23) | data formatting | bytes 131072
  (5 shorter events, 0.1 us)
Async XLA Ops:
  0.0 3.2 %collective-permute-start = (s32[32]{0:T(128)}, s32[32]{0:T(128)S(1)}, u32[]{:S(2)}, u32[]{:S(2)}) collective-permute-start(s32[32]{0:T(128)} %param.6), channel_id=1, source_target_pairs={{0,1},{1,0},{2,3},{3,2},{4,5},{5,4},{6,7},{7,6},{8,9},{9,8},{10,11... | collective-permute-start | bytes 392 | tf_op jit(solution)/shard_map/ppermute | solution.py:190
  0.0 3.2 %collective-permute-start.1 = (s32[32]{0:T(128)}, s32[32]{0:T(128)S(1)}, u32[]{:S(2)}, u32[]{:S(2)}) collective-permute-start(s32[32]{0:T(128)} %param.7), channel_id=1, source_target_pairs={{0,1},{1,0},{2,3},{3,2},{4,5},{5,4},{6,7},{7,6},{8,9},{9,8},{10,11... | collective-permute-start | bytes 392 | tf_op jit(solution)/shard_map/ppermute | solution.py:190
  0.5 2.7 %copy-start = (s32[32]{0:T(128)S(1)}, s32[32]{0:T(128)}, u32[]{:S(2)}) copy-start(s32[32]{0:T(128)} %param.7) | copy-start | bytes 388
  0.5 2.7 %copy-start.1 = (s32[32]{0:T(128)S(1)}, s32[32]{0:T(128)}, u32[]{:S(2)}) copy-start(s32[32]{0:T(128)} %param.6) | copy-start | bytes 388
  3.3 20.0 %collective-permute-start.2 = (f32[32,64,256]{2,1,0:T(8,128)S(1)}, f32[32,64,256]{2,1,0:T(8,128)S(1)}, u32[]{:S(2)}, u32[]{:S(2)}) collective-permute-start(f32[32,64,256]{2,1,0:T(8,128)S(1)} %get-tuple-element.12), channel_id=1, source_target_pairs={{0,1},{1,0},{2,3},{3,2},{4,5},{5,4},{6,7},{7,6},{8,9},{9,8},{10,11... | collective-permute-start | bytes 6291464 | tf_op jit(solution)/shard_map/ppermute | solution.py:196
  24.7 8.1 %collective-permute-start.3 = (f32[4,2,4,8,256]{4,3,2,1,0:T(8,128)S(1)}, f32[4,2,4,8,256]{4,3,2,1,0:T(8,128)S(1)}, u32[]{:S(2)}, u32[]{:S(2)}) collective-permute-start(f32[4,2,4,8,256]{4,3,2,1,0:T(8,128)S(1)} %get-tuple-element.15), channel_id=1, source_target_pairs={{0,4},{1,129},{2,6},{3,131},{4,0},{5,133},{6,2},{7,135},{8,12},{9,... | collective-permute-start | bytes 786440 | tf_op jit(solution)/shard_map/ppermute | solution.py:163
  26.3 8.5 %collective-permute-start.4 = (f32[4,2,4,8,256]{4,3,2,1,0:T(8,128)S(1)}, f32[4,2,4,8,256]{4,3,2,1,0:T(8,128)S(1)}, u32[]{:S(2)}, u32[]{:S(2)}) collective-permute-start(f32[4,2,4,8,256]{4,3,2,1,0:T(8,128)S(1)} %get-tuple-element.14), channel_id=1, source_target_pairs={{0,2},{1,65},{2,4},{3,67},{4,6},{5,69},{6,0},{7,71},{8,10},{9,73},... | collective-permute-start | bytes 786440 | tf_op jit(solution)/shard_map/ppermute | solution.py:163
  27.7 7.8 %collective-permute-start.5 = (f32[4,2,4,8,256]{4,3,2,1,0:T(8,128)S(1)}, f32[4,2,4,8,256]{4,3,2,1,0:T(8,128)S(1)}, u32[]{:S(2)}, u32[]{:S(2)}) collective-permute-start(f32[4,2,4,8,256]{4,3,2,1,0:T(8,128)S(1)} %get-tuple-element.13), channel_id=1, source_target_pairs={{0,6},{1,193},{2,0},{3,195},{4,2},{5,197},{6,4},{7,199},{8,14},{9,... | collective-permute-start | bytes 786440 | tf_op jit(solution)/shard_map/ppermute | solution.py:163

commit v15 on v10

--- a/solution.py
+++ b/solution.py
@@ -92,8 +92,8 @@
     targets = near * far
     me = place_ref[0] % sources
     core = me & 1
-    first_x = jnp.where(core == 0, me >> 1, 0)
-    first_y = jnp.where(core == 0, 0, place_ref[0] // sources // low_count)
+    first_x = jnp.where(core == 1, me >> 1, 0)
+    first_y = jnp.where(core == 1, 0, place_ref[0] // sources // low_count)
     index = lax.broadcasted_iota(jnp.int32, (targets, units), 0)
     target = index % far * near + (index // far + first_x) % near
     sums = [jnp.zeros((targets, units), jnp.float32) for _ in range(2)]
@@ -127,7 +127,7 @@
         result = jnp.dot(left, low, preferred_element_type=jnp.float32) + (both[:tall] + both[tall:])
         result = result.reshape(near, far, rows, cols)
         for turn in range(near):
-            out_ref[jnp.where(core == 0, turn, step), jnp.where(core == 0, step, turn), low_z] = result[turn]
+            out_ref[jnp.where(core == 1, turn, step), jnp.where(core == 1, step, turn), low_z] = result[turn]
 
 
 def mix(scale, place, meta, own, other, near, low_count, far):
@@ -159,7 +159,7 @@
 def first_shift(value, step):
     pairs = []
     for y, z_low, z_high, x, core in places():
-        to = (y, z_low, z_high, x + step, core) if core == 0 else (y + step, z_low, z_high, x, core)
+        to = (y, z_low, z_high, x + step, core) if core == 1 else (y + step, z_low, z_high, x, core)
         pairs.append((flat_index(y, z_low, z_high, x, core), flat_index(*to)))
     return lax.ppermute(value, AXES, pairs)
 
@@ -170,7 +170,7 @@
         members = itertools.product(range(Y), range(Z_LOW), range(Z_HIGH))
         groups.append(
             [
-                flat_index(free, z_low, z_high, fixed, core) if core == 0 else flat_index(fixed, z_low, z_high, free, core)
+                flat_index(free, z_low, z_high, fixed, core) if core == 1 else flat_index(fixed, z_low, z_high, free, core)
                 for free, z_low, z_high in members
             ]
         )

time: 62.1 us -> 62.8 us (1.011)
  starting transfers between devices: 3.7 us -> 6.61 us
  waiting for transfers between devices: 7.17 us -> 4.6 us
    ppermute x3, starting transfers between devices: 3.6 us -> 6.52 us  [first_shift(): return lax.ppermute(value, AXES, pairs)]
    ppermute x3, waiting for transfers between devices: 7.17 us -> 4.59 us  [first_shift(): return lax.ppermute(value, AXES, pairs)]
    all_to_all x1, blocking collectives: 10.3 us -> 12.2 us  [body(): lax.all_to_all(jnp.broadcast_to(share[None], (groups, 8, col_count)), 'gr...]
    all_to_all x1, blocking collectives: 15.8 us -> 14.1 us  [body(): lax.all_to_all(pieces, AXES, 0, 0, axis_index_groups=second_groups())]
where the time goes in v15:
time: 62.8 us; the launch traced here: 62.4 us
  blocking collectives  46.4 us (74%)
  starting transfers between devices  6.61 us (11%)
  waiting for transfers between devices  4.6 us (7%)
  Pallas kernels  3.94 us (6%)
  local copies, waits for them, and re-layouts  0.71 us (1%)
    all_to_all x1, blocking collectives, body(): lax.all_to_all(jnp.broadcast_to(mine[None], (devs, 2, units)), 'row', 0, 0)  20.1 us
    all_to_all x1, blocking collectives, body(): lax.all_to_all(pieces, AXES, 0, 0, axis_index_groups=second_groups())  14.1 us
    all_to_all x1, blocking collectives, body(): lax.all_to_all(jnp.broadcast_to(share[None], (groups, 8, col_count)), 'gr...  12.2 us
    ppermute x3, starting transfers between devices, first_shift(): return lax.ppermute(value, AXES, pairs)  6.52 us
    ppermute x3, waiting for transfers between devices, first_shift(): return lax.ppermute(value, AXES, pairs)  4.59 us
    pallas_call x1, Pallas kernels, transform(): pl.pallas_call(functools.partial(transform_kernel, cuts), in_specs=[pl.Bl...  2.66 us
    pallas_call x1, Pallas kernels, mix(): pl.pallas_call(functools.partial(mix_kernel, scale), in_specs=[pl.BlockSp...  1.28 us
  transfers between devices with their start and end apart: 4, of which 3 were waited for; matrix products, arithmetic and copies ran while one was open for 0% of the time, Pallas kernels for 0%

profile of v15, /device:TPU:2, one launch (start us, length us, event | category | flops | bytes accessed | tf_op | source)
XLA Modules:
  0.0 62.4 jit_solution(11233316722099619388)
XLA Ops:
  0.0 0.0 copy-start
  0.0 0.0 copy-start.1
  0.0 2.7 %transform.1 = (f32[32,64,256]{2,1,0:T(8,128)S(1)}, f32[32,64,256]{2,1,0:T(8,128)S(1)}) custom-call(s32[1]{0:T(128)} %bitcast.place_ref, f32[32,128,256]{2,1,0:T(8,128)} %bitcast.19, s32[32,128]{1,0:T(8,128)} %bitcast.22), custom_call_target="tpu_custom_call" | custom-call | flops 536870912 | bytes 8388608 | tf_op jit(solution)/shard_map/transform/pallas_call | solution.py:68
  2.7 0.1 collective-permute-start
  2.8 0.0 copy-done
  2.8 0.0 copy-done.1
  2.8 20.1 %all_to_all.15.meta_ref = s32[32,2,32]{2,1,0:T(2,128)S(1)} all-to-all(s32[32,2,32]{2,1,0:T(2,128)S(1)} %broadcast_in_dim.4), channel_id=1, replica_groups=mesh['grp'=8,'row'=32] {'row'}, dimensions={0} | all-to-all | bytes 16384 | tf_op jit(solution)/shard_map/all_to_all | solution.py:191
  22.9 0.0 collective-permute-done.other_ref
  23.0 1.3 %mix.1 = f32[4,4,2,4,8,256]{5,4,3,2,1,0:T(8,128)S(1)} custom-call(s32[1]{0:T(128)} %bitcast.place_ref, s32[32,2,32]{2,1,0:T(2,128)S(1)} %all_to_all.15.meta_ref, f32[32,64,256]{2,1,0:T(8,128)S(1)} %get-tuple-element.7.own_ref, f32[32,64,256]{2,1,0:T(8,128)S(1)} %collective-permute-done.other_ref), custom_call_target="tpu_custom_call" | custom-call | flops 805306368 | bytes 5242880 | tf_op jit(solution)/shard_map/mix/pallas_call | solution.py:137
  24.2 0.1 slice_bitcast_fusion
  24.3 3.3 %collective-permute-start.1 = (f32[4,2,4,8,256]{4,3,2,1,0:T(8,128)S(1)}, f32[4,2,4,8,256]{4,3,2,1,0:T(8,128)S(1)}, u32[]{:S(2)}, u32[]{:S(2)}) collective-permute-start(f32[4,2,4,8,256]{4,3,2,1,0:T(8,128)S(1)} %get-tuple-element.11), channel_id=1, source_target_pairs={{0,128},{1,5},{2,130},{3,7},{4,132},{5,1},{6,134},{7,3},{8,136},{9... | collective-permute-start | bytes 786440 | tf_op jit(solution)/shard_map/ppermute | solution.py:164
  27.6 0.7 %collective-permute-start.2 = (f32[4,2,4,8,256]{4,3,2,1,0:T(8,128)S(1)}, f32[4,2,4,8,256]{4,3,2,1,0:T(8,128)S(1)}, u32[]{:S(2)}, u32[]{:S(2)}) collective-permute-start(f32[4,2,4,8,256]{4,3,2,1,0:T(8,128)S(1)} %get-tuple-element.10), channel_id=1, source_target_pairs={{0,64},{1,3},{2,66},{3,5},{4,68},{5,7},{6,70},{7,1},{8,72},{9,11},... | collective-permute-start | bytes 786440 | tf_op jit(solution)/shard_map/ppermute | solution.py:164
  28.3 2.6 %collective-permute-start.3 = (f32[4,2,4,8,256]{4,3,2,1,0:T(8,128)S(1)}, f32[4,2,4,8,256]{4,3,2,1,0:T(8,128)S(1)}, u32[]{:S(2)}, u32[]{:S(2)}) collective-permute-start(f32[4,2,4,8,256]{4,3,2,1,0:T(8,128)S(1)} %get-tuple-element.9), channel_id=1, source_target_pairs={{0,192},{1,7},{2,194},{3,1},{4,196},{5,3},{6,198},{7,5},{8,200},{9... | collective-permute-start | bytes 786440 | tf_op jit(solution)/shard_map/ppermute | solution.py:164
  30.8 1.4 %collective-permute-done.1 = f32[4,2,4,8,256]{4,3,2,1,0:T(8,128)S(1)} collective-permute-done((f32[4,2,4,8,256]{4,3,2,1,0:T(8,128)S(1)}, f32[4,2,4,8,256]{4,3,2,1,0:T(8,128)S(1)}, u32[]{:S(2)}, u32[]{:S(2)}) %collective-permute-start.1) | collective-permute-done | bytes 262176 | tf_op jit(solution)/shard_map/ppermute | solution.py:164
  32.3 2.9 %collective-permute-done.2 = f32[4,2,4,8,256]{4,3,2,1,0:T(8,128)S(1)} collective-permute-done((f32[4,2,4,8,256]{4,3,2,1,0:T(8,128)S(1)}, f32[4,2,4,8,256]{4,3,2,1,0:T(8,128)S(1)}, u32[]{:S(2)}, u32[]{:S(2)}) %collective-permute-start.2) | collective-permute-done | bytes 262176 | tf_op jit(solution)/shard_map/ppermute | solution.py:164
  35.2 0.2 collective-permute-done.3
  35.4 0.1 fusion.1
  35.5 14.1 %all_to_all.16 = f32[32,8,256]{2,1,0:T(8,128)S(1)} all-to-all(f32[32,8,256]{2,1,0:T(8,128)S(1)} %bitcast.20), channel_id=1, replica_groups={{0,8,16,24,32,40,48,56,2,10,18,26,34,42,50,58,4,12,20,28,36,44,52,60,6,..., dimensions={0} | all-to-all | bytes 524288 | tf_op jit(solution)/shard_map/all_to_all | solution.py:201
  49.6 12.2 %all_to_all.17 = f32[8,8,256]{2,1,0:T(8,128)S(1)} all-to-all(f32[8,8,256]{2,1,0:T(8,128)S(1)} %broadcast_in_dim.5), channel_id=1, replica_groups=mesh['grp'=8,'row'=32] {'grp'}, dimensions={0} | all-to-all | bytes 131072 | tf_op jit(solution)/shard_map/all_to_all | solution.py:203
  61.8 0.6 %copy.6 = f32[64,256]{1,0:T(8,128)} copy(f32[64,256]{1,0:T(8,128)S(1)} %bitcast.21) | data formatting | bytes 131072
  (4 shorter events, 0.1 us)
Async XLA Ops:
  0.0 2.8 %copy-start = (s32[32]{0:T(128)S(1)}, s32[32]{0:T(128)}, u32[]{:S(2)}) copy-start(s32[32]{0:T(128)} %param.7) | copy-start | bytes 388
  0.0 2.8 %copy-start.1 = (s32[32]{0:T(128)S(1)}, s32[32]{0:T(128)}, u32[]{:S(2)}) copy-start(s32[32]{0:T(128)} %param.6) | copy-start | bytes 388
  2.7 20.3 %collective-permute-start = (f32[32,64,256]{2,1,0:T(8,128)S(1)}, f32[32,64,256]{2,1,0:T(8,128)S(1)}, u32[]{:S(2)}, u32[]{:S(2)}) collective-permute-start(f32[32,64,256]{2,1,0:T(8,128)S(1)} %get-tuple-element.8), channel_id=1, source_target_pairs={{0,1},{1,0},{2,3},{3,2},{4,5},{5,4},{6,7},{7,6},{8,9},{9,8},{10,11... | collective-permute-start | bytes 6291464 | tf_op jit(solution)/shard_map/ppermute | solution.py:195
  24.3 8.0 %collective-permute-start.1 = (f32[4,2,4,8,256]{4,3,2,1,0:T(8,128)S(1)}, f32[4,2,4,8,256]{4,3,2,1,0:T(8,128)S(1)}, u32[]{:S(2)}, u32[]{:S(2)}) collective-permute-start(f32[4,2,4,8,256]{4,3,2,1,0:T(8,128)S(1)} %get-tuple-element.11), channel_id=1, source_target_pairs={{0,128},{1,5},{2,130},{3,7},{4,132},{5,1},{6,134},{7,3},{8,136},{9... | collective-permute-start | bytes 786440 | tf_op jit(solution)/shard_map/ppermute | solution.py:164
  27.6 7.6 %collective-permute-start.2 = (f32[4,2,4,8,256]{4,3,2,1,0:T(8,128)S(1)}, f32[4,2,4,8,256]{4,3,2,1,0:T(8,128)S(1)}, u32[]{:S(2)}, u32[]{:S(2)}) collective-permute-start(f32[4,2,4,8,256]{4,3,2,1,0:T(8,128)S(1)} %get-tuple-element.10), channel_id=1, source_target_pairs={{0,64},{1,3},{2,66},{3,5},{4,68},{5,7},{6,70},{7,1},{8,72},{9,11},... | collective-permute-start | bytes 786440 | tf_op jit(solution)/shard_map/ppermute | solution.py:164
  28.3 7.2 %collective-permute-start.3 = (f32[4,2,4,8,256]{4,3,2,1,0:T(8,128)S(1)}, f32[4,2,4,8,256]{4,3,2,1,0:T(8,128)S(1)}, u32[]{:S(2)}, u32[]{:S(2)}) collective-permute-start(f32[4,2,4,8,256]{4,3,2,1,0:T(8,128)S(1)} %get-tuple-element.9), channel_id=1, source_target_pairs={{0,192},{1,7},{2,194},{3,1},{4,196},{5,3},{6,198},{7,5},{8,200},{9... | collective-permute-start | bytes 786440 | tf_op jit(solution)/shard_map/ppermute | solution.py:164

commit v16 on v10

--- a/solution.py
+++ b/solution.py
@@ -61,7 +61,7 @@
 
 def transform(place, matrix, row_signs):
     count, block, cols = matrix.shape
-    cuts = (0, count // 4, count * 5 // 8, count)
+    cuts = (0, count // 4, count * 11 // 16, count)
     half = jax.ShapeDtypeStruct((count, block // 2, cols), jnp.float32)
     hbm = pl.BlockSpec(memory_space=pltpu.HBM)
     vmem = pl.BlockSpec(memory_space=pltpu.VMEM)

time: 62.1 us -> 62.1 us (level)
  no operation moved by 1% of the time
where the time goes in v16:
time: 62.1 us; the launch traced here: 61.9 us
  blocking collectives  46.2 us (74%)
  waiting for transfers between devices  7.17 us (12%)
  Pallas kernels  4.01 us (6%)
  starting transfers between devices  3.7 us (6%)
  local copies, waits for them, and re-layouts  0.71 us (1%)
    all_to_all x1, blocking collectives, body(): lax.all_to_all(jnp.broadcast_to(mine[None], (devs, 2, units)), 'row', 0, 0)  20.1 us
    all_to_all x1, blocking collectives, body(): lax.all_to_all(pieces, AXES, 0, 0, axis_index_groups=second_groups())  15.8 us
    all_to_all x1, blocking collectives, body(): lax.all_to_all(jnp.broadcast_to(share[None], (groups, 8, col_count)), 'gr...  10.3 us
    ppermute x3, waiting for transfers between devices, first_shift(): return lax.ppermute(value, AXES, pairs)  7.17 us
    ppermute x3, starting transfers between devices, first_shift(): return lax.ppermute(value, AXES, pairs)  3.6 us
    pallas_call x1, Pallas kernels, transform(): pl.pallas_call(functools.partial(transform_kernel, cuts), in_specs=[pl.Bl...  2.74 us
    pallas_call x1, Pallas kernels, mix(): pl.pallas_call(functools.partial(mix_kernel, scale), in_specs=[pl.BlockSp...  1.28 us
  transfers between devices with their start and end apart: 4, of which 3 were waited for; matrix products, arithmetic and copies ran while one was open for 0% of the time, Pallas kernels for 0%

profile of v16, /device:TPU:2, one launch (start us, length us, event | category | flops | bytes accessed | tf_op | source)
XLA Modules:
  0.0 61.9 jit_solution(16889037822640267471)
XLA Ops:
  0.0 0.0 copy-start
  0.0 0.0 copy-start.1
  0.0 2.7 %transform.1 = (f32[32,64,256]{2,1,0:T(8,128)S(1)}, f32[32,64,256]{2,1,0:T(8,128)S(1)}) custom-call(s32[1]{0:T(128)} %bitcast.place_ref, f32[32,128,256]{2,1,0:T(8,128)} %bitcast.19, s32[32,128]{1,0:T(8,128)} %bitcast.22), custom_call_target="tpu_custom_call" | custom-call | flops 536870912 | bytes 8388608 | tf_op jit(solution)/shard_map/transform/pallas_call | solution.py:68
  2.7 0.1 collective-permute-start
  2.8 0.0 copy-done
  2.9 0.0 copy-done.1
  2.9 20.1 %all_to_all.15.meta_ref = s32[32,2,32]{2,1,0:T(2,128)S(1)} all-to-all(s32[32,2,32]{2,1,0:T(2,128)S(1)} %broadcast_in_dim.4), channel_id=1, replica_groups=mesh['grp'=8,'row'=32] {'row'}, dimensions={0} | all-to-all | bytes 16384 | tf_op jit(solution)/shard_map/all_to_all | solution.py:191
  23.0 0.0 collective-permute-done.other_ref
  23.0 1.3 %mix.1 = f32[4,4,2,4,8,256]{5,4,3,2,1,0:T(8,128)S(1)} custom-call(s32[1]{0:T(128)} %bitcast.place_ref, s32[32,2,32]{2,1,0:T(2,128)S(1)} %all_to_all.15.meta_ref, f32[32,64,256]{2,1,0:T(8,128)S(1)} %get-tuple-element.7.own_ref, f32[32,64,256]{2,1,0:T(8,128)S(1)} %collective-permute-done.other_ref), custom_call_target="tpu_custom_call" | custom-call | flops 805306368 | bytes 5242880 | tf_op jit(solution)/shard_map/mix/pallas_call | solution.py:137
  24.3 0.1 slice_bitcast_fusion
  24.4 1.6 %collective-permute-start.1 = (f32[4,2,4,8,256]{4,3,2,1,0:T(8,128)S(1)}, f32[4,2,4,8,256]{4,3,2,1,0:T(8,128)S(1)}, u32[]{:S(2)}, u32[]{:S(2)}) collective-permute-start(f32[4,2,4,8,256]{4,3,2,1,0:T(8,128)S(1)} %get-tuple-element.11), channel_id=1, source_target_pairs={{0,4},{1,129},{2,6},{3,131},{4,0},{5,133},{6,2},{7,135},{8,12},{9,... | collective-permute-start | bytes 786440 | tf_op jit(solution)/shard_map/ppermute | solution.py:164
  26.0 1.4 %collective-permute-start.2 = (f32[4,2,4,8,256]{4,3,2,1,0:T(8,128)S(1)}, f32[4,2,4,8,256]{4,3,2,1,0:T(8,128)S(1)}, u32[]{:S(2)}, u32[]{:S(2)}) collective-permute-start(f32[4,2,4,8,256]{4,3,2,1,0:T(8,128)S(1)} %get-tuple-element.10), channel_id=1, source_target_pairs={{0,2},{1,65},{2,4},{3,67},{4,6},{5,69},{6,0},{7,71},{8,10},{9,73},... | collective-permute-start | bytes 786440 | tf_op jit(solution)/shard_map/ppermute | solution.py:164
  27.4 0.6 collective-permute-start.3
  28.0 4.5 %collective-permute-done.1 = f32[4,2,4,8,256]{4,3,2,1,0:T(8,128)S(1)} collective-permute-done((f32[4,2,4,8,256]{4,3,2,1,0:T(8,128)S(1)}, f32[4,2,4,8,256]{4,3,2,1,0:T(8,128)S(1)}, u32[]{:S(2)}, u32[]{:S(2)}) %collective-permute-start.1) | collective-permute-done | bytes 262176 | tf_op jit(solution)/shard_map/ppermute | solution.py:164
  32.4 1.8 %collective-permute-done.2 = f32[4,2,4,8,256]{4,3,2,1,0:T(8,128)S(1)} collective-permute-done((f32[4,2,4,8,256]{4,3,2,1,0:T(8,128)S(1)}, f32[4,2,4,8,256]{4,3,2,1,0:T(8,128)S(1)}, u32[]{:S(2)}, u32[]{:S(2)}) %collective-permute-start.2) | collective-permute-done | bytes 262176 | tf_op jit(solution)/shard_map/ppermute | solution.py:164
  34.3 0.9 %collective-permute-done.3 = f32[4,2,4,8,256]{4,3,2,1,0:T(8,128)S(1)} collective-permute-done((f32[4,2,4,8,256]{4,3,2,1,0:T(8,128)S(1)}, f32[4,2,4,8,256]{4,3,2,1,0:T(8,128)S(1)}, u32[]{:S(2)}, u32[]{:S(2)}) %collective-permute-start.3) | collective-permute-done | bytes 262176 | tf_op jit(solution)/shard_map/ppermute | solution.py:164
  35.1 0.1 fusion.1
  35.2 15.8 %all_to_all.16 = f32[32,8,256]{2,1,0:T(8,128)S(1)} all-to-all(f32[32,8,256]{2,1,0:T(8,128)S(1)} %bitcast.20), channel_id=1, replica_groups={{0,8,16,24,32,40,48,56,64,72,80,88,96,104,112,120,128,136,144,152,160,1..., dimensions={0} | all-to-all | bytes 524288 | tf_op jit(solution)/shard_map/all_to_all | solution.py:201
  51.1 10.3 %all_to_all.17 = f32[8,8,256]{2,1,0:T(8,128)S(1)} all-to-all(f32[8,8,256]{2,1,0:T(8,128)S(1)} %broadcast_in_dim.5), channel_id=1, replica_groups=mesh['grp'=8,'row'=32] {'grp'}, dimensions={0} | all-to-all | bytes 131072 | tf_op jit(solution)/shard_map/all_to_all | solution.py:203
  61.3 0.6 %copy.6 = f32[64,256]{1,0:T(8,128)} copy(f32[64,256]{1,0:T(8,128)S(1)} %bitcast.21) | data formatting | bytes 131072
  (4 shorter events, 0.1 us)
Async XLA Ops:
  0.0 2.9 %copy-start = (s32[32]{0:T(128)S(1)}, s32[32]{0:T(128)}, u32[]{:S(2)}) copy-start(s32[32]{0:T(128)} %param.7) | copy-start | bytes 388
  0.0 2.9 %copy-start.1 = (s32[32]{0:T(128)S(1)}, s32[32]{0:T(128)}, u32[]{:S(2)}) copy-start(s32[32]{0:T(128)} %param.6) | copy-start | bytes 388
  2.7 20.3 %collective-permute-start = (f32[32,64,256]{2,1,0:T(8,128)S(1)}, f32[32,64,256]{2,1,0:T(8,128)S(1)}, u32[]{:S(2)}, u32[]{:S(2)}) collective-permute-start(f32[32,64,256]{2,1,0:T(8,128)S(1)} %get-tuple-element.8), channel_id=1, source_target_pairs={{0,1},{1,0},{2,3},{3,2},{4,5},{5,4},{6,7},{7,6},{8,9},{9,8},{10,11... | collective-permute-start | bytes 6291464 | tf_op jit(solution)/shard_map/ppermute | solution.py:195
  24.4 8.1 %collective-permute-start.1 = (f32[4,2,4,8,256]{4,3,2,1,0:T(8,128)S(1)}, f32[4,2,4,8,256]{4,3,2,1,0:T(8,128)S(1)}, u32[]{:S(2)}, u32[]{:S(2)}) collective-permute-start(f32[4,2,4,8,256]{4,3,2,1,0:T(8,128)S(1)} %get-tuple-element.11), channel_id=1, source_target_pairs={{0,4},{1,129},{2,6},{3,131},{4,0},{5,133},{6,2},{7,135},{8,12},{9,... | collective-permute-start | bytes 786440 | tf_op jit(solution)/shard_map/ppermute | solution.py:164
  26.0 8.3 %collective-permute-start.2 = (f32[4,2,4,8,256]{4,3,2,1,0:T(8,128)S(1)}, f32[4,2,4,8,256]{4,3,2,1,0:T(8,128)S(1)}, u32[]{:S(2)}, u32[]{:S(2)}) collective-permute-start(f32[4,2,4,8,256]{4,3,2,1,0:T(8,128)S(1)} %get-tuple-element.10), channel_id=1, source_target_pairs={{0,2},{1,65},{2,4},{3,67},{4,6},{5,69},{6,0},{7,71},{8,10},{9,73},... | collective-permute-start | bytes 786440 | tf_op jit(solution)/shard_map/ppermute | solution.py:164
  27.4 7.7 %collective-permute-start.3 = (f32[4,2,4,8,256]{4,3,2,1,0:T(8,128)S(1)}, f32[4,2,4,8,256]{4,3,2,1,0:T(8,128)S(1)}, u32[]{:S(2)}, u32[]{:S(2)}) collective-permute-start(f32[4,2,4,8,256]{4,3,2,1,0:T(8,128)S(1)} %get-tuple-element.9), channel_id=1, source_target_pairs={{0,6},{1,193},{2,0},{3,195},{4,2},{5,197},{6,4},{7,199},{8,14},{9,... | collective-permute-start | bytes 786440 | tf_op jit(solution)/shard_map/ppermute | solution.py:164
